TPU v7x, 256 devices: a whole 4x4x8 slice. The times are simulated.
256 devices in a mesh: prow: 16 (over y_hi, x, core), pcol: 16 (over z, y_lo).
Axes of the slice: x: 4, y: 4 (y_hi: 2, y_lo: 2; y = y_hi * 2 + y_lo), z: 8, core: 2. Of those that a mesh axis runs over, the one named last changes fastest.
Arguments:
- anc_inverse: bfloat16 [2, 1, 16, 256, 1, 16, 256], P(None, None, 'prow', None, None, 'pcol'), may hold values from -6 to 6
- factor_panel: bfloat16 [2, 1, 16, 256, 1, 16, 256], P(None, None, 'prow', None, None, 'pcol'), may hold values from -0.09375 to 0.09375
- diag_inverse: bfloat16 [2, 1, 16, 256, 1, 16, 256], P(None, None, 'pcol', None, None, 'prow'), may hold values from -6 to 6
- block_pattern: int32 [2, 16, 16], replicated, may hold values from 0 to 1, as said below
Outputs:
- sigma_off: bfloat16 [2, 1, 16, 256, 1, 16, 256], P(None, None, 'prow', None, None, 'pcol')
- sigma_diag: bfloat16 [2, 1, 16, 256, 1, 16, 256], P(None, None, 'pcol', None, None, 'prow')
Inputs may be any that keep to these rules, and one draw needn't show every extreme that they name: `block_pattern`: symmetric in its last two dimensions, with ones on the diagonal.
All inputs are finite; a program needn't handle non-finite values.
Results may differ from a plain program's by a relative error of at most 0.0039.
Values may be sent and summed in bfloat16 or wider, within the bound.
No kernel may reach another device: no remote copies, remote signals or barrier semaphores. Data moves between devices by JAX's collectives and lax.ppermute only.
A program may use at most 64 MiB of HBM per device.

v0:
```python
import jax
import jax.numpy as jnp
from jax import lax
from jax.sharding import PartitionSpec as P


def invert_window(anc_local, panel_local, diag_local, owned_rows, col_index):
    own_mask = lax.dynamic_slice_in_dim(owned_rows, col_index, 1, 4)
    keep_mask = own_mask[:, :, :, None, :, :, None] != 0
    masked = jnp.where(keep_mask, anc_local, jnp.zeros_like(anc_local))
    gathered = lax.all_gather(panel_local, "prow", axis=2, tiled=True)
    owner_panel = lax.all_to_all(gathered, "pcol", split_axis=2, concat_axis=5, tiled=True)
    partial_terms = jnp.einsum(
        "sraicbj,scbjwnm->sraiwnm", masked, owner_panel, preferred_element_type=jnp.float32
    )
    product = lax.psum_scatter(partial_terms, "pcol", scatter_dimension=5, tiled=True)
    sigma_off = (-product).astype(jnp.bfloat16)
    all_cols = lax.all_gather(sigma_off, "pcol", axis=5, tiled=True)
    inner_sum = jnp.einsum(
        "sraiwbm,sraivnk->swbmvnk", panel_local, all_cols, preferred_element_type=jnp.float32
    )
    summed = lax.psum_scatter(inner_sum, "prow", scatter_dimension=5, tiled=True)
    sigma_diag = (diag_local.astype(jnp.float32) - summed).astype(jnp.bfloat16)
    return (sigma_off, sigma_diag)


def on_device(anc_inverse, factor_panel, diag_inverse, block_pattern):
    row_index = lax.axis_index("prow")
    col_index = lax.axis_index("pcol")
    row_devices = lax.axis_size("prow")
    col_devices = lax.axis_size("pcol")
    nodes_all = anc_inverse.shape[0]
    pattern_grid = block_pattern.reshape(
        nodes_all, anc_inverse.shape[1], row_devices, anc_inverse.shape[4], col_devices
    )
    owned_rows = lax.dynamic_slice_in_dim(pattern_grid, row_index, 1, 2)
    off_list = []
    diag_list = []
    for supernode in range(nodes_all):
        off_block, diag_block = invert_window(
            anc_inverse[supernode : supernode + 1],
            factor_panel[supernode : supernode + 1],
            diag_inverse[supernode : supernode + 1],
            owned_rows[supernode : supernode + 1],
            col_index,
        )
        off_list.append(off_block)
        diag_list.append(diag_block)
    return (jnp.concatenate(off_list, axis=0), jnp.concatenate(diag_list, axis=0))


def solution(mesh):
    return jax.shard_map(
        on_device,
        mesh=mesh,
        in_specs=(
            P(None, None, "prow", None, None, "pcol", None),
            P(None, None, "prow", None, None, "pcol", None),
            P(None, None, "pcol", None, None, "prow", None),
            P(),
        ),
        out_specs=(
            P(None, None, "prow", None, None, "pcol", None),
            P(None, None, "pcol", None, None, "prow", None),
        ),
        check_vma=False,
    )
```

profile of v0, /device:TPU:6, one launch (start us, length us, event | category | flops | bytes accessed | tf_op | source)
XLA Modules:
  0.0 709.8 jit_solution(2358859241753849992)
XLA Ops:
  7.2 0.0 all-gather.7.cloned.1.call-start
  7.2 1.7 slice_bitcast_fusion.1
  8.9 0.0 all-gather.7.cloned.1.call-update
  8.9 0.0 copy-start.3
  8.9 58.6 %all-gather.7.cloned.1.call-done = bf16[1,1,16,256,1,1,256]{6,3,5,4,1,0,2:T(8,128)(2,1)} async-done(((bf16[1,1,1,256,1,1,256]{6,3,5,4,1,0,2:T(8,128)(2,1)}), bf16[1,1,16,256,1,1,256]{6,3,5,4,1,0,2:T(8,128)(2,1)}) %all-gather.7.cloned.1.call-update) | async-done | bytes 2097168 | tf_op jit(solution)/shard_map/all_gather | solution.py:11
  67.5 7.1 %all-to-all-start.1 = ((bf16[1,1,16,256,1,1,256]{6,3,5,4,1,0,2:T(8,128)(2,1)}), bf16[1,1,16,256,1,1,256]{6,3,5,4,1,0,2:T(8,128)(2,1)S(1)}, u32[]{:S(2)}, u32[]{:S(2)}) async-start(bf16[1,1,16,256,1,1,256]{6,3,5,4,1,0,2:T(8,128)(2,1)} %all-gather.7.cloned.1.call-done), calls=%async_computation.2 | async-start | bytes 4194304 | tf_op jit(solution)/shard_map/all_to_all | solution.py:12
  74.6 0.0 all-gather.5.cloned.1.call-start
  74.7 0.7 all-gather.5.cloned.1.call-update
  75.4 0.0 reduce-scatter.7.cloned.1.call-start
  75.4 0.7 constant_dynamic-slice_fusion
  76.2 0.6 fusion.21
  76.7 48.6 %all-to-all-done.1 = bf16[1,1,16,256,1,1,256]{6,3,5,4,1,0,2:T(8,128)(2,1)S(1)} async-done(((bf16[1,1,16,256,1,1,256]{6,3,5,4,1,0,2:T(8,128)(2,1)}), bf16[1,1,16,256,1,1,256]{6,3,5,4,1,0,2:T(8,128)(2,1)S(1)}, u32[]{:S(2)}, u32[]{:S(2)}) %all-to-all-start.1) | async-done | bytes 2097184 | tf_op jit(solution)/shard_map/all_to_all | solution.py:12
  125.3 0.0 copy-done.3
  125.3 3.3 convolution_bitcast_fusion.2
  128.6 0.0 reduce-scatter.7.cloned.1.call-update
  128.6 11.7 %all-gather.5.cloned.1.call-done = bf16[1,1,16,256,1,1,256]{6,3,5,4,1,0,2:T(8,128)(2,1)} async-done(((bf16[1,1,1,256,1,1,256]{6,3,5,4,1,0,2:T(8,128)(2,1)}), bf16[1,1,16,256,1,1,256]{6,3,5,4,1,0,2:T(8,128)(2,1)}) %all-gather.5.cloned.1.call-update) | async-done | bytes 2097168 | tf_op jit(solution)/shard_map/all_gather | solution.py:11
  140.3 4.4 all-to-all-start
  144.7 0.0 reduce-scatter.5.cloned.1.call-start
  144.8 0.6 fusion.22
  145.3 57.8 %all-to-all-done = bf16[1,1,16,256,1,1,256]{6,3,5,4,1,0,2:T(8,128)(2,1)S(1)} async-done(((bf16[1,1,16,256,1,1,256]{6,3,5,4,1,0,2:T(8,128)(2,1)}), bf16[1,1,16,256,1,1,256]{6,3,5,4,1,0,2:T(8,128)(2,1)S(1)}, u32[]{:S(2)}, u32[]{:S(2)}) %all-to-all-start) | async-done | bytes 2097184 | tf_op jit(solution)/shard_map/all_to_all | solution.py:12
  203.2 3.4 convolution_bitcast_fusion.3
  206.5 0.0 reduce-scatter.5.cloned.1.call-update
  206.6 0.0 all-gather.11.cloned.1.call-start
  206.6 61.2 %reduce-scatter.7.cloned.1.call-done = f32[1,1,1,256,1,1,256]{6,3,5,4,2,1,0:T(8,128)} async-done(((f32[1,1,1,256,1,16,256]{6,3,5,4,2,1,0:T(8,128)}), f32[1,1,1,256,1,1,256]{6,3,5,4,2,1,0:T(8,128)}) %reduce-scatter.7.cloned.1.call-update) | async-done | bytes 262160 | tf_op jit(solution)/shard_map/reduce_scatter | solution.py:16
  267.9 1.6 fusion.24
  269.5 0.0 all-gather.11.cloned.1.call-update
  269.5 0.0 all-gather.9.cloned.1.call-start
  269.6 101.1 %reduce-scatter.5.cloned.1.call-done = f32[1,1,1,256,1,1,256]{6,3,5,4,2,1,0:T(8,128)} async-done(((f32[1,1,1,256,1,16,256]{6,3,5,4,2,1,0:T(8,128)}), f32[1,1,1,256,1,1,256]{6,3,5,4,2,1,0:T(8,128)}) %reduce-scatter.5.cloned.1.call-update) | async-done | bytes 262160 | tf_op jit(solution)/shard_map/reduce_scatter | solution.py:16
  370.7 1.6 fusion.23
  372.3 0.0 all-gather.9.cloned.1.call-update
  372.3 0.0 reduce-scatter.11.cloned.1.call-start
  372.4 73.7 %all-gather.11.cloned.1.call-done = bf16[1,1,1,256,1,16,256]{6,3,4,2,1,0,5:T(8,128)(2,1)} async-done(((bf16[1,1,1,256,1,1,256]{6,3,4,2,1,0,5:T(8,128)(2,1)}), bf16[1,1,1,256,1,16,256]{6,3,4,2,1,0,5:T(8,128)(2,1)}) %all-gather.11.cloned.1.call-update) | async-done | bytes 2097168 | tf_op jit(solution)/shard_map/all_gather | solution.py:18
  446.0 0.0 copy-done
  446.1 4.3 convolution_bitcast_fusion
  450.4 0.0 reduce-scatter.11.cloned.1.call-update
  450.4 0.0 reduce-scatter.9.cloned.1.call-start
  450.4 68.8 %all-gather.9.cloned.1.call-done = bf16[1,1,1,256,1,16,256]{6,3,4,2,1,0,5:T(8,128)(2,1)} async-done(((bf16[1,1,1,256,1,1,256]{6,3,4,2,1,0,5:T(8,128)(2,1)}), bf16[1,1,1,256,1,16,256]{6,3,4,2,1,0,5:T(8,128)(2,1)}) %all-gather.9.cloned.1.call-update) | async-done | bytes 2097168 | tf_op jit(solution)/shard_map/all_gather | solution.py:18
  519.2 4.3 convolution_bitcast_fusion.1
  523.6 0.0 reduce-scatter.9.cloned.1.call-update
  523.6 0.9 copy-done.4
  524.5 0.1 copy.23
  524.6 0.1 copy.22
  524.8 0.7 pad_maximum_fusion
  525.5 83.6 %reduce-scatter.11.cloned.1.call-done = f32[1,1,1,256,1,1,256]{3,6,5,4,2,1,0:T(8,128)} async-done(((f32[1,1,1,256,1,16,256]{3,6,5,4,2,1,0:T(8,128)}), f32[1,1,1,256,1,1,256]{3,6,5,4,2,1,0:T(8,128)}) %reduce-scatter.11.cloned.1.call-update) | async-done | bytes 262160 | tf_op jit(solution)/shard_map/reduce_scatter | solution.py:22
  609.1 1.0 subtract_convert_fusion
  610.1 91.0 %reduce-scatter.9.cloned.1.call-done = f32[1,1,1,256,1,1,256]{3,6,5,4,2,1,0:T(8,128)} async-done(((f32[1,1,1,256,1,16,256]{3,6,5,4,2,1,0:T(8,128)}), f32[1,1,1,256,1,1,256]{3,6,5,4,2,1,0:T(8,128)}) %reduce-scatter.9.cloned.1.call-update) | async-done | bytes 262160 | tf_op jit(solution)/shard_map/reduce_scatter | solution.py:22
  701.1 1.0 subtract_convert_fusion.1
  702.1 0.8 copy.21
  (10 shorter events, 0.1 us)
Async XLA Ops:
  7.2 60.3 %all-gather.7.cloned.1.call-start = ((), (), s32[]{:S(2)}) async-start(), calls=%async_computation.8 | async-start | bytes 2228224 | tf_op jit(solution)/shard_map/all_gather | solution.py:11
  8.9 116.4 %copy-start.3 = (bf16[2,1,1,256,1,1,256]{6,3,5,4,2,1,0:T(8,128)(2,1)S(1)}, bf16[2,1,1,256,1,1,256]{6,3,5,4,2,1,0:T(8,128)(2,1)}, u32[]{:S(2)}) copy-start(bf16[2,1,1,256,1,1,256]{6,3,5,4,2,1,0:T(8,128)(2,1)} %param.4) | copy-start | bytes 786436
  67.5 57.8 %all-to-all-start.1 = ((bf16[1,1,16,256,1,1,256]{6,3,5,4,1,0,2:T(8,128)(2,1)}), bf16[1,1,16,256,1,1,256]{6,3,5,4,1,0,2:T(8,128)(2,1)S(1)}, u32[]{:S(2)}, u32[]{:S(2)}) async-start(bf16[1,1,16,256,1,1,256]{6,3,5,4,1,0,2:T(8,128)(2,1)} %all-gather.7.cloned.1.call-done), calls=%async_computation.2 | async-start | bytes 4194304 | tf_op jit(solution)/shard_map/all_to_all | solution.py:12
  74.6 65.7 %all-gather.5.cloned.1.call-start = ((), (), s32[]{:S(2)}) async-start(), calls=%async_computation.6 | async-start | bytes 2228224 | tf_op jit(solution)/shard_map/all_gather | solution.py:11
  75.4 192.5 %reduce-scatter.7.cloned.1.call-start = ((), (), s32[]{:S(2)}) async-start(), calls=%async_computation.9 | async-start | bytes 4456448 | tf_op jit(solution)/shard_map/reduce_scatter | solution.py:16
  140.3 62.8 %all-to-all-start = ((bf16[1,1,16,256,1,1,256]{6,3,5,4,1,0,2:T(8,128)(2,1)}), bf16[1,1,16,256,1,1,256]{6,3,5,4,1,0,2:T(8,128)(2,1)S(1)}, u32[]{:S(2)}, u32[]{:S(2)}) async-start(bf16[1,1,16,256,1,1,256]{6,3,5,4,1,0,2:T(8,128)(2,1)} %all-gather.5.cloned.1.call-done), calls=%async_computation | async-start | bytes 4194304 | tf_op jit(solution)/shard_map/all_to_all | solution.py:12
  144.7 226.0 %reduce-scatter.5.cloned.1.call-start = ((), (), s32[]{:S(2)}) async-start(), calls=%async_computation.7 | async-start | bytes 4456448 | tf_op jit(solution)/shard_map/reduce_scatter | solution.py:16
  206.5 239.5 %copy-start = (bf16[2,1,1,256,1,1,256]{6,3,5,4,2,1,0:T(8,128)(2,1)S(1)}, bf16[2,1,1,256,1,1,256]{6,3,5,4,2,1,0:T(8,128)(2,1)}, u32[]{:S(2)}) copy-start(bf16[2,1,1,256,1,1,256]{6,3,5,4,2,1,0:T(8,128)(2,1)} %param.5) | copy-start | bytes 786436
  206.6 239.5 %all-gather.11.cloned.1.call-start = ((), (), s32[]{:S(2)}) async-start(), calls=%async_computation.12 | async-start | bytes 2228224 | tf_op jit(solution)/shard_map/all_gather | solution.py:18
  269.5 249.7 %all-gather.9.cloned.1.call-start = ((), (), s32[]{:S(2)}) async-start(), calls=%async_computation.10 | async-start | bytes 2228224 | tf_op jit(solution)/shard_map/all_gather | solution.py:18
  372.3 236.8 %reduce-scatter.11.cloned.1.call-start = ((), (), s32[]{:S(2)}) async-start(), calls=%async_computation.13 | async-start | bytes 4456448 | tf_op jit(solution)/shard_map/reduce_scatter | solution.py:22
  450.4 250.7 %reduce-scatter.9.cloned.1.call-start = ((), (), s32[]{:S(2)}) async-start(), calls=%async_computation.11 | async-start | bytes 4456448 | tf_op jit(solution)/shard_map/reduce_scatter | solution.py:22
  523.5 0.9 copy-start.4
  523.6 1.2 copy-start.1
  523.6 1.2 copy-start.2
Sparse Core Ops, SparseCore 0:
  11.3 56.1 all-gather.6
  78.8 61.5 all-gather.4
  142.9 124.9 reduce-scatter.6
  270.3 100.3 reduce-scatter.4
  372.9 73.1 all-gather.10
  448.3 70.8 all-gather.8
  523.5 85.5 reduce-scatter.10
  614.1 86.9 reduce-scatter.8
where the time goes:
time: 710 us
  waiting for transfers between devices  657 us (93%)
  matrix products  15.3 us (2%)
  between operations  14.2 us (2%)
  starting transfers between devices  11.8 us (2%)
  other arithmetic  7.16 us (1%)
    reduce_scatter x2, waiting for transfers between devices, invert_window(): lax.psum_scatter(inner_sum, 'prow', scatter_dimension=5, tiled=True)  175 us
    reduce_scatter x2, waiting for transfers between devices, invert_window(): lax.psum_scatter(partial_terms, 'pcol', scatter_dimension=5, tiled=True)  162 us
    all_gather x2, waiting for transfers between devices, invert_window(): all_cols = lax.all_gather(sigma_off, 'pcol', axis=5, tiled=True)  142 us
    all_to_all x2, waiting for transfers between devices, invert_window(): lax.all_to_all(gathered, 'pcol', split_axis=2, concat_axis=5, tiled=True)  106 us
    all_gather x2, waiting for transfers between devices, invert_window(): gathered = lax.all_gather(panel_local, 'prow', axis=2, tiled=True)  70.3 us
  transfers between devices with their start and end apart: 10, of which 10 were waited for; matrix products, arithmetic and copies ran while one was open for 3% of the time, Pallas kernels for 0%

commit v1 on v0

v1 whole, which is shorter than its diff:
```python
import jax
import jax.numpy as jnp
from jax import lax
from jax.sharding import PartitionSpec as P

NX = 4
NZ = 8


def row_perm(fn):
    pairs = []
    for i in range(16):
        yh, x, c = fn(i // 8, (i // 2) % NX, i % 2)
        pairs.append((i, yh * 8 + (x % NX) * 2 + c))
    return pairs


def col_perm(fn):
    pairs = []
    for i in range(16):
        z, yl = fn(i // 2, i % 2)
        pairs.append((i, (z % NZ) * 2 + yl))
    return pairs


def flip_perm(cross):
    pairs = []
    for p in range(16):
        for q in range(16):
            to_p = (q // 2) * 2 + (p % 2) ^ cross
            to_q = (p // 2) * 2 + q % 2
            pairs.append((p * 16 + q, to_p * 16 + to_q))
    return pairs


SWAP = col_perm(lambda z, yl: (z, 1 - yl))
UP = col_perm(lambda z, yl: (z + 1, yl))
DOWN = col_perm(lambda z, yl: (z - 1, yl))


def z_ring(piece):
    found = [(0, piece)]
    ahead = behind = piece
    for step in range(1, NZ // 2):
        ahead = lax.ppermute(ahead, "pcol", UP)
        behind = lax.ppermute(behind, "pcol", DOWN)
        found += [(-step, ahead), (step, behind)]
    half = piece.shape[0] // 2
    ahead = lax.ppermute(ahead[:half], "pcol", UP)
    behind = lax.ppermute(behind[half:], "pcol", DOWN)
    found.append((NZ // 2, jnp.concatenate([ahead, behind], axis=0)))
    return found


def on_device(anc_inverse, factor_panel, diag_inverse, block_pattern):
    p = lax.axis_index("prow")
    q = lax.axis_index("pcol")
    yh, x, c = p // 8, (p // 2) % NX, p % 2
    z, yl = q // 2, q % 2
    anc = anc_inverse.reshape(2, 256, 256)
    panel = factor_panel.reshape(2, 256, 256)
    diag = diag_inverse.reshape(2, 256, 256)
    keep = lax.dynamic_slice(block_pattern, (0, p, q), (2, 1, 1))
    masked = jnp.where(keep != 0, anc, jnp.zeros_like(anc))

    def mine(pair):
        return jnp.where(yl == 0, pair[0], pair[1])

    def other(pair):
        return jnp.where(yl == 0, pair[1], pair[0])

    def swap(block):
        return lax.ppermute(block, "pcol", SWAP)

    own_m, got_m = mine(masked), swap(other(masked))
    own_u, got_u = mine(panel), swap(other(panel))
    same = yl == c
    m_piece = jnp.concatenate(
        [jnp.where(same, own_m, got_m), jnp.where(same, got_m, own_m)], axis=1
    )
    u_piece = jnp.concatenate(
        [jnp.where(yl == 0, own_u, got_u), jnp.where(yl == 0, got_u, own_u)], axis=1
    )
    u_far = lax.ppermute(u_piece, "prow", row_perm(lambda h, x, c: (1 - h, x, c)))
    both = jnp.stack([u_piece, u_far])
    groups = [both]
    for step in range(1, NX):
        groups.append(
            lax.ppermute(both, "prow", row_perm(lambda h, x, c: (h, x + step, c)))
        )
    cross = row_perm(lambda h, x, c: (h, x, 1 - c))
    u_all = jnp.stack([jnp.stack([g, lax.ppermute(g, "prow", cross)]) for g in groups])

    def u_rows(offset):
        owner = (z + offset + NZ) % NZ
        back = (x - owner % NX + NX) % NX
        away = jnp.where(owner // NX == yh, 0, 1)
        return lax.dynamic_slice(
            u_all, (back, 0, away, 0, 0), (1, 2, 1, 256, 512)
        ).reshape(512, 512)

    product = jnp.zeros((256, 512), jnp.float32)
    for offset, piece in z_ring(m_piece):
        product += jnp.dot(piece, u_rows(offset), preferred_element_type=jnp.float32)
    off = (-product).astype(jnp.bfloat16)
    left, right = off[:, :256], off[:, 256:]
    off_mine = jnp.where(yl == 0, left, right)
    off_got = swap(jnp.where(yl == 0, right, left))
    same_core = lax.ppermute(
        jnp.where(c == 0, left, right), ("prow", "pcol"), flip_perm(0)
    )
    cross_core = lax.ppermute(
        jnp.where(c == 0, right, left), ("prow", "pcol"), flip_perm(1)
    )
    o_piece = jnp.concatenate([same_core, cross_core], axis=0)
    inner = jnp.zeros((512, 256), jnp.float32)
    for offset, piece in z_ring(o_piece):
        inner += lax.dot_general(
            u_rows(offset),
            piece,
            (((0,), (0,)), ((), ())),
            preferred_element_type=jnp.float32,
        )
    d_mine, d_got = mine(diag), swap(other(diag))
    top, bottom = inner[:256], inner[256:]
    diag_mine = (
        d_mine.astype(jnp.float32) - jnp.where(yl == 0, top, bottom)
    ).astype(jnp.bfloat16)
    diag_got = swap(
        (d_got.astype(jnp.float32) - jnp.where(yl == 0, bottom, top)).astype(
            jnp.bfloat16
        )
    )

    def place(own, got):
        return jnp.stack(
            [jnp.where(yl == 0, own, got), jnp.where(yl == 0, got, own)]
        ).reshape(anc_inverse.shape)

    return place(off_mine, off_got), place(diag_mine, diag_got)


def solution(mesh):
    return jax.shard_map(
        on_device,
        mesh=mesh,
        in_specs=(
            P(None, None, "prow", None, None, "pcol", None),
            P(None, None, "prow", None, None, "pcol", None),
            P(None, None, "pcol", None, None, "prow", None),
            P(),
        ),
        out_specs=(
            P(None, None, "prow", None, None, "pcol", None),
            P(None, None, "pcol", None, None, "prow", None),
        ),
        check_vma=False,
    )
```

time: 710 us -> 142 us (0.20)
  the two profiles are of different devices: /device:TPU:6 before, /device:TPU:8 now
where the time goes in v1:
time: 142 us
  starting transfers between devices  77.3 us (54%)
  waiting for transfers between devices  43.1 us (30%)
  other arithmetic  12.8 us (9%)
  matrix products  6.04 us (4%)
    ppermute x6, starting transfers between devices, z_ring(): behind = lax.ppermute(behind, 'pcol', DOWN)  50.3 us
    ppermute x6, waiting for transfers between devices, z_ring(): behind = lax.ppermute(behind, 'pcol', DOWN)  12.6 us
    ppermute x6, waiting for transfers between devices, z_ring(): ahead = lax.ppermute(ahead, 'pcol', UP)  11.8 us
    ppermute x5, starting transfers between devices, swap(): return lax.ppermute(block, 'pcol', SWAP)  9.01 us
    ppermute x5, waiting for transfers between devices, swap(): return lax.ppermute(block, 'pcol', SWAP)  7.69 us
    ppermute x3, waiting for transfers between devices, on_device(): lax.ppermute(both, 'prow', row_perm(lambda h, x, c: (h, x + step, c)))  7 us
    ppermute x2, starting transfers between devices, z_ring(): behind = lax.ppermute(behind[half:], 'pcol', DOWN)  6.95 us
    ppermute x3, starting transfers between devices, on_device(): lax.ppermute(both, 'prow', row_perm(lambda h, x, c: (h, x + step, c)))  5.78 us
  transfers between devices with their start and end apart: 31, of which 17 were waited for; matrix products, arithmetic and copies ran while one was open for 11% of the time, Pallas kernels for 0%

profile of v1, /device:TPU:8, one launch (start us, length us, event | category | flops | bytes accessed | tf_op | source)
XLA Modules:
  0.0 141.7 jit_solution(16645531689160818936)
XLA Ops:
  0.6 1.0 select_bitcast_fusion.5
  1.6 2.3 %collective-permute-start.1 = (bf16[256,256]{1,0:T(8,128)(2,1)S(1)}, bf16[256,256]{1,0:T(8,128)(2,1)S(1)}, u32[]{:S(2)}, u32[]{:S(2)}) collective-permute-start(bf16[256,256]{1,0:T(8,128)(2,1)S(1)} %select_bitcast_fusion.5), channel_id=1, source_target_pairs={{0,1},{1,0},{2,3},{3,2},{4,5},{5,4},{6,7},{7,6},{8,9},{9,8},{10,11... | collective-permute-start | bytes 393224 | tf_op jit(solution)/shard_map/ppermute | solution.py:73
  3.9 0.9 compare_reduce_fusion
  4.8 1.0 bitcast_select_fusion
  6.0 1.7 %collective-permute-done.1 = bf16[256,256]{1,0:T(8,128)(2,1)S(1)} collective-permute-done((bf16[256,256]{1,0:T(8,128)(2,1)S(1)}, bf16[256,256]{1,0:T(8,128)(2,1)S(1)}, u32[]{:S(2)}, u32[]{:S(2)}) %collective-permute-start.1) | collective-permute-done | bytes 131104 | tf_op jit(solution)/shard_map/ppermute | solution.py:73
  7.7 1.0 bitcast_select_fusion.2
  8.8 1.9 %collective-permute-start.2 = (bf16[256,512]{1,0:T(8,128)(2,1)S(1)}, bf16[256,512]{1,0:T(8,128)(2,1)S(1)}, u32[]{:S(2)}, u32[]{:S(2)}) collective-permute-start(bf16[256,512]{1,0:T(8,128)(2,1)S(1)} %get-tuple-element.27), channel_id=1, source_target_pairs={{0,128},{16,144},{32,160},{48,176},{64,192},{80,208},{96,224},{112... | collective-permute-start | bytes 786440 | tf_op jit(solution)/shard_map/ppermute | solution.py:84
  11.0 5.6 %collective-permute-start.11 = (bf16[256,512]{1,0:T(8,128)(2,1)S(1)}, bf16[256,512]{1,0:T(8,128)(2,1)S(1)}, u32[]{:S(2)}, u32[]{:S(2)}) collective-permute-start(bf16[256,512]{1,0:T(8,128)(2,1)S(1)} %pad_maximum_fusion.2), channel_id=1, source_target_pairs={{0,14},{1,15},{2,0},{3,1},{4,2},{5,3},{6,4},{7,5},{8,6},{9,7},{10,... | collective-permute-start | bytes 786440 | tf_op jit(solution)/shard_map/ppermute | solution.py:46
  16.8 1.6 %collective-permute-start.4 = (bf16[2,256,512]{2,1,0:T(8,128)(2,1)S(1)}, bf16[2,256,512]{2,1,0:T(8,128)(2,1)S(1)}, u32[]{:S(2)}, u32[]{:S(2)}) collective-permute-start(bf16[2,256,512]{2,1,0:T(8,128)(2,1)S(1)} %get-tuple-element.17), channel_id=1, source_target_pairs={{0,32},{16,48},{32,64},{48,80},{64,96},{80,112},{96,0},{112,16},{1... | collective-permute-start | bytes 1572872 | tf_op jit(solution)/shard_map/ppermute | solution.py:89
  18.4 1.9 %collective-permute-start.10 = (bf16[256,512]{1,0:T(8,128)(2,1)S(1)}, bf16[256,512]{1,0:T(8,128)(2,1)S(1)}, u32[]{:S(2)}, u32[]{:S(2)}) collective-permute-start(bf16[256,512]{1,0:T(8,128)(2,1)S(1)} %pad_maximum_fusion.2), channel_id=1, source_target_pairs={{0,2},{1,3},{2,4},{3,5},{4,6},{5,7},{6,8},{7,9},{8,10},{9,11},{10,... | collective-permute-start | bytes 786440 | tf_op jit(solution)/shard_map/ppermute | solution.py:45
  20.3 2.7 %collective-permute-start.6 = (bf16[2,256,512]{2,1,0:T(8,128)(2,1)S(1)}, bf16[2,256,512]{2,1,0:T(8,128)(2,1)S(1)}, u32[]{:S(2)}, u32[]{:S(2)}) collective-permute-start(bf16[2,256,512]{2,1,0:T(8,128)(2,1)S(1)} %get-tuple-element.17), channel_id=1, source_target_pairs={{0,64},{16,80},{32,96},{48,112},{64,0},{80,16},{96,32},{112,48},{1... | collective-permute-start | bytes 1572872 | tf_op jit(solution)/shard_map/ppermute | solution.py:89
  23.1 3.9 %collective-permute-start.13 = (bf16[256,512]{1,0:T(8,128)(2,1)S(1)}, bf16[256,512]{1,0:T(8,128)(2,1)}, u32[]{:S(2)}, u32[]{:S(2)}) collective-permute-start(bf16[256,512]{1,0:T(8,128)(2,1)S(1)} %collective-permute-done.11), channel_id=1, source_target_pairs={{0,14},{1,15},{2,0},{3,1},{4,2},{5,3},{6,4},{7,5},{8,6},{9,7},{10,... | collective-permute-start | bytes 786440 | tf_op jit(solution)/shard_map/ppermute | solution.py:46
  27.0 1.4 %collective-permute-start.8 = (bf16[2,256,512]{2,1,0:T(8,128)(2,1)S(1)}, bf16[2,256,512]{2,1,0:T(8,128)(2,1)S(1)}, u32[]{:S(2)}, u32[]{:S(2)}) collective-permute-start(bf16[2,256,512]{2,1,0:T(8,128)(2,1)S(1)} %get-tuple-element.17), channel_id=1, source_target_pairs={{0,96},{16,112},{32,0},{48,16},{64,32},{80,48},{96,64},{112,80},{1... | collective-permute-start | bytes 1572872 | tf_op jit(solution)/shard_map/ppermute | solution.py:89
  28.6 2.3 %collective-permute-done.13 = bf16[256,512]{1,0:T(8,128)(2,1)} collective-permute-done((bf16[256,512]{1,0:T(8,128)(2,1)S(1)}, bf16[256,512]{1,0:T(8,128)(2,1)}, u32[]{:S(2)}, u32[]{:S(2)}) %collective-permute-start.13) | collective-permute-done | bytes 262176 | tf_op jit(solution)/shard_map/ppermute | solution.py:46
  30.9 1.1 collective-permute-done.4
  32.0 4.3 %collective-permute-done.12 = bf16[256,512]{1,0:T(8,128)(2,1)S(1)} collective-permute-done((bf16[256,512]{1,0:T(8,128)(2,1)S(1)}, bf16[256,512]{1,0:T(8,128)(2,1)S(1)}, u32[]{:S(2)}, u32[]{:S(2)}) %collective-permute-start.12) | collective-permute-done | bytes 262176 | tf_op jit(solution)/shard_map/ppermute | solution.py:45
  36.3 5.9 %collective-permute-done.6 = bf16[2,256,512]{2,1,0:T(8,128)(2,1)S(1)} collective-permute-done((bf16[2,256,512]{2,1,0:T(8,128)(2,1)S(1)}, bf16[2,256,512]{2,1,0:T(8,128)(2,1)S(1)}, u32[]{:S(2)}, u32[]{:S(2)}) %collective-permute-start.6) | collective-permute-done | bytes 524320 | tf_op jit(solution)/shard_map/ppermute | solution.py:89
  42.2 5.3 %collective-permute-start.15 = (bf16[256,512]{1,0:T(8,128)(2,1)}, bf16[256,512]{1,0:T(8,128)(2,1)S(1)}, u32[]{:S(2)}, u32[]{:S(2)}) collective-permute-start(bf16[256,512]{1,0:T(8,128)(2,1)} %collective-permute-done.13), channel_id=1, source_target_pairs={{0,14},{1,15},{2,0},{3,1},{4,2},{5,3},{6,4},{7,5},{8,6},{9,7},{10,... | collective-permute-start | bytes 786440 | tf_op jit(solution)/shard_map/ppermute | solution.py:46
  47.6 0.6 collective-permute-start.9
  48.3 3.4 %collective-permute-done.15 = bf16[256,512]{1,0:T(8,128)(2,1)S(1)} collective-permute-done((bf16[256,512]{1,0:T(8,128)(2,1)}, bf16[256,512]{1,0:T(8,128)(2,1)S(1)}, u32[]{:S(2)}, u32[]{:S(2)}) %collective-permute-start.15) | collective-permute-done | bytes 262176 | tf_op jit(solution)/shard_map/ppermute | solution.py:46
  51.7 3.7 %collective-permute-start.17 = (bf16[128,512]{1,0:T(8,128)(2,1)S(1)}, bf16[128,512]{1,0:T(8,128)(2,1)S(1)}, u32[]{:S(2)}, u32[]{:S(2)}) collective-permute-start(bf16[128,512]{1,0:T(8,128)(2,1)S(1)} %slice.69), channel_id=1, source_target_pairs={{0,14},{1,15},{2,0},{3,1},{4,2},{5,3},{6,4},{7,5},{8,6},{9,7},{10,... | collective-permute-start | bytes 393224 | tf_op jit(solution)/shard_map/ppermute | solution.py:50
  55.4 1.1 maximum_bitcast_fusion
  56.6 1.1 maximum_bitcast_fusion.1
  57.7 1.1 maximum_bitcast_fusion.2
  58.9 1.1 maximum_bitcast_fusion.3
  60.0 0.6 pad_maximum_fusion
  60.6 0.5 constant_dynamic-slice_fusion.2
  61.1 0.4 copy-done.12
  62.5 1.2 fusion.26
  65.1 3.2 %collective-permute-start.18 = (bf16[256,256]{1,0:T(8,128)(2,1)S(1)}, bf16[256,256]{1,0:T(8,128)(2,1)}, u32[]{:S(2)}, u32[]{:S(2)}) collective-permute-start(bf16[256,256]{1,0:T(8,128)(2,1)S(1)} %broadcast_select_fusion.4), channel_id=1, source_target_pairs={{0,1},{1,0},{2,3},{3,2},{4,5},{5,4},{6,7},{7,6},{8,9},{9,8},{10,11... | collective-permute-start | bytes 393224 | tf_op jit(solution)/shard_map/ppermute | solution.py:73
  68.2 3.1 %collective-permute-done.18 = bf16[256,256]{1,0:T(8,128)(2,1)} collective-permute-done((bf16[256,256]{1,0:T(8,128)(2,1)S(1)}, bf16[256,256]{1,0:T(8,128)(2,1)}, u32[]{:S(2)}, u32[]{:S(2)}) %collective-permute-start.18) | collective-permute-done | bytes 131104 | tf_op jit(solution)/shard_map/ppermute | solution.py:73
  71.3 0.9 select_bitcast_fusion.4
  72.2 0.7 collective-permute-start.19
  73.1 1.3 collective-permute-done.20
  74.4 28.0 %collective-permute-start.22 = (bf16[512,256]{1,0:T(8,128)(2,1)S(1)}, bf16[512,256]{1,0:T(8,128)(2,1)S(1)}, u32[]{:S(2)}, u32[]{:S(2)}) collective-permute-start(bf16[512,256]{1,0:T(8,128)(2,1)S(1)} %constant_dynamic-update-slice_fusion), channel_id=1, source_target_pairs={{0,14},{1,15},{2,0},{3,1},{4,2},{5,3},{6,4},{7,5},{8,6},{9,7},{10,... | collective-permute-start | bytes 786440 | tf_op jit(solution)/shard_map/ppermute | solution.py:46
  102.4 1.0 select_bitcast_fusion.2
  103.4 1.7 %collective-permute-start.29 = (bf16[256,256]{1,0:T(8,128)(2,1)S(1)}, bf16[256,256]{1,0:T(8,128)(2,1)S(1)}, u32[]{:S(2)}, u32[]{:S(2)}) collective-permute-start(bf16[256,256]{1,0:T(8,128)(2,1)S(1)} %select_bitcast_fusion.2), channel_id=1, source_target_pairs={{0,1},{1,0},{2,3},{3,2},{4,5},{5,4},{6,7},{7,6},{8,9},{9,8},{10,11... | collective-permute-start | bytes 393224 | tf_op jit(solution)/shard_map/ppermute | solution.py:73
  105.1 3.1 %collective-permute-done.22 = bf16[512,256]{1,0:T(8,128)(2,1)S(1)} collective-permute-done((bf16[512,256]{1,0:T(8,128)(2,1)S(1)}, bf16[512,256]{1,0:T(8,128)(2,1)S(1)}, u32[]{:S(2)}, u32[]{:S(2)}) %collective-permute-start.22) | collective-permute-done | bytes 262176 | tf_op jit(solution)/shard_map/ppermute | solution.py:46
  108.2 3.7 %collective-permute-start.24 = (bf16[512,256]{1,0:T(8,128)(2,1)S(1)}, bf16[512,256]{1,0:T(8,128)(2,1)S(1)}, u32[]{:S(2)}, u32[]{:S(2)}) collective-permute-start(bf16[512,256]{1,0:T(8,128)(2,1)S(1)} %collective-permute-done.22), channel_id=1, source_target_pairs={{0,14},{1,15},{2,0},{3,1},{4,2},{5,3},{6,4},{7,5},{8,6},{9,7},{10,... | collective-permute-start | bytes 786440 | tf_op jit(solution)/shard_map/ppermute | solution.py:46
  113.1 3.9 %collective-permute-done.24 = bf16[512,256]{1,0:T(8,128)(2,1)S(1)} collective-permute-done((bf16[512,256]{1,0:T(8,128)(2,1)S(1)}, bf16[512,256]{1,0:T(8,128)(2,1)S(1)}, u32[]{:S(2)}, u32[]{:S(2)}) %collective-permute-start.24) | collective-permute-done | bytes 262176 | tf_op jit(solution)/shard_map/ppermute | solution.py:46
  117.0 3.7 %collective-permute-start.26 = (bf16[512,256]{1,0:T(8,128)(2,1)S(1)}, bf16[512,256]{1,0:T(8,128)(2,1)S(1)}, u32[]{:S(2)}, u32[]{:S(2)}) collective-permute-start(bf16[512,256]{1,0:T(8,128)(2,1)S(1)} %collective-permute-done.24), channel_id=1, source_target_pairs={{0,14},{1,15},{2,0},{3,1},{4,2},{5,3},{6,4},{7,5},{8,6},{9,7},{10,... | collective-permute-start | bytes 786440 | tf_op jit(solution)/shard_map/ppermute | solution.py:46
  121.5 7.2 %collective-permute-done.25 = bf16[512,256]{1,0:T(8,128)(2,1)S(1)} collective-permute-done((bf16[512,256]{1,0:T(8,128)(2,1)S(1)}, bf16[512,256]{1,0:T(8,128)(2,1)S(1)}, u32[]{:S(2)}, u32[]{:S(2)}) %collective-permute-start.25) | collective-permute-done | bytes 262176 | tf_op jit(solution)/shard_map/ppermute | solution.py:45
  128.9 3.3 %collective-permute-start.28 = (bf16[256,256]{1,0:T(8,128)(2,1)S(1)}, bf16[256,256]{1,0:T(8,128)(2,1)S(1)}, u32[]{:S(2)}, u32[]{:S(2)}) collective-permute-start(bf16[256,256]{1,0:T(8,128)(2,1)S(1)} %slice.73), channel_id=1, source_target_pairs={{0,14},{1,15},{2,0},{3,1},{4,2},{5,3},{6,4},{7,5},{8,6},{9,7},{10,... | collective-permute-start | bytes 393224 | tf_op jit(solution)/shard_map/ppermute | solution.py:50
  132.5 2.5 %collective-permute-done.27 = bf16[256,256]{1,0:T(8,128)(2,1)S(1)} collective-permute-done((bf16[256,256]{1,0:T(8,128)(2,1)S(1)}, bf16[256,256]{1,0:T(8,128)(2,1)S(1)}, u32[]{:S(2)}, u32[]{:S(2)}) %collective-permute-start.27) | collective-permute-done | bytes 131104 | tf_op jit(solution)/shard_map/ppermute | solution.py:49
  135.8 1.7 %collective-permute-start.30 = (bf16[256,256]{1,0:T(8,128)(2,1)S(1)}, bf16[256,256]{1,0:T(8,128)(2,1)S(1)}, u32[]{:S(2)}, u32[]{:S(2)}) collective-permute-start(bf16[256,256]{1,0:T(8,128)(2,1)S(1)} %subtract_convert_fusion), channel_id=1, source_target_pairs={{0,1},{1,0},{2,3},{3,2},{4,5},{5,4},{6,7},{7,6},{8,9},{9,8},{10,11... | collective-permute-start | bytes 393224 | tf_op jit(solution)/shard_map/ppermute | solution.py:73
  137.5 0.7 maximum_bitcast_fusion.4
  138.2 2.6 %collective-permute-done.30 = bf16[256,256]{1,0:T(8,128)(2,1)S(1)} collective-permute-done((bf16[256,256]{1,0:T(8,128)(2,1)S(1)}, bf16[256,256]{1,0:T(8,128)(2,1)S(1)}, u32[]{:S(2)}, u32[]{:S(2)}) %collective-permute-start.30) | collective-permute-done | bytes 131104 | tf_op jit(solution)/shard_map/ppermute | solution.py:73
  140.9 0.7 maximum_bitcast_fusion.5
  (89 shorter events, 6.4 us)
Async XLA Ops:
  1.6 6.1 %collective-permute-start.1 = (bf16[256,256]{1,0:T(8,128)(2,1)S(1)}, bf16[256,256]{1,0:T(8,128)(2,1)S(1)}, u32[]{:S(2)}, u32[]{:S(2)}) collective-permute-start(bf16[256,256]{1,0:T(8,128)(2,1)S(1)} %select_bitcast_fusion.5), channel_id=1, source_target_pairs={{0,1},{1,0},{2,3},{3,2},{4,5},{5,4},{6,7},{7,6},{8,9},{9,8},{10,11... | collective-permute-start | bytes 393224 | tf_op jit(solution)/shard_map/ppermute | solution.py:73
  5.9 5.1 %collective-permute-start = (bf16[256,256]{1,0:T(8,128)(2,1)S(1)}, bf16[256,256]{1,0:T(8,128)(2,1)S(1)}, u32[]{:S(2)}, u32[]{:S(2)}) collective-permute-start(bf16[256,256]{1,0:T(8,128)(2,1)S(1)} %select_bitcast_fusion.6), channel_id=1, source_target_pairs={{0,1},{1,0},{2,3},{3,2},{4,5},{5,4},{6,7},{7,6},{8,9},{9,8},{10,11... | collective-permute-start | bytes 393224 | tf_op jit(solution)/shard_map/ppermute | solution.py:73
  8.8 8.0 %collective-permute-start.2 = (bf16[256,512]{1,0:T(8,128)(2,1)S(1)}, bf16[256,512]{1,0:T(8,128)(2,1)S(1)}, u32[]{:S(2)}, u32[]{:S(2)}) collective-permute-start(bf16[256,512]{1,0:T(8,128)(2,1)S(1)} %get-tuple-element.27), channel_id=1, source_target_pairs={{0,128},{16,144},{32,160},{48,176},{64,192},{80,208},{96,224},{112... | collective-permute-start | bytes 786440 | tf_op jit(solution)/shard_map/ppermute | solution.py:84
  11.0 12.1 %collective-permute-start.11 = (bf16[256,512]{1,0:T(8,128)(2,1)S(1)}, bf16[256,512]{1,0:T(8,128)(2,1)S(1)}, u32[]{:S(2)}, u32[]{:S(2)}) collective-permute-start(bf16[256,512]{1,0:T(8,128)(2,1)S(1)} %pad_maximum_fusion.2), channel_id=1, source_target_pairs={{0,14},{1,15},{2,0},{3,1},{4,2},{5,3},{6,4},{7,5},{8,6},{9,7},{10,... | collective-permute-start | bytes 786440 | tf_op jit(solution)/shard_map/ppermute | solution.py:46
  16.8 15.2 %collective-permute-start.4 = (bf16[2,256,512]{2,1,0:T(8,128)(2,1)S(1)}, bf16[2,256,512]{2,1,0:T(8,128)(2,1)S(1)}, u32[]{:S(2)}, u32[]{:S(2)}) collective-permute-start(bf16[2,256,512]{2,1,0:T(8,128)(2,1)S(1)} %get-tuple-element.17), channel_id=1, source_target_pairs={{0,32},{16,48},{32,64},{48,80},{64,96},{80,112},{96,0},{112,16},{1... | collective-permute-start | bytes 1572872 | tf_op jit(solution)/shard_map/ppermute | solution.py:89
  18.4 10.2 %collective-permute-start.10 = (bf16[256,512]{1,0:T(8,128)(2,1)S(1)}, bf16[256,512]{1,0:T(8,128)(2,1)S(1)}, u32[]{:S(2)}, u32[]{:S(2)}) collective-permute-start(bf16[256,512]{1,0:T(8,128)(2,1)S(1)} %pad_maximum_fusion.2), channel_id=1, source_target_pairs={{0,2},{1,3},{2,4},{3,5},{4,6},{5,7},{6,8},{7,9},{8,10},{9,11},{10,... | collective-permute-start | bytes 786440 | tf_op jit(solution)/shard_map/ppermute | solution.py:45
  20.3 21.9 %collective-permute-start.6 = (bf16[2,256,512]{2,1,0:T(8,128)(2,1)S(1)}, bf16[2,256,512]{2,1,0:T(8,128)(2,1)S(1)}, u32[]{:S(2)}, u32[]{:S(2)}) collective-permute-start(bf16[2,256,512]{2,1,0:T(8,128)(2,1)S(1)} %get-tuple-element.17), channel_id=1, source_target_pairs={{0,64},{16,80},{32,96},{48,112},{64,0},{80,16},{96,32},{112,48},{1... | collective-permute-start | bytes 1572872 | tf_op jit(solution)/shard_map/ppermute | solution.py:89
  23.1 24.5 %copy-start.9 = (bf16[256,512]{1,0:T(8,128)(2,1)}, bf16[256,512]{1,0:T(8,128)(2,1)S(1)}, u32[]{:S(2)}) copy-start(bf16[256,512]{1,0:T(8,128)(2,1)S(1)} %collective-permute-done.11) | copy-start | bytes 786436
  23.1 7.8 %collective-permute-start.13 = (bf16[256,512]{1,0:T(8,128)(2,1)S(1)}, bf16[256,512]{1,0:T(8,128)(2,1)}, u32[]{:S(2)}, u32[]{:S(2)}) collective-permute-start(bf16[256,512]{1,0:T(8,128)(2,1)S(1)} %collective-permute-done.11), channel_id=1, source_target_pairs={{0,14},{1,15},{2,0},{3,1},{4,2},{5,3},{6,4},{7,5},{8,6},{9,7},{10,... | collective-permute-start | bytes 786440 | tf_op jit(solution)/shard_map/ppermute | solution.py:46
  27.0 20.5 %collective-permute-start.8 = (bf16[2,256,512]{2,1,0:T(8,128)(2,1)S(1)}, bf16[2,256,512]{2,1,0:T(8,128)(2,1)S(1)}, u32[]{:S(2)}, u32[]{:S(2)}) collective-permute-start(bf16[2,256,512]{2,1,0:T(8,128)(2,1)S(1)} %get-tuple-element.17), channel_id=1, source_target_pairs={{0,96},{16,112},{32,0},{48,16},{64,32},{80,48},{96,64},{112,80},{1... | collective-permute-start | bytes 1572872 | tf_op jit(solution)/shard_map/ppermute | solution.py:89
  28.6 18.9 %copy-start.11 = (bf16[256,512]{1,0:T(8,128)(2,1)}, bf16[256,512]{1,0:T(8,128)(2,1)S(1)}, u32[]{:S(2)}) copy-start(bf16[256,512]{1,0:T(8,128)(2,1)S(1)} %collective-permute-done.10) | copy-start | bytes 786436
  28.6 7.7 %collective-permute-start.12 = (bf16[256,512]{1,0:T(8,128)(2,1)S(1)}, bf16[256,512]{1,0:T(8,128)(2,1)S(1)}, u32[]{:S(2)}, u32[]{:S(2)}) collective-permute-start(bf16[256,512]{1,0:T(8,128)(2,1)S(1)} %collective-permute-done.10), channel_id=1, source_target_pairs={{0,2},{1,3},{2,4},{3,5},{4,6},{5,7},{6,8},{7,9},{8,10},{9,11},{10,... | collective-permute-start | bytes 786440 | tf_op jit(solution)/shard_map/ppermute | solution.py:45
  30.9 20.8 %collective-permute-start.3 = (bf16[2,256,512]{2,1,0:T(8,128)(2,1)S(1)}, bf16[2,256,512]{2,1,0:T(8,128)(2,1)}, u32[]{:S(2)}, u32[]{:S(2)}) collective-permute-start(bf16[2,256,512]{2,1,0:T(8,128)(2,1)S(1)} %get-tuple-element.17), channel_id=1, source_target_pairs={{0,16},{16,0},{32,48},{48,32},{64,80},{80,64},{96,112},{112,96},{1... | collective-permute-start | bytes 1572872 | tf_op jit(solution)/shard_map/ppermute | solution.py:92
  32.0 24.5 %collective-permute-start.5 = (bf16[2,256,512]{2,1,0:T(8,128)(2,1)S(1)}, bf16[2,256,512]{2,1,0:T(8,128)(2,1)}, u32[]{:S(2)}, u32[]{:S(2)}) collective-permute-start(bf16[2,256,512]{2,1,0:T(8,128)(2,1)S(1)} %collective-permute-done.4), channel_id=1, source_target_pairs={{0,16},{16,0},{32,48},{48,32},{64,80},{80,64},{96,112},{112,96},{1... | collective-permute-start | bytes 1572872 | tf_op jit(solution)/shard_map/ppermute | solution.py:92
  36.3 11.2 %copy-start.13 = (bf16[256,512]{1,0:T(8,128)(2,1)}, bf16[256,512]{1,0:T(8,128)(2,1)S(1)}, u32[]{:S(2)}) copy-start(bf16[256,512]{1,0:T(8,128)(2,1)S(1)} %collective-permute-done.12) | copy-start | bytes 786436
  36.3 11.2 %collective-permute-start.14 = (bf16[256,512]{1,0:T(8,128)(2,1)S(1)}, bf16[256,512]{1,0:T(8,128)(2,1)S(1)}, u32[]{:S(2)}, u32[]{:S(2)}) collective-permute-start(bf16[256,512]{1,0:T(8,128)(2,1)S(1)} %collective-permute-done.12), channel_id=1, source_target_pairs={{0,2},{1,3},{2,4},{3,5},{4,6},{5,7},{6,8},{7,9},{8,10},{9,11},{10,... | collective-permute-start | bytes 786440 | tf_op jit(solution)/shard_map/ppermute | solution.py:45
  42.2 9.5 %collective-permute-start.15 = (bf16[256,512]{1,0:T(8,128)(2,1)}, bf16[256,512]{1,0:T(8,128)(2,1)S(1)}, u32[]{:S(2)}, u32[]{:S(2)}) collective-permute-start(bf16[256,512]{1,0:T(8,128)(2,1)} %collective-permute-done.13), channel_id=1, source_target_pairs={{0,14},{1,15},{2,0},{3,1},{4,2},{5,3},{6,4},{7,5},{8,6},{9,7},{10,... | collective-permute-start | bytes 786440 | tf_op jit(solution)/shard_map/ppermute | solution.py:46
  47.5 10.2 %collective-permute-start.7 = (bf16[2,256,512]{2,1,0:T(8,128)(2,1)S(1)}, bf16[2,256,512]{2,1,0:T(8,128)(2,1)}, u32[]{:S(2)}, u32[]{:S(2)}) collective-permute-start(bf16[2,256,512]{2,1,0:T(8,128)(2,1)S(1)} %collective-permute-done.6), channel_id=1, source_target_pairs={{0,16},{16,0},{32,48},{48,32},{64,80},{80,64},{96,112},{112,96},{1... | collective-permute-start | bytes 1572872 | tf_op jit(solution)/shard_map/ppermute | solution.py:92
  47.5 12.5 %copy-start.5 = (bf16[256,512]{1,0:T(8,128)(2,1)}, bf16[256,512]{1,0:T(8,128)(2,1)S(1)}, u32[]{:S(2)}) copy-start(bf16[256,512]{1,0:T(8,128)(2,1)S(1)} %collective-permute-done.14) | copy-start | bytes 786436
  47.6 11.3 %collective-permute-start.9 = (bf16[2,256,512]{2,1,0:T(8,128)(2,1)S(1)}, bf16[2,256,512]{2,1,0:T(8,128)(2,1)}, u32[]{:S(2)}, u32[]{:S(2)}) collective-permute-start(bf16[2,256,512]{2,1,0:T(8,128)(2,1)S(1)} %collective-permute-done.8), channel_id=1, source_target_pairs={{0,16},{16,0},{32,48},{48,32},{64,80},{80,64},{96,112},{112,96},{1... | collective-permute-start | bytes 1572872 | tf_op jit(solution)/shard_map/ppermute | solution.py:92
  51.7 8.3 %copy-start.7 = (bf16[256,512]{1,0:T(8,128)(2,1)}, bf16[256,512]{1,0:T(8,128)(2,1)S(1)}, u32[]{:S(2)}) copy-start(bf16[256,512]{1,0:T(8,128)(2,1)S(1)} %collective-permute-done.15) | copy-start | bytes 786436
  51.7 12.7 %collective-permute-start.16 = (bf16[128,512]{1,0:T(8,128)(2,1)S(1)}, bf16[128,512]{1,0:T(8,128)(2,1)S(1)}, u32[]{:S(2)}, u32[]{:S(2)}) collective-permute-start(bf16[128,512]{1,0:T(8,128)(2,1)S(1)} %slice.68), channel_id=1, source_target_pairs={{0,2},{1,3},{2,4},{3,5},{4,6},{5,7},{6,8},{7,9},{8,10},{9,11},{10,... | collective-permute-start | bytes 393224 | tf_op jit(solution)/shard_map/ppermute | solution.py:49
  51.7 12.7 %collective-permute-start.17 = (bf16[128,512]{1,0:T(8,128)(2,1)S(1)}, bf16[128,512]{1,0:T(8,128)(2,1)S(1)}, u32[]{:S(2)}, u32[]{:S(2)}) collective-permute-start(bf16[128,512]{1,0:T(8,128)(2,1)S(1)} %slice.69), channel_id=1, source_target_pairs={{0,14},{1,15},{2,0},{3,1},{4,2},{5,3},{6,4},{7,5},{8,6},{9,7},{10,... | collective-permute-start | bytes 393224 | tf_op jit(solution)/shard_map/ppermute | solution.py:50
  60.6 1.0 copy-start.12
  60.6 1.2 copy-start.10
  61.1 3.0 %copy-start = (bf16[1,2,1,256,512]{4,3,2,1,0:T(8,128)(2,1)}, bf16[1,2,1,256,512]{4,3,2,1,0:T(8,128)(2,1)S(1)}, u32[]{:S(2)}) copy-start(bf16[1,2,1,256,512]{4,3,2,1,0:T(8,128)(2,1)S(1)} %get-tuple-element.15) | copy-start | bytes 1572868
  61.1 3.3 %copy-start.2 = (bf16[1,2,1,256,512]{4,3,2,1,0:T(8,128)(2,1)}, bf16[1,2,1,256,512]{4,3,2,1,0:T(8,128)(2,1)S(1)}, u32[]{:S(2)}) copy-start(bf16[1,2,1,256,512]{4,3,2,1,0:T(8,128)(2,1)S(1)} %get-tuple-element.9) | copy-start | bytes 1572868
  61.1 2.6 %copy-start.14 = (bf16[256,512]{1,0:T(8,128)(2,1)S(1)}, bf16[256,512]{1,0:T(8,128)(2,1)}, u32[]{:S(2)}) copy-start(bf16[256,512]{1,0:T(8,128)(2,1)} %copy-done.13) | copy-start | bytes 786436
  61.6 2.5 %copy-start.8 = (bf16[256,512]{1,0:T(8,128)(2,1)S(1)}, bf16[256,512]{1,0:T(8,128)(2,1)}, u32[]{:S(2)}) copy-start(bf16[256,512]{1,0:T(8,128)(2,1)} %copy-done.7) | copy-start | bytes 786436
  62.2 2.5 %copy-start.6 = (bf16[256,512]{1,0:T(8,128)(2,1)S(1)}, bf16[256,512]{1,0:T(8,128)(2,1)}, u32[]{:S(2)}) copy-start(bf16[256,512]{1,0:T(8,128)(2,1)} %copy-done.5) | copy-start | bytes 786436
  65.1 6.2 %collective-permute-start.18 = (bf16[256,256]{1,0:T(8,128)(2,1)S(1)}, bf16[256,256]{1,0:T(8,128)(2,1)}, u32[]{:S(2)}, u32[]{:S(2)}) collective-permute-start(bf16[256,256]{1,0:T(8,128)(2,1)S(1)} %broadcast_select_fusion.4), channel_id=1, source_target_pairs={{0,1},{1,0},{2,3},{3,2},{4,5},{5,4},{6,7},{7,6},{8,9},{9,8},{10,11... | collective-permute-start | bytes 393224 | tf_op jit(solution)/shard_map/ppermute | solution.py:73
  68.2 44.5 %copy-start.1 = (bf16[1,2,1,256,512]{4,3,2,1,0:T(8,128)(2,1)S(1)}, bf16[1,2,1,256,512]{4,3,2,1,0:T(8,128)(2,1)}, u32[]{:S(2)}) copy-start(bf16[1,2,1,256,512]{4,3,2,1,0:T(8,128)(2,1)} %copy-done) | copy-start | bytes 1572868
  72.2 0.8 collective-permute-start.19
  72.9 1.4 %collective-permute-start.20 = (bf16[256,256]{1,0:T(8,128)(2,1)S(1)}, bf16[256,256]{1,0:T(8,128)(2,1)S(1)}, u32[]{:S(2)}, u32[]{:S(2)}) collective-permute-start(bf16[256,256]{1,0:T(8,128)(2,1)S(1)} %get-tuple-element.24), channel_id=1, source_target_pairs={{0,16},{1,17},{2,48},{3,49},{4,80},{5,81},{6,112},{7,113},{8,144},... | collective-permute-start | bytes 393224 | tf_op jit(solution)/shard_map/ppermute | solution.py:112
  74.4 33.9 %collective-permute-start.22 = (bf16[512,256]{1,0:T(8,128)(2,1)S(1)}, bf16[512,256]{1,0:T(8,128)(2,1)S(1)}, u32[]{:S(2)}, u32[]{:S(2)}) collective-permute-start(bf16[512,256]{1,0:T(8,128)(2,1)S(1)} %constant_dynamic-update-slice_fusion), channel_id=1, source_target_pairs={{0,14},{1,15},{2,0},{3,1},{4,2},{5,3},{6,4},{7,5},{8,6},{9,7},{10,... | collective-permute-start | bytes 786440 | tf_op jit(solution)/shard_map/ppermute | solution.py:46
  102.4 9.9 %collective-permute-start.21 = (bf16[512,256]{1,0:T(8,128)(2,1)S(1)}, bf16[512,256]{1,0:T(8,128)(2,1)S(1)}, u32[]{:S(2)}, u32[]{:S(2)}) collective-permute-start(bf16[512,256]{1,0:T(8,128)(2,1)S(1)} %constant_dynamic-update-slice_fusion), channel_id=1, source_target_pairs={{0,2},{1,3},{2,4},{3,5},{4,6},{5,7},{6,8},{7,9},{8,10},{9,11},{10,... | collective-permute-start | bytes 786440 | tf_op jit(solution)/shard_map/ppermute | solution.py:45
  103.4 32.3 %collective-permute-start.29 = (bf16[256,256]{1,0:T(8,128)(2,1)S(1)}, bf16[256,256]{1,0:T(8,128)(2,1)S(1)}, u32[]{:S(2)}, u32[]{:S(2)}) collective-permute-start(bf16[256,256]{1,0:T(8,128)(2,1)S(1)} %select_bitcast_fusion.2), channel_id=1, source_target_pairs={{0,1},{1,0},{2,3},{3,2},{4,5},{5,4},{6,7},{7,6},{8,9},{9,8},{10,11... | collective-permute-start | bytes 393224 | tf_op jit(solution)/shard_map/ppermute | solution.py:73
  108.2 8.7 %collective-permute-start.24 = (bf16[512,256]{1,0:T(8,128)(2,1)S(1)}, bf16[512,256]{1,0:T(8,128)(2,1)S(1)}, u32[]{:S(2)}, u32[]{:S(2)}) collective-permute-start(bf16[512,256]{1,0:T(8,128)(2,1)S(1)} %collective-permute-done.22), channel_id=1, source_target_pairs={{0,14},{1,15},{2,0},{3,1},{4,2},{5,3},{6,4},{7,5},{8,6},{9,7},{10,... | collective-permute-start | bytes 786440 | tf_op jit(solution)/shard_map/ppermute | solution.py:46
  112.6 22.4 %copy-start.3 = (bf16[1,2,1,256,512]{4,3,2,1,0:T(8,128)(2,1)S(1)}, bf16[1,2,1,256,512]{4,3,2,1,0:T(8,128)(2,1)}, u32[]{:S(2)}) copy-start(bf16[1,2,1,256,512]{4,3,2,1,0:T(8,128)(2,1)} %copy-done.2) | copy-start | bytes 1572868
  112.6 8.5 %collective-permute-start.23 = (bf16[512,256]{1,0:T(8,128)(2,1)S(1)}, bf16[512,256]{1,0:T(8,128)(2,1)S(1)}, u32[]{:S(2)}, u32[]{:S(2)}) collective-permute-start(bf16[512,256]{1,0:T(8,128)(2,1)S(1)} %collective-permute-done.21), channel_id=1, source_target_pairs={{0,2},{1,3},{2,4},{3,5},{4,6},{5,7},{6,8},{7,9},{8,10},{9,11},{10,... | collective-permute-start | bytes 786440 | tf_op jit(solution)/shard_map/ppermute | solution.py:45
  117.0 11.9 %collective-permute-start.26 = (bf16[512,256]{1,0:T(8,128)(2,1)S(1)}, bf16[512,256]{1,0:T(8,128)(2,1)S(1)}, u32[]{:S(2)}, u32[]{:S(2)}) collective-permute-start(bf16[512,256]{1,0:T(8,128)(2,1)S(1)} %collective-permute-done.24), channel_id=1, source_target_pairs={{0,14},{1,15},{2,0},{3,1},{4,2},{5,3},{6,4},{7,5},{8,6},{9,7},{10,... | collective-permute-start | bytes 786440 | tf_op jit(solution)/shard_map/ppermute | solution.py:46
  121.1 7.6 %collective-permute-start.25 = (bf16[512,256]{1,0:T(8,128)(2,1)S(1)}, bf16[512,256]{1,0:T(8,128)(2,1)S(1)}, u32[]{:S(2)}, u32[]{:S(2)}) collective-permute-start(bf16[512,256]{1,0:T(8,128)(2,1)S(1)} %collective-permute-done.23), channel_id=1, source_target_pairs={{0,2},{1,3},{2,4},{3,5},{4,6},{5,7},{6,8},{7,9},{8,10},{9,11},{10,... | collective-permute-start | bytes 786440 | tf_op jit(solution)/shard_map/ppermute | solution.py:45
  121.5 19.3 %copy-start.4 = (bf16[2,1,1,256,1,1,256]{6,3,5,4,2,1,0:T(8,128)(2,1)S(1)}, bf16[2,1,1,256,1,1,256]{6,3,5,4,2,1,0:T(8,128)(2,1)}, u32[]{:S(2)}) copy-start(bf16[2,1,1,256,1,1,256]{6,3,5,4,2,1,0:T(8,128)(2,1)} %param.6) | copy-start | bytes 786436
  128.7 6.3 %collective-permute-start.27 = (bf16[256,256]{1,0:T(8,128)(2,1)S(1)}, bf16[256,256]{1,0:T(8,128)(2,1)S(1)}, u32[]{:S(2)}, u32[]{:S(2)}) collective-permute-start(bf16[256,256]{1,0:T(8,128)(2,1)S(1)} %slice.72), channel_id=1, source_target_pairs={{0,2},{1,3},{2,4},{3,5},{4,6},{5,7},{6,8},{7,9},{8,10},{9,11},{10,... | collective-permute-start | bytes 393224 | tf_op jit(solution)/shard_map/ppermute | solution.py:49
  128.9 6.1 %collective-permute-start.28 = (bf16[256,256]{1,0:T(8,128)(2,1)S(1)}, bf16[256,256]{1,0:T(8,128)(2,1)S(1)}, u32[]{:S(2)}, u32[]{:S(2)}) collective-permute-start(bf16[256,256]{1,0:T(8,128)(2,1)S(1)} %slice.73), channel_id=1, source_target_pairs={{0,14},{1,15},{2,0},{3,1},{4,2},{5,3},{6,4},{7,5},{8,6},{9,7},{10,... | collective-permute-start | bytes 393224 | tf_op jit(solution)/shard_map/ppermute | solution.py:50
  135.8 5.1 %collective-permute-start.30 = (bf16[256,256]{1,0:T(8,128)(2,1)S(1)}, bf16[256,256]{1,0:T(8,128)(2,1)S(1)}, u32[]{:S(2)}, u32[]{:S(2)}) collective-permute-start(bf16[256,256]{1,0:T(8,128)(2,1)S(1)} %subtract_convert_fusion), channel_id=1, source_target_pairs={{0,1},{1,0},{2,3},{3,2},{4,5},{5,4},{6,7},{7,6},{8,9},{9,8},{10,11... | collective-permute-start | bytes 393224 | tf_op jit(solution)/shard_map/ppermute | solution.py:73

commit v2 on v1

v2 whole, which is shorter than its diff:
```python
import jax
import jax.numpy as jnp
from jax import lax
from jax.sharding import PartitionSpec as P

NX = 4
NZ = 8


def row_perm(fn):
    pairs = []
    for i in range(16):
        yh, x, c = fn(i // 8, (i // 2) % NX, i % 2)
        pairs.append((i, yh * 8 + (x % NX) * 2 + c))
    return pairs


def col_perm(fn):
    pairs = []
    for i in range(16):
        z, yl = fn(i // 2, i % 2)
        pairs.append((i, (z % NZ) * 2 + yl))
    return pairs


def both_perm(fn):
    pairs = []
    for p in range(16):
        for q in range(16):
            chip, c, z, yl = fn(p // 2, p % 2, q // 2, q % 2)
            pairs.append((p * 16 + q, (chip * 2 + c) * 16 + (z % NZ) * 2 + yl))
    return pairs


def move(block, pairs):
    return lax.ppermute(block, ("prow", "pcol"), pairs)


SWAP = col_perm(lambda z, yl: (z, 1 - yl))
UP = col_perm(lambda z, yl: (z + 1, yl))
DOWN = col_perm(lambda z, yl: (z - 1, yl))
CROSS = row_perm(lambda h, x, c: (h, x, 1 - c))
FLIP_H = row_perm(lambda h, x, c: (1 - h, x, c))
SPLIT = both_perm(lambda chip, c, z, yl: (chip, c, z + 1 - 2 * c, yl))


def z_ring(piece, core, beside=()):
    found = [(0, piece)]
    swapped = []
    ahead = behind = piece
    for step in range(1, NZ // 2):
        hold = None
        if 2 <= step < 2 + len(beside):
            ahead, behind, hold = lax.optimization_barrier(
                (ahead, behind, beside[step - 2])
            )
            swapped.append(lax.ppermute(hold, "pcol", SWAP))
        ahead = lax.ppermute(ahead, "pcol", UP)
        behind = lax.ppermute(behind, "pcol", DOWN)
        if hold is not None:
            ahead, behind, swapped[-1] = lax.optimization_barrier(
                (ahead, behind, swapped[-1])
            )
        found += [(-step, ahead), (step, behind)]
    found.append((NZ // 2, move(jnp.where(core == 0, ahead, behind), SPLIT)))
    return found, swapped


def on_device(anc_inverse, factor_panel, diag_inverse, block_pattern):
    p = lax.axis_index("prow")
    q = lax.axis_index("pcol")
    yh, x, c = p // 8, (p // 2) % NX, p % 2
    z, yl = q // 2, q % 2
    anc = anc_inverse.reshape(2, 256, 256)
    panel = factor_panel.reshape(2, 256, 256)
    diag = diag_inverse.reshape(2, 256, 256)

    def mine(pair):
        return jnp.where(yl == 0, pair[0], pair[1])

    def other(pair):
        return jnp.where(yl == 0, pair[1], pair[0])

    def swap(block):
        return lax.ppermute(block, "pcol", SWAP)

    near = move(
        jnp.where(c == 0, anc[0], anc[1]),
        both_perm(lambda chip, c, z, yl: (chip, yl, z, c)),
    )
    far = move(
        jnp.where(c == 0, anc[1], anc[0]),
        both_perm(lambda chip, c, z, yl: (chip, yl, z, 1 - c)),
    )
    keep = lax.dynamic_slice(block_pattern, (yl, p - c, 2 * z + c), (1, 2, 1))
    keep = jnp.where(yl == 0, keep, keep[:, ::-1]).reshape(2, 1, 1) != 0
    m_piece = jnp.stack([near, far])
    m_piece = jnp.where(keep, m_piece, jnp.zeros_like(m_piece)).reshape(512, 256)

    own_u, got_u = mine(panel), swap(other(panel))
    u_piece = jnp.concatenate(
        [jnp.where(yl == 0, own_u, got_u), jnp.where(yl == 0, got_u, own_u)], axis=1
    )

    def along_x(block, step):
        return lax.ppermute(block, "prow", row_perm(lambda h, x, c: (h, x + step, c)))

    u_far = lax.ppermute(u_piece, "prow", FLIP_H)
    u_two = along_x(u_piece, 2)
    both = jnp.stack([u_piece, u_far])
    u_one = along_x(both, 1)
    u_three = along_x(both, 3)
    u_two_far = lax.ppermute(u_two, "prow", FLIP_H)
    u_all = jnp.zeros((NX, 2, 256, 512), jnp.bfloat16)
    for back, away, block in (
        (0, 0, both),
        (2, 0, u_two[None]),
        (2, 1, u_two_far[None]),
        (1, 0, u_one),
        (3, 0, u_three),
    ):
        u_all = lax.dynamic_update_slice(u_all, block[None], (back, away, 0, 0))

    def find(offset):
        owner = (z + offset + NZ) % NZ
        back = (x - owner % NX + NX) % NX
        return back, jnp.where(owner // NX == yh, 0, 1)

    def u_rows(offset):
        at = (*find(offset), 0, 0)
        return lax.dynamic_slice(u_all, at, (1, 1, 256, 512)).reshape(256, 512)

    product = jnp.zeros((512, 512), jnp.float32)
    for offset, piece in z_ring(m_piece, c)[0]:
        product += jnp.dot(piece, u_rows(offset), preferred_element_type=jnp.float32)
    first, second = product[:256], product[256:]
    theirs = lax.ppermute(jnp.where(yl == c, second, first), "prow", CROSS)
    off = (-(jnp.where(yl == c, first, second) + theirs)).astype(jnp.bfloat16)
    left, right = off[:, :256], off[:, 256:]
    off_mine = jnp.where(yl == 0, left, right)

    u_both = jnp.stack([u_all, lax.ppermute(u_all, "prow", CROSS)], axis=2)

    def u_pair(offset):
        at = (*find(offset), 0, 0, 0)
        return lax.dynamic_slice(u_both, at, (1, 1, 2, 256, 512)).reshape(512, 512)

    straight = move(
        jnp.where(c == 0, left, right),
        both_perm(lambda chip, c, z, yl: (z, c, chip, yl)),
    )
    around = lax.ppermute(jnp.where(c == 0, right, left), "prow", FLIP_H)
    around = move(around, both_perm(lambda chip, c, z, yl: (z, 1 - c, chip ^ 4, yl)))
    o_piece = jnp.concatenate([straight, around], axis=0)
    ring, (off_got, d_got) = z_ring(
        o_piece, c, (jnp.where(yl == 0, right, left), other(diag))
    )
    d_mine = mine(diag)
    total = jnp.zeros((512, 256), jnp.float32)
    for offset, piece in ring:
        total += lax.dot_general(
            u_pair(offset),
            piece,
            (((0,), (0,)), ((), ())),
            preferred_element_type=jnp.float32,
        )
    top, bottom = total[:256], total[256:]
    diag_mine = (
        d_mine.astype(jnp.float32) - jnp.where(yl == 0, top, bottom)
    ).astype(jnp.bfloat16)
    diag_got = swap(
        (d_got.astype(jnp.float32) - jnp.where(yl == 0, bottom, top)).astype(
            jnp.bfloat16
        )
    )

    def place(own, got):
        return jnp.stack(
            [jnp.where(yl == 0, own, got), jnp.where(yl == 0, got, own)]
        ).reshape(anc_inverse.shape)

    return place(off_mine, off_got), place(diag_mine, diag_got)


def solution(mesh):
    return jax.shard_map(
        on_device,
        mesh=mesh,
        in_specs=(
            P(None, None, "prow", None, None, "pcol", None),
            P(None, None, "prow", None, None, "pcol", None),
            P(None, None, "pcol", None, None, "prow", None),
            P(),
        ),
        out_specs=(
            P(None, None, "prow", None, None, "pcol", None),
            P(None, None, "pcol", None, None, "prow", None),
        ),
        check_vma=False,
    )
```

time: 142 us -> 116 us (0.82)
  the two profiles are of different devices: /device:TPU:8 before, /device:TPU:6 now
where the time goes in v2:
time: 116 us
  starting transfers between devices  55.5 us (48%)
  waiting for transfers between devices  47.6 us (41%)
  other arithmetic  5.66 us (5%)
  matrix products  5.21 us (4%)
  local copies, waits for them, and re-layouts  1.2 us (1%)
    ppermute x6, waiting for transfers between devices, move(): return lax.ppermute(block, ('prow', 'pcol'), pairs)  19.3 us
    ppermute x6, starting transfers between devices, z_ring(): behind = lax.ppermute(behind, 'pcol', DOWN)  16.3 us
    ppermute x6, waiting for transfers between devices, z_ring(): ahead = lax.ppermute(ahead, 'pcol', UP)  11.7 us
    ppermute x6, starting transfers between devices, z_ring(): ahead = lax.ppermute(ahead, 'pcol', UP)  9.61 us
    ppermute x6, starting transfers between devices, move(): return lax.ppermute(block, ('prow', 'pcol'), pairs)  9.44 us
    ppermute x2, waiting for transfers between devices, z_ring(): swapped.append(lax.ppermute(hold, 'pcol', SWAP))  6.96 us
    ppermute x3, starting transfers between devices, along_x(): lax.ppermute(block, 'prow', row_perm(lambda h, x, c: (h, x + step, c)))  3.6 us
    ppermute x2, starting transfers between devices, swap(): return lax.ppermute(block, 'pcol', SWAP)  3.45 us
  transfers between devices with their start and end apart: 30, of which 14 were waited for; matrix products, arithmetic and copies ran while one was open for 7% of the time, Pallas kernels for 0%

profile of v2, /device:TPU:6, one launch (start us, length us, event | category | flops | bytes accessed | tf_op | source)
XLA Modules:
  0.0 116.2 jit_solution(17151350675889091937)
XLA Ops:
  0.7 1.0 select_bitcast_fusion.7
  1.7 1.7 %collective-permute-start.1 = (bf16[256,256]{1,0:T(8,128)(2,1)S(1)}, bf16[256,256]{1,0:T(8,128)(2,1)S(1)}, u32[]{:S(2)}, u32[]{:S(2)}) collective-permute-start(bf16[256,256]{1,0:T(8,128)(2,1)S(1)} %get-tuple-element.52), channel_id=1, source_target_pairs={{0,1},{1,17},{2,3},{3,19},{4,5},{5,21},{6,7},{7,23},{8,9},{9,25},{... | collective-permute-start | bytes 393224 | tf_op jit(solution)/shard_map/ppermute | solution.py:36
  3.4 0.7 collective-permute-start
  4.0 1.0 select_bitcast_fusion.5
  5.0 1.9 %collective-permute-start.2 = (bf16[256,256]{1,0:T(8,128)(2,1)S(1)}, bf16[256,256]{1,0:T(8,128)(2,1)S(1)}, u32[]{:S(2)}, u32[]{:S(2)}) collective-permute-start(bf16[256,256]{1,0:T(8,128)(2,1)S(1)} %select_bitcast_fusion.5), channel_id=1, source_target_pairs={{0,1},{1,0},{2,3},{3,2},{4,5},{5,4},{6,7},{7,6},{8,9},{9,8},{10,11... | collective-permute-start | bytes 393224 | tf_op jit(solution)/shard_map/ppermute | solution.py:85
  6.9 0.8 dynamic_slice.51
  7.7 0.9 compare_reduce_fusion
  8.9 2.0 %collective-permute-start.8 = (bf16[512,256]{1,0:T(8,128)(2,1)S(1)}, bf16[512,256]{1,0:T(8,128)(2,1)S(1)}, u32[]{:S(2)}, u32[]{:S(2)}) collective-permute-start(bf16[512,256]{1,0:T(8,128)(2,1)S(1)} %bitcast_select_fusion), channel_id=1, source_target_pairs={{0,2},{1,3},{2,4},{3,5},{4,6},{5,7},{6,8},{7,9},{8,10},{9,11},{10,... | collective-permute-start | bytes 786440 | tf_op jit(solution)/shard_map/ppermute | solution.py:58
  10.9 4.0 %collective-permute-start.9 = (bf16[512,256]{1,0:T(8,128)(2,1)S(1)}, bf16[512,256]{1,0:T(8,128)(2,1)S(1)}, u32[]{:S(2)}, u32[]{:S(2)}) collective-permute-start(bf16[512,256]{1,0:T(8,128)(2,1)S(1)} %bitcast_select_fusion), channel_id=1, source_target_pairs={{0,14},{1,15},{2,0},{3,1},{4,2},{5,3},{6,4},{7,5},{8,6},{9,7},{10,... | collective-permute-start | bytes 786440 | tf_op jit(solution)/shard_map/ppermute | solution.py:59
  15.0 1.5 %collective-permute-start.4 = (bf16[256,512]{1,0:T(8,128)(2,1)S(1)}, bf16[256,512]{1,0:T(8,128)(2,1)S(1)}, u32[]{:S(2)}, u32[]{:S(2)}) collective-permute-start(bf16[256,512]{1,0:T(8,128)(2,1)S(1)} %get-tuple-element.50), channel_id=1, source_target_pairs={{0,64},{16,80},{32,96},{48,112},{64,0},{80,16},{96,32},{112,48},{1... | collective-permute-start | bytes 786440 | tf_op jit(solution)/shard_map/ppermute | solution.py:106
  16.5 3.2 %collective-permute-start.3 = (bf16[256,512]{1,0:T(8,128)(2,1)S(1)}, bf16[256,512]{1,0:T(8,128)(2,1)S(1)}, u32[]{:S(2)}, u32[]{:S(2)}) collective-permute-start(bf16[256,512]{1,0:T(8,128)(2,1)S(1)} %get-tuple-element.50), channel_id=1, source_target_pairs={{0,128},{16,144},{32,160},{48,176},{64,192},{80,208},{96,224},{112... | collective-permute-start | bytes 786440 | tf_op jit(solution)/shard_map/ppermute | solution.py:108
  19.7 1.5 %collective-permute-done.8 = bf16[512,256]{1,0:T(8,128)(2,1)S(1)} collective-permute-done((bf16[512,256]{1,0:T(8,128)(2,1)S(1)}, bf16[512,256]{1,0:T(8,128)(2,1)S(1)}, u32[]{:S(2)}, u32[]{:S(2)}) %collective-permute-start.8) | collective-permute-done | bytes 262176 | tf_op jit(solution)/shard_map/ppermute | solution.py:58
  21.2 3.2 %collective-permute-start.11 = (bf16[512,256]{1,0:T(8,128)(2,1)S(1)}, bf16[512,256]{1,0:T(8,128)(2,1)S(1)}, u32[]{:S(2)}, u32[]{:S(2)}) collective-permute-start(bf16[512,256]{1,0:T(8,128)(2,1)S(1)} %collective-permute-done.9), channel_id=1, source_target_pairs={{0,14},{1,15},{2,0},{3,1},{4,2},{5,3},{6,4},{7,5},{8,6},{9,7},{10,... | collective-permute-start | bytes 786440 | tf_op jit(solution)/shard_map/ppermute | solution.py:59
  24.4 3.2 %collective-permute-start.5 = (bf16[256,512]{1,0:T(8,128)(2,1)S(1)}, bf16[256,512]{1,0:T(8,128)(2,1)S(1)}, u32[]{:S(2)}, u32[]{:S(2)}) collective-permute-start(bf16[256,512]{1,0:T(8,128)(2,1)S(1)} %collective-permute-done.4), channel_id=1, source_target_pairs={{0,128},{16,144},{32,160},{48,176},{64,192},{80,208},{96,224},{112... | collective-permute-start | bytes 786440 | tf_op jit(solution)/shard_map/ppermute | solution.py:113
  27.7 0.6 collective-permute-start.6
  28.3 1.5 %collective-permute-start.7 = (bf16[2,256,512]{2,1,0:T(8,128)(2,1)S(1)}, bf16[2,256,512]{2,1,0:T(8,128)(2,1)S(1)}, u32[]{:S(2)}, u32[]{:S(2)}) collective-permute-start(bf16[2,256,512]{2,1,0:T(8,128)(2,1)S(1)} %get-tuple-element.38), channel_id=1, source_target_pairs={{0,96},{16,112},{32,0},{48,16},{64,32},{80,48},{96,64},{112,80},{1... | collective-permute-start | bytes 1572872 | tf_op jit(solution)/shard_map/ppermute | solution.py:106
  30.1 3.2 %collective-permute-start.13 = (bf16[512,256]{1,0:T(8,128)(2,1)S(1)}, bf16[512,256]{1,0:T(8,128)(2,1)S(1)}, u32[]{:S(2)}, u32[]{:S(2)}) collective-permute-start(bf16[512,256]{1,0:T(8,128)(2,1)S(1)} %collective-permute-done.11), channel_id=1, source_target_pairs={{0,14},{1,15},{2,0},{3,1},{4,2},{5,3},{6,4},{7,5},{8,6},{9,7},{10,... | collective-permute-start | bytes 786440 | tf_op jit(solution)/shard_map/ppermute | solution.py:59
  33.4 4.5 %collective-permute-done.12 = bf16[512,256]{1,0:T(8,128)(2,1)S(1)} collective-permute-done((bf16[512,256]{1,0:T(8,128)(2,1)S(1)}, bf16[512,256]{1,0:T(8,128)(2,1)S(1)}, u32[]{:S(2)}, u32[]{:S(2)}) %collective-permute-start.12) | collective-permute-done | bytes 262176 | tf_op jit(solution)/shard_map/ppermute | solution.py:58
  38.2 2.0 %collective-permute-done.6 = bf16[2,256,512]{2,1,0:T(8,128)(2,1)S(1)} collective-permute-done((bf16[2,256,512]{2,1,0:T(8,128)(2,1)S(1)}, bf16[2,256,512]{2,1,0:T(8,128)(2,1)S(1)}, u32[]{:S(2)}, u32[]{:S(2)}) %collective-permute-start.6) | collective-permute-done | bytes 524320 | tf_op jit(solution)/shard_map/ppermute | solution.py:106
  40.1 1.4 %collective-permute-done.7 = bf16[2,256,512]{2,1,0:T(8,128)(2,1)S(1)} collective-permute-done((bf16[2,256,512]{2,1,0:T(8,128)(2,1)S(1)}, bf16[2,256,512]{2,1,0:T(8,128)(2,1)S(1)}, u32[]{:S(2)}, u32[]{:S(2)}) %collective-permute-start.7) | collective-permute-done | bytes 524320 | tf_op jit(solution)/shard_map/ppermute | solution.py:106
  43.4 2.3 %collective-permute-done.14 = bf16[512,256]{1,0:T(8,128)(2,1)S(1)} collective-permute-done((bf16[512,256]{1,0:T(8,128)(2,1)S(1)}, bf16[512,256]{1,0:T(8,128)(2,1)S(1)}, u32[]{:S(2)}, u32[]{:S(2)}) %collective-permute-start.14) | collective-permute-done | bytes 262176 | tf_op jit(solution)/shard_map/ppermute | solution.py:36
  46.0 0.4 fusion.2
  46.6 0.5 collective-permute-start.24
  47.1 1.4 %collective-permute-done.15 = f32[256,512]{1,0:T(8,128)S(1)} collective-permute-done((f32[256,512]{1,0:T(8,128)S(1)}, f32[256,512]{1,0:T(8,128)S(1)}, u32[]{:S(2)}, u32[]{:S(2)}) %collective-permute-start.15) | collective-permute-done | bytes 524320 | tf_op jit(solution)/shard_map/ppermute | solution.py:137
  48.7 3.2 %collective-permute-start.17 = (bf16[256,256]{1,0:T(8,128)(2,1)S(1)}, bf16[256,256]{1,0:T(8,128)(2,1)S(1)}, u32[]{:S(2)}, u32[]{:S(2)}) collective-permute-start(bf16[256,256]{1,0:T(8,128)(2,1)S(1)} %get-tuple-element.45), channel_id=1, source_target_pairs={{0,128},{16,144},{32,160},{48,176},{64,192},{80,208},{96,224},{112... | collective-permute-start | bytes 393224 | tf_op jit(solution)/shard_map/ppermute | solution.py:152
  52.0 6.0 %collective-permute-start.16 = (bf16[256,256]{1,0:T(8,128)(2,1)S(1)}, bf16[256,256]{1,0:T(8,128)(2,1)S(1)}, u32[]{:S(2)}, u32[]{:S(2)}) collective-permute-start(bf16[256,256]{1,0:T(8,128)(2,1)S(1)} %get-tuple-element.46), channel_id=1, source_target_pairs={{0,0},{1,1},{2,32},{3,33},{4,64},{5,65},{6,96},{7,97},{8,128},{9,1... | collective-permute-start | bytes 393224 | tf_op jit(solution)/shard_map/ppermute | solution.py:36
  58.3 4.9 %collective-permute-done.16 = bf16[256,256]{1,0:T(8,128)(2,1)S(1)} collective-permute-done((bf16[256,256]{1,0:T(8,128)(2,1)S(1)}, bf16[256,256]{1,0:T(8,128)(2,1)S(1)}, u32[]{:S(2)}, u32[]{:S(2)}) %collective-permute-start.16) | collective-permute-done | bytes 131104 | tf_op jit(solution)/shard_map/ppermute | solution.py:36
  63.2 7.2 %collective-permute-done.18 = bf16[256,256]{1,0:T(8,128)(2,1)S(1)} collective-permute-done((bf16[256,256]{1,0:T(8,128)(2,1)S(1)}, bf16[256,256]{1,0:T(8,128)(2,1)S(1)}, u32[]{:S(2)}, u32[]{:S(2)}) %collective-permute-start.18) | collective-permute-done | bytes 131104 | tf_op jit(solution)/shard_map/ppermute | solution.py:36
  70.4 6.8 %collective-permute-start.19 = (bf16[512,256]{1,0:T(8,128)(2,1)S(1)}, bf16[512,256]{1,0:T(8,128)(2,1)S(1)}, u32[]{:S(2)}, u32[]{:S(2)}) collective-permute-start(bf16[512,256]{1,0:T(8,128)(2,1)S(1)} %constant_dynamic-update-slice_fusion), channel_id=1, source_target_pairs={{0,2},{1,3},{2,4},{3,5},{4,6},{5,7},{6,8},{7,9},{8,10},{9,11},{10,... | collective-permute-start | bytes 786440 | tf_op jit(solution)/shard_map/ppermute | solution.py:58
  77.2 5.7 %collective-permute-done.19 = bf16[512,256]{1,0:T(8,128)(2,1)S(1)} collective-permute-done((bf16[512,256]{1,0:T(8,128)(2,1)S(1)}, bf16[512,256]{1,0:T(8,128)(2,1)S(1)}, u32[]{:S(2)}, u32[]{:S(2)}) %collective-permute-start.19) | collective-permute-done | bytes 262176 | tf_op jit(solution)/shard_map/ppermute | solution.py:58
  82.9 2.2 %collective-permute-done.20 = bf16[512,256]{1,0:T(8,128)(2,1)S(1)} collective-permute-done((bf16[512,256]{1,0:T(8,128)(2,1)S(1)}, bf16[512,256]{1,0:T(8,128)(2,1)S(1)}, u32[]{:S(2)}, u32[]{:S(2)}) %collective-permute-start.20) | collective-permute-done | bytes 262176 | tf_op jit(solution)/shard_map/ppermute | solution.py:59
  85.1 0.4 collective-permute-start.21
  85.5 2.9 %collective-permute-start.22 = (bf16[512,256]{1,0:T(8,128)(2,1)S(1)}, bf16[512,256]{1,0:T(8,128)(2,1)S(1)}, u32[]{:S(2)}, u32[]{:S(2)}) collective-permute-start(bf16[512,256]{1,0:T(8,128)(2,1)S(1)} %collective-permute-done.20), channel_id=1, source_target_pairs={{0,14},{1,15},{2,0},{3,1},{4,2},{5,3},{6,4},{7,5},{8,6},{9,7},{10,... | collective-permute-start | bytes 786440 | tf_op jit(solution)/shard_map/ppermute | solution.py:59
  88.4 1.5 %collective-permute-start.23 = (bf16[256,256]{1,0:T(8,128)(2,1)S(1)}, bf16[256,256]{1,0:T(8,128)(2,1)S(1)}, u32[]{:S(2)}, u32[]{:S(2)}) collective-permute-start(bf16[256,256]{1,0:T(8,128)(2,1)S(1)} %get-tuple-element.16), channel_id=1, source_target_pairs={{0,1},{1,0},{2,3},{3,2},{4,5},{5,4},{6,7},{7,6},{8,9},{9,8},{10,11... | collective-permute-start | bytes 393224 | tf_op jit(solution)/shard_map/ppermute | solution.py:57
  89.9 3.5 %collective-permute-done.23 = bf16[256,256]{1,0:T(8,128)(2,1)S(1)} collective-permute-done((bf16[256,256]{1,0:T(8,128)(2,1)S(1)}, bf16[256,256]{1,0:T(8,128)(2,1)S(1)}, u32[]{:S(2)}, u32[]{:S(2)}) %collective-permute-start.23) | collective-permute-done | bytes 131104 | tf_op jit(solution)/shard_map/ppermute | solution.py:57
  93.7 2.9 %collective-permute-start.26 = (bf16[512,256]{1,0:T(8,128)(2,1)S(1)}, bf16[512,256]{1,0:T(8,128)(2,1)S(1)}, u32[]{:S(2)}, u32[]{:S(2)}) collective-permute-start(bf16[512,256]{1,0:T(8,128)(2,1)S(1)} %collective-permute-done.22), channel_id=1, source_target_pairs={{0,14},{1,15},{2,0},{3,1},{4,2},{5,3},{6,4},{7,5},{8,6},{9,7},{10,... | collective-permute-start | bytes 786440 | tf_op jit(solution)/shard_map/ppermute | solution.py:59
  96.6 1.5 %collective-permute-start.27 = (bf16[256,256]{1,0:T(8,128)(2,1)S(1)}, bf16[256,256]{1,0:T(8,128)(2,1)S(1)}, u32[]{:S(2)}, u32[]{:S(2)}) collective-permute-start(bf16[256,256]{1,0:T(8,128)(2,1)S(1)} %select_bitcast_fusion.2), channel_id=1, source_target_pairs={{0,1},{1,0},{2,3},{3,2},{4,5},{5,4},{6,7},{7,6},{8,9},{9,8},{10,11... | collective-permute-start | bytes 393224 | tf_op jit(solution)/shard_map/ppermute | solution.py:57
  98.1 3.5 %collective-permute-done.27 = bf16[256,256]{1,0:T(8,128)(2,1)S(1)} collective-permute-done((bf16[256,256]{1,0:T(8,128)(2,1)S(1)}, bf16[256,256]{1,0:T(8,128)(2,1)S(1)}, u32[]{:S(2)}, u32[]{:S(2)}) %collective-permute-start.27) | collective-permute-done | bytes 131104 | tf_op jit(solution)/shard_map/ppermute | solution.py:57
  101.6 0.5 collective-permute-start.28
  102.6 0.3 fusion.54
  102.9 0.3 fusion.53
  103.9 0.3 fusion.50
  104.6 4.9 %collective-permute-done.28 = bf16[512,256]{1,0:T(8,128)(2,1)S(1)} collective-permute-done((bf16[512,256]{1,0:T(8,128)(2,1)S(1)}, bf16[512,256]{1,0:T(8,128)(2,1)S(1)}, u32[]{:S(2)}, u32[]{:S(2)}) %collective-permute-start.28) | collective-permute-done | bytes 262176 | tf_op jit(solution)/shard_map/ppermute | solution.py:36
  109.8 0.4 fusion.8
  110.3 1.6 %collective-permute-start.29 = (bf16[256,256]{1,0:T(8,128)(2,1)S(1)}, bf16[256,256]{1,0:T(8,128)(2,1)S(1)}, u32[]{:S(2)}, u32[]{:S(2)}) collective-permute-start(bf16[256,256]{1,0:T(8,128)(2,1)S(1)} %subtract_convert_fusion), channel_id=1, source_target_pairs={{0,1},{1,0},{2,3},{3,2},{4,5},{5,4},{6,7},{7,6},{8,9},{9,8},{10,11... | collective-permute-start | bytes 393224 | tf_op jit(solution)/shard_map/ppermute | solution.py:85
  111.9 0.7 maximum_bitcast_fusion
  112.6 2.7 %collective-permute-done.29 = bf16[256,256]{1,0:T(8,128)(2,1)S(1)} collective-permute-done((bf16[256,256]{1,0:T(8,128)(2,1)S(1)}, bf16[256,256]{1,0:T(8,128)(2,1)S(1)}, u32[]{:S(2)}, u32[]{:S(2)}) %collective-permute-start.29) | collective-permute-done | bytes 131104 | tf_op jit(solution)/shard_map/ppermute | solution.py:85
  115.4 0.7 maximum_bitcast_fusion.1
  (65 shorter events, 6.3 us)
Async XLA Ops:
  0.6 14.3 %copy-start = (bf16[2,1,1,256,1,1,256]{6,3,5,4,2,1,0:T(8,128)(2,1)S(1)}, bf16[2,1,1,256,1,1,256]{6,3,5,4,2,1,0:T(8,128)(2,1)}, u32[]{:S(2)}) copy-start(bf16[2,1,1,256,1,1,256]{6,3,5,4,2,1,0:T(8,128)(2,1)} %param.5) | copy-start | bytes 786436
  1.7 7.0 %collective-permute-start.1 = (bf16[256,256]{1,0:T(8,128)(2,1)S(1)}, bf16[256,256]{1,0:T(8,128)(2,1)S(1)}, u32[]{:S(2)}, u32[]{:S(2)}) collective-permute-start(bf16[256,256]{1,0:T(8,128)(2,1)S(1)} %get-tuple-element.52), channel_id=1, source_target_pairs={{0,1},{1,17},{2,3},{3,19},{4,5},{5,21},{6,7},{7,23},{8,9},{9,25},{... | collective-permute-start | bytes 393224 | tf_op jit(solution)/shard_map/ppermute | solution.py:36
  3.4 5.3 %collective-permute-start = (bf16[256,256]{1,0:T(8,128)(2,1)S(1)}, bf16[256,256]{1,0:T(8,128)(2,1)S(1)}, u32[]{:S(2)}, u32[]{:S(2)}) collective-permute-start(bf16[256,256]{1,0:T(8,128)(2,1)S(1)} %get-tuple-element.51), channel_id=1, source_target_pairs={{0,0},{1,16},{2,2},{3,18},{4,4},{5,20},{6,6},{7,22},{8,8},{9,24},{... | collective-permute-start | bytes 393224 | tf_op jit(solution)/shard_map/ppermute | solution.py:36
  5.0 9.9 %collective-permute-start.2 = (bf16[256,256]{1,0:T(8,128)(2,1)S(1)}, bf16[256,256]{1,0:T(8,128)(2,1)S(1)}, u32[]{:S(2)}, u32[]{:S(2)}) collective-permute-start(bf16[256,256]{1,0:T(8,128)(2,1)S(1)} %select_bitcast_fusion.5), channel_id=1, source_target_pairs={{0,1},{1,0},{2,3},{3,2},{4,5},{5,4},{6,7},{7,6},{8,9},{9,8},{10,11... | collective-permute-start | bytes 393224 | tf_op jit(solution)/shard_map/ppermute | solution.py:85
  8.9 12.3 %collective-permute-start.8 = (bf16[512,256]{1,0:T(8,128)(2,1)S(1)}, bf16[512,256]{1,0:T(8,128)(2,1)S(1)}, u32[]{:S(2)}, u32[]{:S(2)}) collective-permute-start(bf16[512,256]{1,0:T(8,128)(2,1)S(1)} %bitcast_select_fusion), channel_id=1, source_target_pairs={{0,2},{1,3},{2,4},{3,5},{4,6},{5,7},{6,8},{7,9},{8,10},{9,11},{10,... | collective-permute-start | bytes 786440 | tf_op jit(solution)/shard_map/ppermute | solution.py:58
  10.9 10.3 %collective-permute-start.9 = (bf16[512,256]{1,0:T(8,128)(2,1)S(1)}, bf16[512,256]{1,0:T(8,128)(2,1)S(1)}, u32[]{:S(2)}, u32[]{:S(2)}) collective-permute-start(bf16[512,256]{1,0:T(8,128)(2,1)S(1)} %bitcast_select_fusion), channel_id=1, source_target_pairs={{0,14},{1,15},{2,0},{3,1},{4,2},{5,3},{6,4},{7,5},{8,6},{9,7},{10,... | collective-permute-start | bytes 786440 | tf_op jit(solution)/shard_map/ppermute | solution.py:59
  15.0 9.4 %collective-permute-start.4 = (bf16[256,512]{1,0:T(8,128)(2,1)S(1)}, bf16[256,512]{1,0:T(8,128)(2,1)S(1)}, u32[]{:S(2)}, u32[]{:S(2)}) collective-permute-start(bf16[256,512]{1,0:T(8,128)(2,1)S(1)} %get-tuple-element.50), channel_id=1, source_target_pairs={{0,64},{16,80},{32,96},{48,112},{64,0},{80,16},{96,32},{112,48},{1... | collective-permute-start | bytes 786440 | tf_op jit(solution)/shard_map/ppermute | solution.py:106
  16.5 11.1 %collective-permute-start.3 = (bf16[256,512]{1,0:T(8,128)(2,1)S(1)}, bf16[256,512]{1,0:T(8,128)(2,1)S(1)}, u32[]{:S(2)}, u32[]{:S(2)}) collective-permute-start(bf16[256,512]{1,0:T(8,128)(2,1)S(1)} %get-tuple-element.50), channel_id=1, source_target_pairs={{0,128},{16,144},{32,160},{48,176},{64,192},{80,208},{96,224},{112... | collective-permute-start | bytes 786440 | tf_op jit(solution)/shard_map/ppermute | solution.py:108
  21.2 8.8 %collective-permute-start.10 = (bf16[512,256]{1,0:T(8,128)(2,1)S(1)}, bf16[512,256]{1,0:T(8,128)(2,1)S(1)}, u32[]{:S(2)}, u32[]{:S(2)}) collective-permute-start(bf16[512,256]{1,0:T(8,128)(2,1)S(1)} %collective-permute-done.8), channel_id=1, source_target_pairs={{0,2},{1,3},{2,4},{3,5},{4,6},{5,7},{6,8},{7,9},{8,10},{9,11},{10,... | collective-permute-start | bytes 786440 | tf_op jit(solution)/shard_map/ppermute | solution.py:58
  21.2 8.9 %collective-permute-start.11 = (bf16[512,256]{1,0:T(8,128)(2,1)S(1)}, bf16[512,256]{1,0:T(8,128)(2,1)S(1)}, u32[]{:S(2)}, u32[]{:S(2)}) collective-permute-start(bf16[512,256]{1,0:T(8,128)(2,1)S(1)} %collective-permute-done.9), channel_id=1, source_target_pairs={{0,14},{1,15},{2,0},{3,1},{4,2},{5,3},{6,4},{7,5},{8,6},{9,7},{10,... | collective-permute-start | bytes 786440 | tf_op jit(solution)/shard_map/ppermute | solution.py:59
  24.4 8.9 %collective-permute-start.5 = (bf16[256,512]{1,0:T(8,128)(2,1)S(1)}, bf16[256,512]{1,0:T(8,128)(2,1)S(1)}, u32[]{:S(2)}, u32[]{:S(2)}) collective-permute-start(bf16[256,512]{1,0:T(8,128)(2,1)S(1)} %collective-permute-done.4), channel_id=1, source_target_pairs={{0,128},{16,144},{32,160},{48,176},{64,192},{80,208},{96,224},{112... | collective-permute-start | bytes 786440 | tf_op jit(solution)/shard_map/ppermute | solution.py:113
  27.7 12.4 %collective-permute-start.6 = (bf16[2,256,512]{2,1,0:T(8,128)(2,1)S(1)}, bf16[2,256,512]{2,1,0:T(8,128)(2,1)S(1)}, u32[]{:S(2)}, u32[]{:S(2)}) collective-permute-start(bf16[2,256,512]{2,1,0:T(8,128)(2,1)S(1)} %get-tuple-element.38), channel_id=1, source_target_pairs={{0,32},{16,48},{32,64},{48,80},{64,96},{80,112},{96,0},{112,16},{1... | collective-permute-start | bytes 1572872 | tf_op jit(solution)/shard_map/ppermute | solution.py:106
  28.3 13.2 %collective-permute-start.7 = (bf16[2,256,512]{2,1,0:T(8,128)(2,1)S(1)}, bf16[2,256,512]{2,1,0:T(8,128)(2,1)S(1)}, u32[]{:S(2)}, u32[]{:S(2)}) collective-permute-start(bf16[2,256,512]{2,1,0:T(8,128)(2,1)S(1)} %get-tuple-element.38), channel_id=1, source_target_pairs={{0,96},{16,112},{32,0},{48,16},{64,32},{80,48},{96,64},{112,80},{1... | collective-permute-start | bytes 1572872 | tf_op jit(solution)/shard_map/ppermute | solution.py:106
  30.0 7.8 %collective-permute-start.12 = (bf16[512,256]{1,0:T(8,128)(2,1)S(1)}, bf16[512,256]{1,0:T(8,128)(2,1)S(1)}, u32[]{:S(2)}, u32[]{:S(2)}) collective-permute-start(bf16[512,256]{1,0:T(8,128)(2,1)S(1)} %collective-permute-done.10), channel_id=1, source_target_pairs={{0,2},{1,3},{2,4},{3,5},{4,6},{5,7},{6,8},{7,9},{8,10},{9,11},{10,... | collective-permute-start | bytes 786440 | tf_op jit(solution)/shard_map/ppermute | solution.py:58
  30.1 7.7 %collective-permute-start.13 = (bf16[512,256]{1,0:T(8,128)(2,1)S(1)}, bf16[512,256]{1,0:T(8,128)(2,1)S(1)}, u32[]{:S(2)}, u32[]{:S(2)}) collective-permute-start(bf16[512,256]{1,0:T(8,128)(2,1)S(1)} %collective-permute-done.11), channel_id=1, source_target_pairs={{0,14},{1,15},{2,0},{3,1},{4,2},{5,3},{6,4},{7,5},{8,6},{9,7},{10,... | collective-permute-start | bytes 786440 | tf_op jit(solution)/shard_map/ppermute | solution.py:59
  37.9 7.8 %collective-permute-start.14 = (bf16[512,256]{1,0:T(8,128)(2,1)S(1)}, bf16[512,256]{1,0:T(8,128)(2,1)S(1)}, u32[]{:S(2)}, u32[]{:S(2)}) collective-permute-start(bf16[512,256]{1,0:T(8,128)(2,1)S(1)} %broadcast_select_fusion.2), channel_id=1, source_target_pairs={{0,2},{1,3},{2,4},{3,5},{4,6},{5,7},{6,8},{7,9},{8,10},{9,11},{10,... | collective-permute-start | bytes 786440 | tf_op jit(solution)/shard_map/ppermute | solution.py:36
  46.4 43.5 %copy-start.1 = (bf16[2,1,1,256,1,1,256]{6,3,5,4,2,1,0:T(8,128)(2,1)S(1)}, bf16[2,1,1,256,1,1,256]{6,3,5,4,2,1,0:T(8,128)(2,1)}, u32[]{:S(2)}) copy-start(bf16[2,1,1,256,1,1,256]{6,3,5,4,2,1,0:T(8,128)(2,1)} %param.6) | copy-start | bytes 786436
  46.5 2.0 %collective-permute-start.15 = (f32[256,512]{1,0:T(8,128)S(1)}, f32[256,512]{1,0:T(8,128)S(1)}, u32[]{:S(2)}, u32[]{:S(2)}) collective-permute-start(f32[256,512]{1,0:T(8,128)S(1)} %slice_select_fusion), channel_id=1, source_target_pairs={{0,16},{16,0},{32,48},{48,32},{64,80},{80,64},{96,112},{112,96},{1... | collective-permute-start | bytes 1572872 | tf_op jit(solution)/shard_map/ppermute | solution.py:137
  46.6 55.6 %collective-permute-start.24 = (bf16[4,2,256,512]{3,2,1,0:T(8,128)(2,1)S(1)}, bf16[4,2,256,512]{3,2,1,0:T(8,128)(2,1)S(1)}, u32[]{:S(2)}, u32[]{:S(2)}) collective-permute-start(bf16[4,2,256,512]{3,2,1,0:T(8,128)(2,1)S(1)} %bitcast_dynamic-update-slice_fusion), channel_id=1, source_target_pairs={{0,16},{16,0},{32,48},{48,32},{64,80},{80,64},{96,112},{112,96},{1... | collective-permute-start | bytes 6291464 | tf_op jit(solution)/shard_map/ppermute | solution.py:142
  48.7 9.2 %collective-permute-start.17 = (bf16[256,256]{1,0:T(8,128)(2,1)S(1)}, bf16[256,256]{1,0:T(8,128)(2,1)S(1)}, u32[]{:S(2)}, u32[]{:S(2)}) collective-permute-start(bf16[256,256]{1,0:T(8,128)(2,1)S(1)} %get-tuple-element.45), channel_id=1, source_target_pairs={{0,128},{16,144},{32,160},{48,176},{64,192},{80,208},{96,224},{112... | collective-permute-start | bytes 393224 | tf_op jit(solution)/shard_map/ppermute | solution.py:152
  52.0 11.3 %collective-permute-start.16 = (bf16[256,256]{1,0:T(8,128)(2,1)S(1)}, bf16[256,256]{1,0:T(8,128)(2,1)S(1)}, u32[]{:S(2)}, u32[]{:S(2)}) collective-permute-start(bf16[256,256]{1,0:T(8,128)(2,1)S(1)} %get-tuple-element.46), channel_id=1, source_target_pairs={{0,0},{1,1},{2,32},{3,33},{4,64},{5,65},{6,96},{7,97},{8,128},{9,1... | collective-permute-start | bytes 393224 | tf_op jit(solution)/shard_map/ppermute | solution.py:36
  58.0 12.4 %collective-permute-start.18 = (bf16[256,256]{1,0:T(8,128)(2,1)S(1)}, bf16[256,256]{1,0:T(8,128)(2,1)S(1)}, u32[]{:S(2)}, u32[]{:S(2)}) collective-permute-start(bf16[256,256]{1,0:T(8,128)(2,1)S(1)} %collective-permute-done.17), channel_id=1, source_target_pairs={{0,24},{1,25},{2,56},{3,57},{4,88},{5,89},{6,120},{7,121},{8,152},... | collective-permute-start | bytes 393224 | tf_op jit(solution)/shard_map/ppermute | solution.py:36
  70.4 12.5 %collective-permute-start.19 = (bf16[512,256]{1,0:T(8,128)(2,1)S(1)}, bf16[512,256]{1,0:T(8,128)(2,1)S(1)}, u32[]{:S(2)}, u32[]{:S(2)}) collective-permute-start(bf16[512,256]{1,0:T(8,128)(2,1)S(1)} %constant_dynamic-update-slice_fusion), channel_id=1, source_target_pairs={{0,2},{1,3},{2,4},{3,5},{4,6},{5,7},{6,8},{7,9},{8,10},{9,11},{10,... | collective-permute-start | bytes 786440 | tf_op jit(solution)/shard_map/ppermute | solution.py:58
  77.2 7.9 %collective-permute-start.20 = (bf16[512,256]{1,0:T(8,128)(2,1)S(1)}, bf16[512,256]{1,0:T(8,128)(2,1)S(1)}, u32[]{:S(2)}, u32[]{:S(2)}) collective-permute-start(bf16[512,256]{1,0:T(8,128)(2,1)S(1)} %constant_dynamic-update-slice_fusion), channel_id=1, source_target_pairs={{0,14},{1,15},{2,0},{3,1},{4,2},{5,3},{6,4},{7,5},{8,6},{9,7},{10,... | collective-permute-start | bytes 786440 | tf_op jit(solution)/shard_map/ppermute | solution.py:59
  85.1 8.2 %collective-permute-start.21 = (bf16[512,256]{1,0:T(8,128)(2,1)S(1)}, bf16[512,256]{1,0:T(8,128)(2,1)S(1)}, u32[]{:S(2)}, u32[]{:S(2)}) collective-permute-start(bf16[512,256]{1,0:T(8,128)(2,1)S(1)} %collective-permute-done.19), channel_id=1, source_target_pairs={{0,2},{1,3},{2,4},{3,5},{4,6},{5,7},{6,8},{7,9},{8,10},{9,11},{10,... | collective-permute-start | bytes 786440 | tf_op jit(solution)/shard_map/ppermute | solution.py:58
  85.5 7.9 %collective-permute-start.22 = (bf16[512,256]{1,0:T(8,128)(2,1)S(1)}, bf16[512,256]{1,0:T(8,128)(2,1)S(1)}, u32[]{:S(2)}, u32[]{:S(2)}) collective-permute-start(bf16[512,256]{1,0:T(8,128)(2,1)S(1)} %collective-permute-done.20), channel_id=1, source_target_pairs={{0,14},{1,15},{2,0},{3,1},{4,2},{5,3},{6,4},{7,5},{8,6},{9,7},{10,... | collective-permute-start | bytes 786440 | tf_op jit(solution)/shard_map/ppermute | solution.py:59
  88.4 5.0 %collective-permute-start.23 = (bf16[256,256]{1,0:T(8,128)(2,1)S(1)}, bf16[256,256]{1,0:T(8,128)(2,1)S(1)}, u32[]{:S(2)}, u32[]{:S(2)}) collective-permute-start(bf16[256,256]{1,0:T(8,128)(2,1)S(1)} %get-tuple-element.16), channel_id=1, source_target_pairs={{0,1},{1,0},{2,3},{3,2},{4,5},{5,4},{6,7},{7,6},{8,9},{9,8},{10,11... | collective-permute-start | bytes 393224 | tf_op jit(solution)/shard_map/ppermute | solution.py:57
  93.4 8.2 %collective-permute-start.25 = (bf16[512,256]{1,0:T(8,128)(2,1)S(1)}, bf16[512,256]{1,0:T(8,128)(2,1)S(1)}, u32[]{:S(2)}, u32[]{:S(2)}) collective-permute-start(bf16[512,256]{1,0:T(8,128)(2,1)S(1)} %collective-permute-done.21), channel_id=1, source_target_pairs={{0,2},{1,3},{2,4},{3,5},{4,6},{5,7},{6,8},{7,9},{8,10},{9,11},{10,... | collective-permute-start | bytes 786440 | tf_op jit(solution)/shard_map/ppermute | solution.py:58
  93.7 7.9 %collective-permute-start.26 = (bf16[512,256]{1,0:T(8,128)(2,1)S(1)}, bf16[512,256]{1,0:T(8,128)(2,1)S(1)}, u32[]{:S(2)}, u32[]{:S(2)}) collective-permute-start(bf16[512,256]{1,0:T(8,128)(2,1)S(1)} %collective-permute-done.22), channel_id=1, source_target_pairs={{0,14},{1,15},{2,0},{3,1},{4,2},{5,3},{6,4},{7,5},{8,6},{9,7},{10,... | collective-permute-start | bytes 786440 | tf_op jit(solution)/shard_map/ppermute | solution.py:59
  96.6 5.0 %collective-permute-start.27 = (bf16[256,256]{1,0:T(8,128)(2,1)S(1)}, bf16[256,256]{1,0:T(8,128)(2,1)S(1)}, u32[]{:S(2)}, u32[]{:S(2)}) collective-permute-start(bf16[256,256]{1,0:T(8,128)(2,1)S(1)} %select_bitcast_fusion.2), channel_id=1, source_target_pairs={{0,1},{1,0},{2,3},{3,2},{4,5},{5,4},{6,7},{7,6},{8,9},{9,8},{10,11... | collective-permute-start | bytes 393224 | tf_op jit(solution)/shard_map/ppermute | solution.py:57
  101.6 7.9 %collective-permute-start.28 = (bf16[512,256]{1,0:T(8,128)(2,1)S(1)}, bf16[512,256]{1,0:T(8,128)(2,1)S(1)}, u32[]{:S(2)}, u32[]{:S(2)}) collective-permute-start(bf16[512,256]{1,0:T(8,128)(2,1)S(1)} %broadcast_select_fusion.1), channel_id=1, source_target_pairs={{0,2},{1,3},{2,4},{3,5},{4,6},{5,7},{6,8},{7,9},{8,10},{9,11},{10,... | collective-permute-start | bytes 786440 | tf_op jit(solution)/shard_map/ppermute | solution.py:36
  110.3 5.1 %collective-permute-start.29 = (bf16[256,256]{1,0:T(8,128)(2,1)S(1)}, bf16[256,256]{1,0:T(8,128)(2,1)S(1)}, u32[]{:S(2)}, u32[]{:S(2)}) collective-permute-start(bf16[256,256]{1,0:T(8,128)(2,1)S(1)} %subtract_convert_fusion), channel_id=1, source_target_pairs={{0,1},{1,0},{2,3},{3,2},{4,5},{5,4},{6,7},{7,6},{8,9},{9,8},{10,11... | collective-permute-start | bytes 393224 | tf_op jit(solution)/shard_map/ppermute | solution.py:85

commit v3 on v2

v3 whole, which is shorter than its diff:
```python
import jax
import jax.numpy as jnp
from jax import lax
from jax.sharding import PartitionSpec as P

NX = 4
NZ = 8


def row_perm(fn):
    pairs = []
    for i in range(16):
        yh, x, c = fn(i // 8, (i // 2) % NX, i % 2)
        pairs.append((i, yh * 8 + (x % NX) * 2 + c))
    return pairs


def col_perm(fn):
    pairs = []
    for i in range(16):
        z, yl = fn(i // 2, i % 2)
        pairs.append((i, (z % NZ) * 2 + yl))
    return pairs


def both_perm(fn):
    pairs = []
    for p in range(16):
        for q in range(16):
            chip, c, z, yl = fn(p // 2, p % 2, q // 2, q % 2)
            pairs.append((p * 16 + q, (chip * 2 + c) * 16 + (z % NZ) * 2 + yl))
    return pairs


def move(block, pairs):
    return lax.ppermute(block, ("prow", "pcol"), pairs)


SWAP = col_perm(lambda z, yl: (z, 1 - yl))
UP = col_perm(lambda z, yl: (z + 1, yl))
DOWN = col_perm(lambda z, yl: (z - 1, yl))
OPPOSITE = col_perm(lambda z, yl: (z + NZ // 2, yl))
CROSS = row_perm(lambda h, x, c: (h, x, 1 - c))
FLIP_H = row_perm(lambda h, x, c: (1 - h, x, c))
SPLIT = both_perm(lambda chip, c, z, yl: (chip, c, z + 1 - 2 * c, yl))


def up(block):
    return lax.ppermute(block, "pcol", UP)


def down(block):
    return lax.ppermute(block, "pcol", DOWN)


def tie(*values):
    return lax.optimization_barrier(values)


def z_ring(piece, core, add, total, beside=()):
    swapped = []
    ahead = behind = piece
    found = [(0, piece)]
    for step in range(1, NZ // 2):
        near = found
        if 2 <= step < 2 + len(beside):
            ahead, behind, hold = tie(ahead, behind, beside[step - 2])
            swapped.append(lax.ppermute(hold, "pcol", SWAP))
        ahead, behind = up(ahead), down(behind)
        found = [(-step, ahead), (step, behind)]
        for offset, block in near:
            total = add(total, offset, block)
        if beside:
            ahead, behind, total = tie(ahead, behind, total)
        if 2 <= step < 2 + len(beside):
            ahead, behind, swapped[-1] = tie(ahead, behind, swapped[-1])
    last = move(jnp.where(core == 0, ahead, behind), SPLIT)
    for offset, block in found:
        total = add(total, offset, block)
    return add(total, NZ // 2, last), swapped


def on_device(anc_inverse, factor_panel, diag_inverse, block_pattern):
    p = lax.axis_index("prow")
    q = lax.axis_index("pcol")
    yh, x, c = p // 8, (p // 2) % NX, p % 2
    z, yl = q // 2, q % 2
    anc = anc_inverse.reshape(2, 256, 256)
    panel = factor_panel.reshape(2, 256, 256)
    diag = diag_inverse.reshape(2, 256, 256)

    def mine(pair):
        return jnp.where(yl == 0, pair[0], pair[1])

    def other(pair):
        return jnp.where(yl == 0, pair[1], pair[0])

    def swap(block):
        return lax.ppermute(block, "pcol", SWAP)

    near = move(
        jnp.where(c == 0, anc[0], anc[1]),
        both_perm(lambda chip, c, z, yl: (chip, yl, z, c)),
    )
    far = move(
        jnp.where(c == 0, anc[1], anc[0]),
        both_perm(lambda chip, c, z, yl: (chip, yl, z, 1 - c)),
    )
    oth_u, near = tie(other(panel), near)
    own_u, got_u = mine(panel), swap(oth_u)
    same = yl == c
    keep = lax.dynamic_slice(block_pattern, (yl, p - c, 2 * z + c), (1, 2, 1))
    keep = jnp.where(c == 0, keep, keep[:, ::-1]).reshape(2, 1, 1) != 0
    m_piece = jnp.where(same, jnp.stack([near, far]), jnp.stack([far, near]))
    m_piece = jnp.where(keep, m_piece, jnp.zeros_like(m_piece)).reshape(512, 256)

    u_piece = jnp.concatenate(
        [jnp.where(same, own_u, got_u), jnp.where(same, got_u, own_u)], axis=1
    )

    def along_x(block, step):
        return lax.ppermute(block, "prow", row_perm(lambda h, x, c: (h, x + step, c)))

    u_far = lax.ppermute(u_piece, "prow", FLIP_H)
    u_two = along_x(u_piece, 2)
    both = jnp.stack([u_piece, u_far])
    u_one = along_x(both, 1)
    u_three = along_x(both, 3)
    u_two_far = lax.ppermute(u_two, "prow", FLIP_H)
    u_all = jnp.zeros((NX, 2, 256, 512), jnp.bfloat16)
    for back, away, block in (
        (0, 0, both),
        (2, 0, u_two[None]),
        (2, 1, u_two_far[None]),
        (1, 0, u_one),
        (3, 0, u_three),
    ):
        u_all = lax.dynamic_update_slice(u_all, block[None], (back, away, 0, 0))

    def find(owner):
        owner = (owner + NZ) % NZ
        back = (x - owner % NX + NX) % NX
        return back, jnp.where(owner // NX == yh, 0, 1)

    def u_rows(panel, owner):
        at = (*find(owner), 0, 0)
        return lax.dynamic_slice(panel, at, (1, 1, 256, 512)).reshape(256, 512)

    def add_product(total, offset, block):
        rows = u_rows(u_all, z + offset)
        return tuple(
            part + jnp.dot(block, cols, preferred_element_type=jnp.float32)
            for part, cols in zip(total, (rows[:, :256], rows[:, 256:]))
        )

    zero = jnp.zeros((512, 256), jnp.float32)
    (kept, sent), _ = z_ring(m_piece, c, add_product, (zero, zero))
    theirs = lax.ppermute(sent, "prow", CROSS)
    off = kept + jnp.concatenate([theirs[256:], theirs[:256]], axis=0)
    off = (-off).astype(jnp.bfloat16)

    o_piece = move(off, both_perm(lambda chip, c, z, yl: (z, c, chip - z, yl)))
    u_cross = lax.ppermute(u_all, "prow", CROSS)
    o_piece, u_cross = tie(o_piece, u_cross)
    first, second = off[:256], lax.ppermute(off[256:], "prow", CROSS)
    off_mine = jnp.where(same, first, second)

    def add_inner(total, offset, block):
        return tuple(
            part
            + lax.dot_general(
                u_rows(panel, p // 2 + z + offset),
                rows,
                (((0,), (0,)), ((), ())),
                preferred_element_type=jnp.float32,
            )
            for part, panel, rows in zip(
                total, (u_all, u_cross), (block[:256], block[256:])
            )
        )

    total, (off_got, d_got) = z_ring(
        o_piece, c, add_inner, (zero, zero), (jnp.where(same, second, first), other(diag))
    )
    first = total[0][:256] + total[1][256:]
    second = total[0][256:] + total[1][:256]
    d_mine = mine(diag)
    diag_mine = (
        d_mine.astype(jnp.float32) - jnp.where(same, first, second)
    ).astype(jnp.bfloat16)
    diag_got = swap(
        (d_got.astype(jnp.float32) - jnp.where(same, second, first)).astype(
            jnp.bfloat16
        )
    )

    def place(own, got):
        return jnp.stack(
            [jnp.where(yl == 0, own, got), jnp.where(yl == 0, got, own)]
        ).reshape(anc_inverse.shape)

    return place(off_mine, off_got), place(diag_mine, diag_got)


def solution(mesh):
    return jax.shard_map(
        on_device,
        mesh=mesh,
        in_specs=(
            P(None, None, "prow", None, None, "pcol", None),
            P(None, None, "prow", None, None, "pcol", None),
            P(None, None, "pcol", None, None, "prow", None),
            P(),
        ),
        out_specs=(
            P(None, None, "prow", None, None, "pcol", None),
            P(None, None, "pcol", None, None, "prow", None),
        ),
        check_vma=False,
    )
```

time: 116 us -> 113 us (0.974); the launches traced: 116 us -> 111 us
  waiting for transfers between devices: 47.6 us -> 35.6 us
  matrix products: 5.21 us -> 15.6 us
  starting transfers between devices: 55.5 us -> 51.2 us
  local copies, waits for them, and re-layouts: 1.2 us -> 2.36 us
    dot_general x16 -> x32, matrix products: 5.21 us -> 15.6 us  [the longest x16 11.9 us: add_inner(): lax.dot_general(u_rows(panel, p // 2 + z + offset), rows, (((0,), (0,)),...]
    ppermute x6 -> x5, waiting for transfers between devices: 19.3 us -> 11 us  [move(): return lax.ppermute(block, ('prow', 'pcol'), pairs)]
    ppermute x2, waiting for transfers between devices: 6.96 us -> 0.55 us  [z_ring(): swapped.append(lax.ppermute(hold, 'pcol', SWAP))]
    ppermute x15, waiting for transfers between devices: 15.3 us -> 19.6 us  [the longest x6 12.9 us: up(): return lax.ppermute(block, 'pcol', UP)]
    ppermute x3, waiting for transfers between devices: 3.33 us -> 0.31 us  [along_x(): lax.ppermute(block, 'prow', row_perm(lambda h, x, c: (h, x + step, c)))]
    ppermute x2, starting transfers between devices: 2.95 us -> 0.22 us  [z_ring(): swapped.append(lax.ppermute(hold, 'pcol', SWAP))]
    ppermute x15, starting transfers between devices: 29.7 us -> 27.2 us  [the longest x6 17.3 us: down(): return lax.ppermute(block, 'pcol', DOWN)]
    ppermute x6 -> x5, starting transfers between devices: 9.44 us -> 10.9 us  [move(): return lax.ppermute(block, ('prow', 'pcol'), pairs)]
  transfers between devices with their start and end apart: 30 -> 29, of which waited for: 14 -> 16; matrix products, arithmetic and copies ran while one was open for 7% -> 17% of each run, Pallas kernels for 0% -> 0%
where the time goes in v3:
time: 113 us; the launch traced here: 111 us
  starting transfers between devices  51.2 us (45%)
  waiting for transfers between devices  35.6 us (32%)
  matrix products  15.6 us (14%)
  other arithmetic  4.96 us (4%)
  local copies, waits for them, and re-layouts  2.36 us (2%)
  between operations  1.75 us (2%)
    ppermute x6, starting transfers between devices, down(): return lax.ppermute(block, 'pcol', DOWN)  17.3 us
    ppermute x6, waiting for transfers between devices, up(): return lax.ppermute(block, 'pcol', UP)  12.9 us
    dot_general x16, matrix products, add_inner(): lax.dot_general(u_rows(panel, p // 2 + z + offset), rows, (((0,), (0,)),...  11.9 us
    ppermute x5, waiting for transfers between devices, move(): return lax.ppermute(block, ('prow', 'pcol'), pairs)  11 us
    ppermute x5, starting transfers between devices, move(): return lax.ppermute(block, ('prow', 'pcol'), pairs)  10.9 us
    ppermute x6, starting transfers between devices, up(): return lax.ppermute(block, 'pcol', UP)  9.27 us
    ppermute x6, waiting for transfers between devices, down(): return lax.ppermute(block, 'pcol', DOWN)  4.89 us
    ppermute x2, waiting for transfers between devices, swap(): return lax.ppermute(block, 'pcol', SWAP)  4.03 us
  transfers between devices with their start and end apart: 29, of which 16 were waited for; matrix products, arithmetic and copies ran while one was open for 17% of the time, Pallas kernels for 0%

profile of v3, /device:TPU:6, one launch (start us, length us, event | category | flops | bytes accessed | tf_op | source)
XLA Modules:
  0.0 111.4 jit_solution(14817080369592206580)
XLA Ops:
  0.7 1.0 select_bitcast_fusion.6
  1.7 1.7 %collective-permute-start.1 = (bf16[256,256]{1,0:T(8,128)(2,1)S(1)}, bf16[256,256]{1,0:T(8,128)(2,1)S(1)}, u32[]{:S(2)}, u32[]{:S(2)}) collective-permute-start(bf16[256,256]{1,0:T(8,128)(2,1)S(1)} %get-tuple-element.81), channel_id=1, source_target_pairs={{0,1},{1,17},{2,3},{3,19},{4,5},{5,21},{6,7},{7,23},{8,9},{9,25},{... | collective-permute-start | bytes 393224 | tf_op jit(solution)/shard_map/ppermute | solution.py:36
  3.4 0.7 collective-permute-start
  4.1 0.8 dynamic_slice.75
  4.9 0.9 compare_reduce_fusion
  5.9 1.0 select_bitcast_fusion.7
  6.9 2.9 %collective-permute-start.2 = (bf16[256,256]{1,0:T(8,128)(2,1)S(1)}, bf16[256,256]{1,0:T(8,128)(2,1)S(1)}, u32[]{:S(2)}, u32[]{:S(2)}) collective-permute-start(bf16[256,256]{1,0:T(8,128)(2,1)S(1)} %select_bitcast_fusion.7), channel_id=1, source_target_pairs={{0,1},{1,0},{2,3},{3,2},{4,5},{5,4},{6,7},{7,6},{8,9},{9,8},{10,11... | collective-permute-start | bytes 393224 | tf_op jit(solution)/shard_map/ppermute | solution.py:99
  9.9 2.0 %collective-permute-start.8 = (bf16[512,256]{1,0:T(8,128)(2,1)S(1)}, bf16[512,256]{1,0:T(8,128)(2,1)S(1)}, u32[]{:S(2)}, u32[]{:S(2)}) collective-permute-start(bf16[512,256]{1,0:T(8,128)(2,1)S(1)} %bitcast_select_fusion), channel_id=1, source_target_pairs={{0,2},{1,3},{2,4},{3,5},{4,6},{5,7},{6,8},{7,9},{8,10},{9,11},{10,... | collective-permute-start | bytes 786440 | tf_op jit(solution)/shard_map/ppermute | solution.py:49
  11.9 4.0 %collective-permute-start.9 = (bf16[512,256]{1,0:T(8,128)(2,1)S(1)}, bf16[512,256]{1,0:T(8,128)(2,1)S(1)}, u32[]{:S(2)}, u32[]{:S(2)}) collective-permute-start(bf16[512,256]{1,0:T(8,128)(2,1)S(1)} %bitcast_select_fusion), channel_id=1, source_target_pairs={{0,14},{1,15},{2,0},{3,1},{4,2},{5,3},{6,4},{7,5},{8,6},{9,7},{10,... | collective-permute-start | bytes 786440 | tf_op jit(solution)/shard_map/ppermute | solution.py:53
  16.0 1.5 %collective-permute-start.4 = (bf16[256,512]{1,0:T(8,128)(2,1)S(1)}, bf16[256,512]{1,0:T(8,128)(2,1)}, u32[]{:S(2)}, u32[]{:S(2)}) collective-permute-start(bf16[256,512]{1,0:T(8,128)(2,1)S(1)} %get-tuple-element.79), channel_id=1, source_target_pairs={{0,64},{16,80},{32,96},{48,112},{64,0},{80,16},{96,32},{112,48},{1... | collective-permute-start | bytes 786440 | tf_op jit(solution)/shard_map/ppermute | solution.py:122
  17.5 2.9 %collective-permute-start.3 = (bf16[256,512]{1,0:T(8,128)(2,1)S(1)}, bf16[256,512]{1,0:T(8,128)(2,1)S(1)}, u32[]{:S(2)}, u32[]{:S(2)}) collective-permute-start(bf16[256,512]{1,0:T(8,128)(2,1)S(1)} %get-tuple-element.79), channel_id=1, source_target_pairs={{0,128},{16,144},{32,160},{48,176},{64,192},{80,208},{96,224},{112... | collective-permute-start | bytes 786440 | tf_op jit(solution)/shard_map/ppermute | solution.py:124
  20.4 0.7 collective-permute-done.8
  21.2 3.2 %collective-permute-start.11 = (bf16[512,256]{1,0:T(8,128)(2,1)S(1)}, bf16[512,256]{1,0:T(8,128)(2,1)S(1)}, u32[]{:S(2)}, u32[]{:S(2)}) collective-permute-start(bf16[512,256]{1,0:T(8,128)(2,1)S(1)} %collective-permute-done.9), channel_id=1, source_target_pairs={{0,14},{1,15},{2,0},{3,1},{4,2},{5,3},{6,4},{7,5},{8,6},{9,7},{10,... | collective-permute-start | bytes 786440 | tf_op jit(solution)/shard_map/ppermute | solution.py:53
  24.5 3.2 %collective-permute-start.5 = (bf16[256,512]{1,0:T(8,128)(2,1)}, bf16[256,512]{1,0:T(8,128)(2,1)S(1)}, u32[]{:S(2)}, u32[]{:S(2)}) collective-permute-start(bf16[256,512]{1,0:T(8,128)(2,1)} %collective-permute-done.4), channel_id=1, source_target_pairs={{0,128},{16,144},{32,160},{48,176},{64,192},{80,208},{96,224},{112... | collective-permute-start | bytes 786440 | tf_op jit(solution)/shard_map/ppermute | solution.py:129
  27.7 0.6 collective-permute-start.6
  28.3 1.5 %collective-permute-start.7 = (bf16[2,256,512]{2,1,0:T(8,128)(2,1)S(1)}, bf16[2,256,512]{2,1,0:T(8,128)(2,1)S(1)}, u32[]{:S(2)}, u32[]{:S(2)}) collective-permute-start(bf16[2,256,512]{2,1,0:T(8,128)(2,1)S(1)} %get-tuple-element.74), channel_id=1, source_target_pairs={{0,96},{16,112},{32,0},{48,16},{64,32},{80,48},{96,64},{112,80},{1... | collective-permute-start | bytes 1572872 | tf_op jit(solution)/shard_map/ppermute | solution.py:122
  30.4 1.0 collective-permute-start.12
  31.4 4.0 %collective-permute-start.13 = (bf16[512,256]{1,0:T(8,128)(2,1)S(1)}, bf16[512,256]{1,0:T(8,128)(2,1)S(1)}, u32[]{:S(2)}, u32[]{:S(2)}) collective-permute-start(bf16[512,256]{1,0:T(8,128)(2,1)S(1)} %collective-permute-done.11), channel_id=1, source_target_pairs={{0,14},{1,15},{2,0},{3,1},{4,2},{5,3},{6,4},{7,5},{8,6},{9,7},{10,... | collective-permute-start | bytes 786440 | tf_op jit(solution)/shard_map/ppermute | solution.py:53
  35.5 1.0 bitcast_dynamic-update-slice_fusion.3
  36.5 4.0 %collective-permute-done.12 = bf16[512,256]{1,0:T(8,128)(2,1)S(1)} collective-permute-done((bf16[512,256]{1,0:T(8,128)(2,1)S(1)}, bf16[512,256]{1,0:T(8,128)(2,1)S(1)}, u32[]{:S(2)}, u32[]{:S(2)}) %collective-permute-start.12) | collective-permute-done | bytes 262176 | tf_op jit(solution)/shard_map/ppermute | solution.py:49
  44.0 4.2 %collective-permute-done.14 = bf16[512,256]{1,0:T(8,128)(2,1)S(1)} collective-permute-done((bf16[512,256]{1,0:T(8,128)(2,1)S(1)}, bf16[512,256]{1,0:T(8,128)(2,1)S(1)}, u32[]{:S(2)}, u32[]{:S(2)}) %collective-permute-start.14) | collective-permute-done | bytes 262176 | tf_op jit(solution)/shard_map/ppermute | solution.py:36
  49.5 1.2 %collective-permute-done.15 = f32[512,256]{1,0:T(8,128)S(1)} collective-permute-done((f32[512,256]{1,0:T(8,128)S(1)}, f32[512,256]{1,0:T(8,128)S(1)}, u32[]{:S(2)}, u32[]{:S(2)}) %collective-permute-start.15) | collective-permute-done | bytes 524320 | tf_op jit(solution)/shard_map/ppermute | solution.py:158
  51.0 6.0 %collective-permute-start.17 = (bf16[512,256]{1,0:T(8,128)(2,1)S(1)}, bf16[512,256]{1,0:T(8,128)(2,1)S(1)}, u32[]{:S(2)}, u32[]{:S(2)}) collective-permute-start(bf16[512,256]{1,0:T(8,128)(2,1)S(1)} %fusion.8), channel_id=1, source_target_pairs={{0,0},{1,1},{2,46},{3,47},{4,76},{5,77},{6,106},{7,107},{8,136},{9... | collective-permute-start | bytes 786440 | tf_op jit(solution)/shard_map/ppermute | solution.py:36
  57.7 0.7 collective-permute-done.16
  58.5 4.6 %collective-permute-done.17 = bf16[512,256]{1,0:T(8,128)(2,1)S(1)} collective-permute-done((bf16[512,256]{1,0:T(8,128)(2,1)S(1)}, bf16[512,256]{1,0:T(8,128)(2,1)S(1)}, u32[]{:S(2)}, u32[]{:S(2)}) %collective-permute-start.17) | collective-permute-done | bytes 262176 | tf_op jit(solution)/shard_map/ppermute | solution.py:36
  63.1 3.7 %collective-permute-start.19 = (bf16[512,256]{1,0:T(8,128)(2,1)S(1)}, bf16[512,256]{1,0:T(8,128)(2,1)S(1)}, u32[]{:S(2)}, u32[]{:S(2)}) collective-permute-start(bf16[512,256]{1,0:T(8,128)(2,1)S(1)} %collective-permute-done.17), channel_id=1, source_target_pairs={{0,2},{1,3},{2,4},{3,5},{4,6},{5,7},{6,8},{7,9},{8,10},{9,11},{10,... | collective-permute-start | bytes 786440 | tf_op jit(solution)/shard_map/ppermute | solution.py:49
  66.8 2.1 %collective-permute-start.20 = (bf16[512,256]{1,0:T(8,128)(2,1)S(1)}, bf16[512,256]{1,0:T(8,128)(2,1)S(1)}, u32[]{:S(2)}, u32[]{:S(2)}) collective-permute-start(bf16[512,256]{1,0:T(8,128)(2,1)S(1)} %collective-permute-done.17), channel_id=1, source_target_pairs={{0,14},{1,15},{2,0},{3,1},{4,2},{5,3},{6,4},{7,5},{8,6},{9,7},{10,... | collective-permute-start | bytes 786440 | tf_op jit(solution)/shard_map/ppermute | solution.py:53
  69.1 1.2 %fusion.50 = f32[512,256]{1,0:T(8,128)S(1)} fusion(bf16[4,2,256,512]{3,2,1,0:T(8,128)(2,1)} %collective-permute-done.18, s32[]{:T(128)S(6)} %select_n.695, s32[]{:T(128)S(6)} %select_n.697, bf16[512,256]{1,0:T(8,128)(2,1)S(1)} %collective-permute-done.17), kind=kOutput, calls=%fused_computation.62 | convolution fusion | flops 67108864 | bytes 917512 | tf_op jit(solution)/shard_map/dot_general | solution.py:171
  70.4 4.2 %collective-permute-done.19 = bf16[512,256]{1,0:T(8,128)(2,1)S(1)} collective-permute-done((bf16[512,256]{1,0:T(8,128)(2,1)S(1)}, bf16[512,256]{1,0:T(8,128)(2,1)S(1)}, u32[]{:S(2)}, u32[]{:S(2)}) %collective-permute-start.19) | collective-permute-done | bytes 262176 | tf_op jit(solution)/shard_map/ppermute | solution.py:49
  74.6 4.9 %collective-permute-done.20 = bf16[512,256]{1,0:T(8,128)(2,1)S(1)} collective-permute-done((bf16[512,256]{1,0:T(8,128)(2,1)S(1)}, bf16[512,256]{1,0:T(8,128)(2,1)S(1)}, u32[]{:S(2)}, u32[]{:S(2)}) %collective-permute-start.20) | collective-permute-done | bytes 262176 | tf_op jit(solution)/shard_map/ppermute | solution.py:53
  79.4 1.7 %collective-permute-start.21 = (bf16[512,256]{1,0:T(8,128)(2,1)S(1)}, bf16[512,256]{1,0:T(8,128)(2,1)S(1)}, u32[]{:S(2)}, u32[]{:S(2)}) collective-permute-start(bf16[512,256]{1,0:T(8,128)(2,1)S(1)} %collective-permute-done.19), channel_id=1, source_target_pairs={{0,2},{1,3},{2,4},{3,5},{4,6},{5,7},{6,8},{7,9},{8,10},{9,11},{10,... | collective-permute-start | bytes 786440 | tf_op jit(solution)/shard_map/ppermute | solution.py:49
  81.2 1.5 %collective-permute-start.22 = (bf16[512,256]{1,0:T(8,128)(2,1)S(1)}, bf16[512,256]{1,0:T(8,128)(2,1)S(1)}, u32[]{:S(2)}, u32[]{:S(2)}) collective-permute-start(bf16[512,256]{1,0:T(8,128)(2,1)S(1)} %collective-permute-done.20), channel_id=1, source_target_pairs={{0,14},{1,15},{2,0},{3,1},{4,2},{5,3},{6,4},{7,5},{8,6},{9,7},{10,... | collective-permute-start | bytes 786440 | tf_op jit(solution)/shard_map/ppermute | solution.py:53
  83.1 1.2 %fusion.42 = f32[512,256]{1,0:T(8,128)S(1)} fusion(bf16[4,2,256,512]{3,2,1,0:T(8,128)(2,1)} %collective-permute-done.18, s32[]{:T(128)S(6)} %select_n.702, s32[]{:T(128)S(6)} %select_n.704, bf16[512,256]{1,0:T(8,128)(2,1)S(1)} %collective-permute-done.19), kind=kOutput, calls=%fused_computation.56 | convolution fusion | flops 67108864 | bytes 917512 | tf_op jit(solution)/shard_map/dot_general | solution.py:171
  84.7 1.2 %add_add_fusion.4 = f32[512,256]{1,0:T(8,128)S(1)} fusion(f32[512,256]{1,0:T(8,128)S(1)} %fusion.50, f32[512,256]{1,0:T(8,128)S(1)} %fusion.42, bf16[4,2,256,512]{3,2,1,0:T(8,128)(2,1)} %collective-permute-done.18, s32[]{:T(128)S(6)} %select_n.708, s32[]{:T(128)S(6)} %select_n.710, bf16[512,256]{1,0:T(8,128)(2,1)S(1)} %collective-permute-done.20), kind=kOutput, calls=%fused_computation.24 | convolution fusion | flops 67371008 | bytes 1966088 | tf_op jit(solution)/shard_map/dot_general | solution.py:171
  85.9 2.1 %collective-permute-done.21 = bf16[512,256]{1,0:T(8,128)(2,1)S(1)} collective-permute-done((bf16[512,256]{1,0:T(8,128)(2,1)S(1)}, bf16[512,256]{1,0:T(8,128)(2,1)S(1)}, u32[]{:S(2)}, u32[]{:S(2)}) %collective-permute-start.21) | collective-permute-done | bytes 262176 | tf_op jit(solution)/shard_map/ppermute | solution.py:49
  88.0 0.8 collective-permute-start.24
  88.8 2.4 %collective-permute-start.25 = (bf16[512,256]{1,0:T(8,128)(2,1)S(1)}, bf16[512,256]{1,0:T(8,128)(2,1)S(1)}, u32[]{:S(2)}, u32[]{:S(2)}) collective-permute-start(bf16[512,256]{1,0:T(8,128)(2,1)S(1)} %collective-permute-done.22), channel_id=1, source_target_pairs={{0,14},{1,15},{2,0},{3,1},{4,2},{5,3},{6,4},{7,5},{8,6},{9,7},{10,... | collective-permute-start | bytes 786440 | tf_op jit(solution)/shard_map/ppermute | solution.py:53
  91.5 1.2 %fusion.30 = f32[512,256]{1,0:T(8,128)S(1)} fusion(bf16[4,2,256,512]{3,2,1,0:T(8,128)(2,1)} %collective-permute-done.18, s32[]{:T(128)S(6)} %select_n.719, s32[]{:T(128)S(6)} %select_n.721, bf16[512,256]{1,0:T(8,128)(2,1)S(1)} %collective-permute-done.21), kind=kOutput, calls=%fused_computation.48 | convolution fusion | flops 67108864 | bytes 917512 | tf_op jit(solution)/shard_map/dot_general | solution.py:171
  93.0 1.2 %add_add_fusion.2 = f32[512,256]{1,0:T(8,128)S(1)} fusion(f32[512,256]{1,0:T(8,128)S(1)} %add_add_fusion.4, f32[512,256]{1,0:T(8,128)S(1)} %fusion.30, bf16[4,2,256,512]{3,2,1,0:T(8,128)(2,1)} %collective-permute-done.18, s32[]{:T(128)S(6)} %select_n.725, s32[]{:T(128)S(6)} %select_n.727, bf16[512,256]{1,0:T(8,128)(2,1)S(1)} %collective-permute-done.22), kind=kOutput, calls=%fused_computation.22 | convolution fusion | flops 67371008 | bytes 1966088 | tf_op jit(solution)/shard_map/dot_general | solution.py:171
  94.3 1.4 %collective-permute-done.24 = bf16[512,256]{1,0:T(8,128)(2,1)S(1)} collective-permute-done((bf16[512,256]{1,0:T(8,128)(2,1)S(1)}, bf16[512,256]{1,0:T(8,128)(2,1)S(1)}, u32[]{:S(2)}, u32[]{:S(2)}) %collective-permute-start.24) | collective-permute-done | bytes 262176 | tf_op jit(solution)/shard_map/ppermute | solution.py:49
  96.3 2.5 %collective-permute-start.27 = (bf16[512,256]{1,0:T(8,128)(2,1)S(1)}, bf16[512,256]{1,0:T(8,128)(2,1)S(1)}, u32[]{:S(2)}, u32[]{:S(2)}) collective-permute-start(bf16[512,256]{1,0:T(8,128)(2,1)S(1)} %broadcast_select_fusion), channel_id=1, source_target_pairs={{0,2},{1,3},{2,4},{3,5},{4,6},{5,7},{6,8},{7,9},{8,10},{9,11},{10,... | collective-permute-start | bytes 786440 | tf_op jit(solution)/shard_map/ppermute | solution.py:36
  98.8 1.2 %fusion.14 = f32[512,256]{1,0:T(8,128)S(1)} fusion(bf16[4,2,256,512]{3,2,1,0:T(8,128)(2,1)} %collective-permute-done.18, s32[]{:T(128)S(6)} %select_n.737, s32[]{:T(128)S(6)} %select_n.739, bf16[512,256]{1,0:T(8,128)(2,1)S(1)} %collective-permute-done.25), kind=kOutput, calls=%fused_computation.36 | convolution fusion | flops 67108864 | bytes 917512 | tf_op jit(solution)/shard_map/dot_general | solution.py:171
  100.2 1.2 %fusion.16 = f32[512,256]{1,0:T(8,128)S(1)} fusion(bf16[4,2,256,512]{3,2,1,0:T(8,128)(2,1)} %collective-permute-done.18, s32[]{:T(128)S(6)} %select_n.731, s32[]{:T(128)S(6)} %select_n.733, bf16[512,256]{1,0:T(8,128)(2,1)S(1)} %collective-permute-done.24), kind=kOutput, calls=%fused_computation.38 | convolution fusion | flops 67108864 | bytes 917512 | tf_op jit(solution)/shard_map/dot_general | solution.py:171
  101.7 2.2 %collective-permute-done.27 = bf16[512,256]{1,0:T(8,128)(2,1)S(1)} collective-permute-done((bf16[512,256]{1,0:T(8,128)(2,1)S(1)}, bf16[512,256]{1,0:T(8,128)(2,1)S(1)}, u32[]{:S(2)}, u32[]{:S(2)}) %collective-permute-start.27) | collective-permute-done | bytes 262176 | tf_op jit(solution)/shard_map/ppermute | solution.py:36
  103.9 1.2 %add_add_fusion = f32[512,256]{1,0:T(8,128)S(1)} fusion(f32[512,256]{1,0:T(8,128)S(1)} %fusion.14, f32[512,256]{1,0:T(8,128)S(1)} %add_add_fusion.2, f32[512,256]{1,0:T(8,128)S(1)} %fusion.16, bf16[4,2,256,512]{3,2,1,0:T(8,128)(2,1)} %collective-permute-done.18, s32[]{:T(128)S(6)} %select_n.743, s32[]{:T(128)S(6)} %select_n.745, ...), kind=kOutput, calls=%fused_computation.20 | convolution fusion | flops 67502080 | bytes 2490376 | tf_op jit(solution)/shard_map/dot_general | solution.py:171
  105.8 0.7 maximum_bitcast_fusion
  106.6 4.0 %collective-permute-done.28 = bf16[256,256]{1,0:T(8,128)(2,1)S(1)} collective-permute-done((bf16[256,256]{1,0:T(8,128)(2,1)S(1)}, bf16[256,256]{1,0:T(8,128)(2,1)S(1)}, u32[]{:S(2)}, u32[]{:S(2)}) %collective-permute-start.28) | collective-permute-done | bytes 131104 | tf_op jit(solution)/shard_map/ppermute | solution.py:99
  110.7 0.7 maximum_bitcast_fusion.1
  (76 shorter events, 9.6 us)
Async XLA Ops:
  0.6 15.3 %copy-start = (bf16[2,1,1,256,1,1,256]{6,3,5,4,2,1,0:T(8,128)(2,1)S(1)}, bf16[2,1,1,256,1,1,256]{6,3,5,4,2,1,0:T(8,128)(2,1)}, u32[]{:S(2)}) copy-start(bf16[2,1,1,256,1,1,256]{6,3,5,4,2,1,0:T(8,128)(2,1)} %param.5) | copy-start | bytes 786436
  1.7 8.0 %collective-permute-start.1 = (bf16[256,256]{1,0:T(8,128)(2,1)S(1)}, bf16[256,256]{1,0:T(8,128)(2,1)S(1)}, u32[]{:S(2)}, u32[]{:S(2)}) collective-permute-start(bf16[256,256]{1,0:T(8,128)(2,1)S(1)} %get-tuple-element.81), channel_id=1, source_target_pairs={{0,1},{1,17},{2,3},{3,19},{4,5},{5,21},{6,7},{7,23},{8,9},{9,25},{... | collective-permute-start | bytes 393224 | tf_op jit(solution)/shard_map/ppermute | solution.py:36
  3.4 3.5 %collective-permute-start = (bf16[256,256]{1,0:T(8,128)(2,1)S(1)}, bf16[256,256]{1,0:T(8,128)(2,1)S(1)}, u32[]{:S(2)}, u32[]{:S(2)}) collective-permute-start(bf16[256,256]{1,0:T(8,128)(2,1)S(1)} %get-tuple-element.80), channel_id=1, source_target_pairs={{0,0},{1,16},{2,2},{3,18},{4,4},{5,20},{6,6},{7,22},{8,8},{9,24},{... | collective-permute-start | bytes 393224 | tf_op jit(solution)/shard_map/ppermute | solution.py:36
  6.9 9.1 %collective-permute-start.2 = (bf16[256,256]{1,0:T(8,128)(2,1)S(1)}, bf16[256,256]{1,0:T(8,128)(2,1)S(1)}, u32[]{:S(2)}, u32[]{:S(2)}) collective-permute-start(bf16[256,256]{1,0:T(8,128)(2,1)S(1)} %select_bitcast_fusion.7), channel_id=1, source_target_pairs={{0,1},{1,0},{2,3},{3,2},{4,5},{5,4},{6,7},{7,6},{8,9},{9,8},{10,11... | collective-permute-start | bytes 393224 | tf_op jit(solution)/shard_map/ppermute | solution.py:99
  9.9 11.2 %collective-permute-start.8 = (bf16[512,256]{1,0:T(8,128)(2,1)S(1)}, bf16[512,256]{1,0:T(8,128)(2,1)S(1)}, u32[]{:S(2)}, u32[]{:S(2)}) collective-permute-start(bf16[512,256]{1,0:T(8,128)(2,1)S(1)} %bitcast_select_fusion), channel_id=1, source_target_pairs={{0,2},{1,3},{2,4},{3,5},{4,6},{5,7},{6,8},{7,9},{8,10},{9,11},{10,... | collective-permute-start | bytes 786440 | tf_op jit(solution)/shard_map/ppermute | solution.py:49
  11.9 9.3 %collective-permute-start.9 = (bf16[512,256]{1,0:T(8,128)(2,1)S(1)}, bf16[512,256]{1,0:T(8,128)(2,1)S(1)}, u32[]{:S(2)}, u32[]{:S(2)}) collective-permute-start(bf16[512,256]{1,0:T(8,128)(2,1)S(1)} %bitcast_select_fusion), channel_id=1, source_target_pairs={{0,14},{1,15},{2,0},{3,1},{4,2},{5,3},{6,4},{7,5},{8,6},{9,7},{10,... | collective-permute-start | bytes 786440 | tf_op jit(solution)/shard_map/ppermute | solution.py:53
  16.0 8.5 %collective-permute-start.4 = (bf16[256,512]{1,0:T(8,128)(2,1)S(1)}, bf16[256,512]{1,0:T(8,128)(2,1)}, u32[]{:S(2)}, u32[]{:S(2)}) collective-permute-start(bf16[256,512]{1,0:T(8,128)(2,1)S(1)} %get-tuple-element.79), channel_id=1, source_target_pairs={{0,64},{16,80},{32,96},{48,112},{64,0},{80,16},{96,32},{112,48},{1... | collective-permute-start | bytes 786440 | tf_op jit(solution)/shard_map/ppermute | solution.py:122
  17.5 10.2 %collective-permute-start.3 = (bf16[256,512]{1,0:T(8,128)(2,1)S(1)}, bf16[256,512]{1,0:T(8,128)(2,1)S(1)}, u32[]{:S(2)}, u32[]{:S(2)}) collective-permute-start(bf16[256,512]{1,0:T(8,128)(2,1)S(1)} %get-tuple-element.79), channel_id=1, source_target_pairs={{0,128},{16,144},{32,160},{48,176},{64,192},{80,208},{96,224},{112... | collective-permute-start | bytes 786440 | tf_op jit(solution)/shard_map/ppermute | solution.py:124
  21.1 9.3 %collective-permute-start.10 = (bf16[512,256]{1,0:T(8,128)(2,1)S(1)}, bf16[512,256]{1,0:T(8,128)(2,1)S(1)}, u32[]{:S(2)}, u32[]{:S(2)}) collective-permute-start(bf16[512,256]{1,0:T(8,128)(2,1)S(1)} %collective-permute-done.8), channel_id=1, source_target_pairs={{0,2},{1,3},{2,4},{3,5},{4,6},{5,7},{6,8},{7,9},{8,10},{9,11},{10,... | collective-permute-start | bytes 786440 | tf_op jit(solution)/shard_map/ppermute | solution.py:49
  21.2 10.3 %collective-permute-start.11 = (bf16[512,256]{1,0:T(8,128)(2,1)S(1)}, bf16[512,256]{1,0:T(8,128)(2,1)S(1)}, u32[]{:S(2)}, u32[]{:S(2)}) collective-permute-start(bf16[512,256]{1,0:T(8,128)(2,1)S(1)} %collective-permute-done.9), channel_id=1, source_target_pairs={{0,14},{1,15},{2,0},{3,1},{4,2},{5,3},{6,4},{7,5},{8,6},{9,7},{10,... | collective-permute-start | bytes 786440 | tf_op jit(solution)/shard_map/ppermute | solution.py:53
  24.5 12.0 %collective-permute-start.5 = (bf16[256,512]{1,0:T(8,128)(2,1)}, bf16[256,512]{1,0:T(8,128)(2,1)S(1)}, u32[]{:S(2)}, u32[]{:S(2)}) collective-permute-start(bf16[256,512]{1,0:T(8,128)(2,1)} %collective-permute-done.4), channel_id=1, source_target_pairs={{0,128},{16,144},{32,160},{48,176},{64,192},{80,208},{96,224},{112... | collective-permute-start | bytes 786440 | tf_op jit(solution)/shard_map/ppermute | solution.py:129
  27.7 12.9 %collective-permute-start.6 = (bf16[2,256,512]{2,1,0:T(8,128)(2,1)S(1)}, bf16[2,256,512]{2,1,0:T(8,128)(2,1)S(1)}, u32[]{:S(2)}, u32[]{:S(2)}) collective-permute-start(bf16[2,256,512]{2,1,0:T(8,128)(2,1)S(1)} %get-tuple-element.74), channel_id=1, source_target_pairs={{0,32},{16,48},{32,64},{48,80},{64,96},{80,112},{96,0},{112,16},{1... | collective-permute-start | bytes 1572872 | tf_op jit(solution)/shard_map/ppermute | solution.py:122
  28.3 12.6 %collective-permute-start.7 = (bf16[2,256,512]{2,1,0:T(8,128)(2,1)S(1)}, bf16[2,256,512]{2,1,0:T(8,128)(2,1)S(1)}, u32[]{:S(2)}, u32[]{:S(2)}) collective-permute-start(bf16[2,256,512]{2,1,0:T(8,128)(2,1)S(1)} %get-tuple-element.74), channel_id=1, source_target_pairs={{0,96},{16,112},{32,0},{48,16},{64,32},{80,48},{96,64},{112,80},{1... | collective-permute-start | bytes 1572872 | tf_op jit(solution)/shard_map/ppermute | solution.py:122
  30.4 10.1 %collective-permute-start.12 = (bf16[512,256]{1,0:T(8,128)(2,1)S(1)}, bf16[512,256]{1,0:T(8,128)(2,1)S(1)}, u32[]{:S(2)}, u32[]{:S(2)}) collective-permute-start(bf16[512,256]{1,0:T(8,128)(2,1)S(1)} %collective-permute-done.10), channel_id=1, source_target_pairs={{0,2},{1,3},{2,4},{3,5},{4,6},{5,7},{6,8},{7,9},{8,10},{9,11},{10,... | collective-permute-start | bytes 786440 | tf_op jit(solution)/shard_map/ppermute | solution.py:49
  31.4 9.1 %collective-permute-start.13 = (bf16[512,256]{1,0:T(8,128)(2,1)S(1)}, bf16[512,256]{1,0:T(8,128)(2,1)S(1)}, u32[]{:S(2)}, u32[]{:S(2)}) collective-permute-start(bf16[512,256]{1,0:T(8,128)(2,1)S(1)} %collective-permute-done.11), channel_id=1, source_target_pairs={{0,14},{1,15},{2,0},{3,1},{4,2},{5,3},{6,4},{7,5},{8,6},{9,7},{10,... | collective-permute-start | bytes 786440 | tf_op jit(solution)/shard_map/ppermute | solution.py:53
  40.5 7.7 %collective-permute-start.14 = (bf16[512,256]{1,0:T(8,128)(2,1)S(1)}, bf16[512,256]{1,0:T(8,128)(2,1)S(1)}, u32[]{:S(2)}, u32[]{:S(2)}) collective-permute-start(bf16[512,256]{1,0:T(8,128)(2,1)S(1)} %broadcast_select_fusion.1), channel_id=1, source_target_pairs={{0,2},{1,3},{2,4},{3,5},{4,6},{5,7},{6,8},{7,9},{8,10},{9,11},{10,... | collective-permute-start | bytes 786440 | tf_op jit(solution)/shard_map/ppermute | solution.py:36
  41.6 21.5 %collective-permute-start.18 = (bf16[4,2,256,512]{3,2,1,0:T(8,128)(2,1)S(1)}, bf16[4,2,256,512]{3,2,1,0:T(8,128)(2,1)}, u32[]{:S(2)}, u32[]{:S(2)}) collective-permute-start(bf16[4,2,256,512]{3,2,1,0:T(8,128)(2,1)S(1)} %bitcast_dynamic-update-slice_fusion), channel_id=1, source_target_pairs={{0,16},{16,0},{32,48},{48,32},{64,80},{80,64},{96,112},{112,96},{1... | collective-permute-start | bytes 6291464 | tf_op jit(solution)/shard_map/ppermute | solution.py:163
  48.7 2.0 %collective-permute-start.15 = (f32[512,256]{1,0:T(8,128)S(1)}, f32[512,256]{1,0:T(8,128)S(1)}, u32[]{:S(2)}, u32[]{:S(2)}) collective-permute-start(f32[512,256]{1,0:T(8,128)S(1)} %fusion.1), channel_id=1, source_target_pairs={{0,16},{16,0},{32,48},{48,32},{64,80},{80,64},{96,112},{112,96},{1... | collective-permute-start | bytes 1572872 | tf_op jit(solution)/shard_map/ppermute | solution.py:158
  49.5 7.6 %copy-start.1 = (bf16[2,1,1,256,1,1,256]{6,3,5,4,2,1,0:T(8,128)(2,1)S(1)}, bf16[2,1,1,256,1,1,256]{6,3,5,4,2,1,0:T(8,128)(2,1)}, u32[]{:S(2)}) copy-start(bf16[2,1,1,256,1,1,256]{6,3,5,4,2,1,0:T(8,128)(2,1)} %param.6) | copy-start | bytes 786436
  51.0 12.1 %collective-permute-start.17 = (bf16[512,256]{1,0:T(8,128)(2,1)S(1)}, bf16[512,256]{1,0:T(8,128)(2,1)S(1)}, u32[]{:S(2)}, u32[]{:S(2)}) collective-permute-start(bf16[512,256]{1,0:T(8,128)(2,1)S(1)} %fusion.8), channel_id=1, source_target_pairs={{0,0},{1,1},{2,46},{3,47},{4,76},{5,77},{6,106},{7,107},{8,136},{9... | collective-permute-start | bytes 786440 | tf_op jit(solution)/shard_map/ppermute | solution.py:36
  57.0 1.4 %collective-permute-start.16 = (bf16[256,256]{1,0:T(8,128)(2,1)S(1)}, bf16[256,256]{1,0:T(8,128)(2,1)S(1)}, u32[]{:S(2)}, u32[]{:S(2)}) collective-permute-start(bf16[256,256]{1,0:T(8,128)(2,1)S(1)} %slice.215), channel_id=1, source_target_pairs={{0,16},{16,0},{32,48},{48,32},{64,80},{80,64},{96,112},{112,96},{1... | collective-permute-start | bytes 393224 | tf_op jit(solution)/shard_map/ppermute | solution.py:165
  63.1 11.5 %collective-permute-start.19 = (bf16[512,256]{1,0:T(8,128)(2,1)S(1)}, bf16[512,256]{1,0:T(8,128)(2,1)S(1)}, u32[]{:S(2)}, u32[]{:S(2)}) collective-permute-start(bf16[512,256]{1,0:T(8,128)(2,1)S(1)} %collective-permute-done.17), channel_id=1, source_target_pairs={{0,2},{1,3},{2,4},{3,5},{4,6},{5,7},{6,8},{7,9},{8,10},{9,11},{10,... | collective-permute-start | bytes 786440 | tf_op jit(solution)/shard_map/ppermute | solution.py:49
  66.8 12.6 %collective-permute-start.20 = (bf16[512,256]{1,0:T(8,128)(2,1)S(1)}, bf16[512,256]{1,0:T(8,128)(2,1)S(1)}, u32[]{:S(2)}, u32[]{:S(2)}) collective-permute-start(bf16[512,256]{1,0:T(8,128)(2,1)S(1)} %collective-permute-done.17), channel_id=1, source_target_pairs={{0,14},{1,15},{2,0},{3,1},{4,2},{5,3},{6,4},{7,5},{8,6},{9,7},{10,... | collective-permute-start | bytes 786440 | tf_op jit(solution)/shard_map/ppermute | solution.py:53
  79.4 8.6 %collective-permute-start.21 = (bf16[512,256]{1,0:T(8,128)(2,1)S(1)}, bf16[512,256]{1,0:T(8,128)(2,1)S(1)}, u32[]{:S(2)}, u32[]{:S(2)}) collective-permute-start(bf16[512,256]{1,0:T(8,128)(2,1)S(1)} %collective-permute-done.19), channel_id=1, source_target_pairs={{0,2},{1,3},{2,4},{3,5},{4,6},{5,7},{6,8},{7,9},{8,10},{9,11},{10,... | collective-permute-start | bytes 786440 | tf_op jit(solution)/shard_map/ppermute | solution.py:49
  81.2 6.8 %collective-permute-start.22 = (bf16[512,256]{1,0:T(8,128)(2,1)S(1)}, bf16[512,256]{1,0:T(8,128)(2,1)S(1)}, u32[]{:S(2)}, u32[]{:S(2)}) collective-permute-start(bf16[512,256]{1,0:T(8,128)(2,1)S(1)} %collective-permute-done.20), channel_id=1, source_target_pairs={{0,14},{1,15},{2,0},{3,1},{4,2},{5,3},{6,4},{7,5},{8,6},{9,7},{10,... | collective-permute-start | bytes 786440 | tf_op jit(solution)/shard_map/ppermute | solution.py:53
  82.7 5.3 %collective-permute-start.23 = (bf16[256,256]{1,0:T(8,128)(2,1)S(1)}, bf16[256,256]{1,0:T(8,128)(2,1)S(1)}, u32[]{:S(2)}, u32[]{:S(2)}) collective-permute-start(bf16[256,256]{1,0:T(8,128)(2,1)S(1)} %broadcast_select_fusion.3), channel_id=1, source_target_pairs={{0,1},{1,0},{2,3},{3,2},{4,5},{5,4},{6,7},{7,6},{8,9},{9,8},{10,11... | collective-permute-start | bytes 393224 | tf_op jit(solution)/shard_map/ppermute | solution.py:68
  88.0 7.7 %collective-permute-start.24 = (bf16[512,256]{1,0:T(8,128)(2,1)S(1)}, bf16[512,256]{1,0:T(8,128)(2,1)S(1)}, u32[]{:S(2)}, u32[]{:S(2)}) collective-permute-start(bf16[512,256]{1,0:T(8,128)(2,1)S(1)} %collective-permute-done.21), channel_id=1, source_target_pairs={{0,2},{1,3},{2,4},{3,5},{4,6},{5,7},{6,8},{7,9},{8,10},{9,11},{10,... | collective-permute-start | bytes 786440 | tf_op jit(solution)/shard_map/ppermute | solution.py:49
  88.8 6.8 %collective-permute-start.25 = (bf16[512,256]{1,0:T(8,128)(2,1)S(1)}, bf16[512,256]{1,0:T(8,128)(2,1)S(1)}, u32[]{:S(2)}, u32[]{:S(2)}) collective-permute-start(bf16[512,256]{1,0:T(8,128)(2,1)S(1)} %collective-permute-done.22), channel_id=1, source_target_pairs={{0,14},{1,15},{2,0},{3,1},{4,2},{5,3},{6,4},{7,5},{8,6},{9,7},{10,... | collective-permute-start | bytes 786440 | tf_op jit(solution)/shard_map/ppermute | solution.py:53
  91.3 5.0 %collective-permute-start.26 = (bf16[256,256]{1,0:T(8,128)(2,1)S(1)}, bf16[256,256]{1,0:T(8,128)(2,1)S(1)}, u32[]{:S(2)}, u32[]{:S(2)}) collective-permute-start(bf16[256,256]{1,0:T(8,128)(2,1)S(1)} %select_bitcast_fusion.2), channel_id=1, source_target_pairs={{0,1},{1,0},{2,3},{3,2},{4,5},{5,4},{6,7},{7,6},{8,9},{9,8},{10,11... | collective-permute-start | bytes 393224 | tf_op jit(solution)/shard_map/ppermute | solution.py:68
  96.3 7.7 %collective-permute-start.27 = (bf16[512,256]{1,0:T(8,128)(2,1)S(1)}, bf16[512,256]{1,0:T(8,128)(2,1)S(1)}, u32[]{:S(2)}, u32[]{:S(2)}) collective-permute-start(bf16[512,256]{1,0:T(8,128)(2,1)S(1)} %broadcast_select_fusion), channel_id=1, source_target_pairs={{0,2},{1,3},{2,4},{3,5},{4,6},{5,7},{6,8},{7,9},{8,10},{9,11},{10,... | collective-permute-start | bytes 786440 | tf_op jit(solution)/shard_map/ppermute | solution.py:36
  105.5 5.1 %collective-permute-start.28 = (bf16[256,256]{1,0:T(8,128)(2,1)S(1)}, bf16[256,256]{1,0:T(8,128)(2,1)S(1)}, u32[]{:S(2)}, u32[]{:S(2)}) collective-permute-start(bf16[256,256]{1,0:T(8,128)(2,1)S(1)} %subtract_convert_fusion), channel_id=1, source_target_pairs={{0,1},{1,0},{2,3},{3,2},{4,5},{5,4},{6,7},{7,6},{8,9},{9,8},{10,11... | collective-permute-start | bytes 393224 | tf_op jit(solution)/shard_map/ppermute | solution.py:99

commit v4 on v3

--- a/solution.py
+++ b/solution.py
@@ -30,6 +30,21 @@
             chip, c, z, yl = fn(p // 2, p % 2, q // 2, q % 2)
             pairs.append((p * 16 + q, (chip * 2 + c) * 16 + (z % NZ) * 2 + yl))
     return pairs
+
+
+LAND = (
+    (0, 5, 7, 2, 1, 4, 6, 7),
+    (6, 3, 1, 0, 6, 7, 1, 0),
+    (7, 2, 0, 1, 3, 2, 0, 1),
+    (5, 4, 2, 7, 4, 5, 7, 2),
+    (2, 7, 4, 5, 7, 6, 5, 4),
+    (1, 0, 6, 3, 5, 0, 2, 3),
+    (4, 1, 3, 6, 0, 1, 3, 6),
+    (3, 6, 5, 4, 2, 3, 4, 5),
+)
+LANDED = [
+    sum(p << (3 * LAND[p][col]) for p in range(NZ)) for col in range(NZ)
+]
 
 
 def move(block, pairs):
@@ -80,6 +95,23 @@
     return add(total, NZ // 2, last), swapped
 
 
+def z_two(piece, opposite, add, total, beside):
+    one = up(piece), down(piece)
+    three = up(opposite), down(opposite)
+    total = add(total, 0, piece)
+    *one, total = tie(*one, total)
+    two = up(one[0]), down(one[1])
+    swapped = []
+    for block, after in zip(beside, one):
+        block, _ = tie(block, after)
+        swapped.append(lax.ppermute(block, "pcol", SWAP))
+    total = add(total, NZ // 2, opposite)
+    for offset, blocks in ((1, one), (-3, three), (2, two)):
+        total = add(total, -offset, blocks[0])
+        total = add(total, offset, blocks[1])
+    return total, swapped
+
+
 def on_device(anc_inverse, factor_panel, diag_inverse, block_pattern):
     p = lax.axis_index("prow")
     q = lax.axis_index("pcol")
@@ -159,17 +191,24 @@
     off = kept + jnp.concatenate([theirs[256:], theirs[:256]], axis=0)
     off = (-off).astype(jnp.bfloat16)
 
-    o_piece = move(off, both_perm(lambda chip, c, z, yl: (z, c, chip - z, yl)))
+    o_piece = move(off, both_perm(lambda chip, c, z, yl: (z, c, LAND[chip][z], yl)))
+    o_other = move(off, both_perm(lambda chip, c, z, yl: (z, c, LAND[chip][z] + 4, yl)))
     u_cross = lax.ppermute(u_all, "prow", CROSS)
-    o_piece, u_cross = tie(o_piece, u_cross)
+    o_piece, o_other, u_cross = tie(o_piece, o_other, u_cross)
+    (u_cross,) = tie(jnp.where(p >= 0, u_cross, jnp.zeros_like(u_cross)))
     first, second = off[:256], lax.ppermute(off[256:], "prow", CROSS)
     off_mine = jnp.where(same, first, second)
 
+    landed = sum(
+        jnp.where(p // 2 == col, parts, 0) for col, parts in enumerate(LANDED)
+    )
+
     def add_inner(total, offset, block):
+        owner = (landed >> (3 * ((z + offset + NZ) % NZ))) & 7
         return tuple(
             part
             + lax.dot_general(
-                u_rows(panel, p // 2 + z + offset),
+                u_rows(panel, owner),
                 rows,
                 (((0,), (0,)), ((), ())),
                 preferred_element_type=jnp.float32,
@@ -179,8 +218,8 @@
             )
         )
 
-    total, (off_got, d_got) = z_ring(
-        o_piece, c, add_inner, (zero, zero), (jnp.where(same, second, first), other(diag))
+    total, (off_got, d_got) = z_two(
+        o_piece, o_other, add_inner, (zero, zero), (jnp.where(same, second, first), other(diag))
     )
     first = total[0][:256] + total[1][256:]
     second = total[0][256:] + total[1][:256]

time: 113 us -> 106 us (0.938); the launches traced: 111 us -> 106 us
  matrix products: 15.6 us -> 8.18 us
  other arithmetic: 4.96 us -> 6.68 us
    dot_general x16, matrix products: 11.9 us -> 4.53 us  [add_inner(): lax.dot_general(u_rows(panel, owner), rows, (((0,), (0,)), ((), ())), pre...]
    ppermute x5, waiting for transfers between devices: 11 us -> 15.7 us  [move(): return lax.ppermute(block, ('prow', 'pcol'), pairs)]
    ppermute x6, waiting for transfers between devices: 4.89 us -> 0.6 us  [down(): return lax.ppermute(block, 'pcol', DOWN)]
    ppermute x6, waiting for transfers between devices: 12.9 us -> 9.07 us  [up(): return lax.ppermute(block, 'pcol', UP)]
    ppermute x6, starting transfers between devices: 9.27 us -> 6.16 us  [up(): return lax.ppermute(block, 'pcol', UP)]
    ppermute x3, waiting for transfers between devices: 0.31 us -> 3.33 us  [along_x(): lax.ppermute(block, 'prow', row_perm(lambda h, x, c: (h, x + step, c)))]
    ppermute x5, starting transfers between devices: 10.9 us -> 13.3 us  [move(): return lax.ppermute(block, ('prow', 'pcol'), pairs)]
    ppermute x6, starting transfers between devices: 17.3 us -> 19.2 us  [down(): return lax.ppermute(block, 'pcol', DOWN)]
  transfers between devices with their start and end apart: 29 -> 29, of which waited for: 16 -> 14; matrix products, arithmetic and copies ran while one was open for 17% -> 14% of each run, Pallas kernels for 0% -> 0%
where the time goes in v4:
time: 106 us
  starting transfers between devices  52.2 us (49%)
  waiting for transfers between devices  34.7 us (33%)
  matrix products  8.18 us (8%)
  other arithmetic  6.68 us (6%)
  local copies, waits for them, and re-layouts  2.34 us (2%)
  between operations  1.76 us (2%)
    ppermute x6, starting transfers between devices, down(): return lax.ppermute(block, 'pcol', DOWN)  19.2 us
    ppermute x5, waiting for transfers between devices, move(): return lax.ppermute(block, ('prow', 'pcol'), pairs)  15.7 us
    ppermute x5, starting transfers between devices, move(): return lax.ppermute(block, ('prow', 'pcol'), pairs)  13.3 us
    ppermute x6, waiting for transfers between devices, up(): return lax.ppermute(block, 'pcol', UP)  9.07 us
    ppermute x6, starting transfers between devices, up(): return lax.ppermute(block, 'pcol', UP)  6.16 us
    dot_general x16, matrix products, add_inner(): lax.dot_general(u_rows(panel, owner), rows, (((0,), (0,)), ((), ())), pre...  4.53 us
    ppermute x2, waiting for transfers between devices, swap(): return lax.ppermute(block, 'pcol', SWAP)  4.18 us
    dot_general x16, matrix products, add_product(): jnp.dot(block, cols, preferred_element_type=jnp.float32)  3.65 us
  transfers between devices with their start and end apart: 29, of which 14 were waited for; matrix products, arithmetic and copies ran while one was open for 14% of the time, Pallas kernels for 0%

profile of v4, /device:TPU:6, one launch (start us, length us, event | category | flops | bytes accessed | tf_op | source)
XLA Modules:
  0.0 105.9 jit_solution(10269207501766957314)
XLA Ops:
  0.7 1.0 select_bitcast_fusion.6
  1.7 0.7 collective-permute-start
  2.4 2.9 %collective-permute-start.1 = (bf16[256,256]{1,0:T(8,128)(2,1)S(1)}, bf16[256,256]{1,0:T(8,128)(2,1)S(1)}, u32[]{:S(2)}, u32[]{:S(2)}) collective-permute-start(bf16[256,256]{1,0:T(8,128)(2,1)S(1)} %get-tuple-element.47), channel_id=1, source_target_pairs={{0,1},{1,17},{2,3},{3,19},{4,5},{5,21},{6,7},{7,23},{8,9},{9,25},{... | collective-permute-start | bytes 393224 | tf_op jit(solution)/shard_map/ppermute | solution.py:51
  5.3 0.8 dynamic_slice.75
  6.1 0.9 compare_reduce_fusion
  7.1 1.0 select_bitcast_fusion.7
  8.1 2.2 %collective-permute-start.2 = (bf16[256,256]{1,0:T(8,128)(2,1)S(1)}, bf16[256,256]{1,0:T(8,128)(2,1)S(1)}, u32[]{:S(2)}, u32[]{:S(2)}) collective-permute-start(bf16[256,256]{1,0:T(8,128)(2,1)S(1)} %select_bitcast_fusion.7), channel_id=1, source_target_pairs={{0,1},{1,0},{2,3},{3,2},{4,5},{5,4},{6,7},{7,6},{8,9},{9,8},{10,11... | collective-permute-start | bytes 393224 | tf_op jit(solution)/shard_map/ppermute | solution.py:131
  10.5 2.0 %collective-permute-start.8 = (bf16[512,256]{1,0:T(8,128)(2,1)S(1)}, bf16[512,256]{1,0:T(8,128)(2,1)S(1)}, u32[]{:S(2)}, u32[]{:S(2)}) collective-permute-start(bf16[512,256]{1,0:T(8,128)(2,1)S(1)} %bitcast_select_fusion), channel_id=1, source_target_pairs={{0,2},{1,3},{2,4},{3,5},{4,6},{5,7},{6,8},{7,9},{8,10},{9,11},{10,... | collective-permute-start | bytes 786440 | tf_op jit(solution)/shard_map/ppermute | solution.py:64
  12.5 4.0 %collective-permute-start.9 = (bf16[512,256]{1,0:T(8,128)(2,1)S(1)}, bf16[512,256]{1,0:T(8,128)(2,1)S(1)}, u32[]{:S(2)}, u32[]{:S(2)}) collective-permute-start(bf16[512,256]{1,0:T(8,128)(2,1)S(1)} %bitcast_select_fusion), channel_id=1, source_target_pairs={{0,14},{1,15},{2,0},{3,1},{4,2},{5,3},{6,4},{7,5},{8,6},{9,7},{10,... | collective-permute-start | bytes 786440 | tf_op jit(solution)/shard_map/ppermute | solution.py:68
  16.6 1.5 %collective-permute-start.4 = (bf16[256,512]{1,0:T(8,128)(2,1)S(1)}, bf16[256,512]{1,0:T(8,128)(2,1)}, u32[]{:S(2)}, u32[]{:S(2)}) collective-permute-start(bf16[256,512]{1,0:T(8,128)(2,1)S(1)} %get-tuple-element.45), channel_id=1, source_target_pairs={{0,64},{16,80},{32,96},{48,112},{64,0},{80,16},{96,32},{112,48},{1... | collective-permute-start | bytes 786440 | tf_op jit(solution)/shard_map/ppermute | solution.py:154
  18.1 2.7 %collective-permute-start.3 = (bf16[256,512]{1,0:T(8,128)(2,1)S(1)}, bf16[256,512]{1,0:T(8,128)(2,1)S(1)}, u32[]{:S(2)}, u32[]{:S(2)}) collective-permute-start(bf16[256,512]{1,0:T(8,128)(2,1)S(1)} %get-tuple-element.45), channel_id=1, source_target_pairs={{0,128},{16,144},{32,160},{48,176},{64,192},{80,208},{96,224},{112... | collective-permute-start | bytes 786440 | tf_op jit(solution)/shard_map/ppermute | solution.py:156
  20.8 1.5 %collective-permute-done.8 = bf16[512,256]{1,0:T(8,128)(2,1)S(1)} collective-permute-done((bf16[512,256]{1,0:T(8,128)(2,1)S(1)}, bf16[512,256]{1,0:T(8,128)(2,1)S(1)}, u32[]{:S(2)}, u32[]{:S(2)}) %collective-permute-start.8) | collective-permute-done | bytes 262176 | tf_op jit(solution)/shard_map/ppermute | solution.py:64
  22.3 3.2 %collective-permute-start.11 = (bf16[512,256]{1,0:T(8,128)(2,1)S(1)}, bf16[512,256]{1,0:T(8,128)(2,1)S(1)}, u32[]{:S(2)}, u32[]{:S(2)}) collective-permute-start(bf16[512,256]{1,0:T(8,128)(2,1)S(1)} %collective-permute-done.9), channel_id=1, source_target_pairs={{0,14},{1,15},{2,0},{3,1},{4,2},{5,3},{6,4},{7,5},{8,6},{9,7},{10,... | collective-permute-start | bytes 786440 | tf_op jit(solution)/shard_map/ppermute | solution.py:68
  25.6 2.9 %collective-permute-start.5 = (bf16[256,512]{1,0:T(8,128)(2,1)}, bf16[256,512]{1,0:T(8,128)(2,1)S(1)}, u32[]{:S(2)}, u32[]{:S(2)}) collective-permute-start(bf16[256,512]{1,0:T(8,128)(2,1)} %collective-permute-done.4), channel_id=1, source_target_pairs={{0,128},{16,144},{32,160},{48,176},{64,192},{80,208},{96,224},{112... | collective-permute-start | bytes 786440 | tf_op jit(solution)/shard_map/ppermute | solution.py:161
  28.6 0.6 collective-permute-start.6
  29.1 1.5 %collective-permute-start.7 = (bf16[2,256,512]{2,1,0:T(8,128)(2,1)S(1)}, bf16[2,256,512]{2,1,0:T(8,128)(2,1)S(1)}, u32[]{:S(2)}, u32[]{:S(2)}) collective-permute-start(bf16[2,256,512]{2,1,0:T(8,128)(2,1)S(1)} %get-tuple-element.40), channel_id=1, source_target_pairs={{0,96},{16,112},{32,0},{48,16},{64,32},{80,48},{96,64},{112,80},{1... | collective-permute-start | bytes 1572872 | tf_op jit(solution)/shard_map/ppermute | solution.py:154
  31.0 3.4 %collective-permute-start.13 = (bf16[512,256]{1,0:T(8,128)(2,1)S(1)}, bf16[512,256]{1,0:T(8,128)(2,1)S(1)}, u32[]{:S(2)}, u32[]{:S(2)}) collective-permute-start(bf16[512,256]{1,0:T(8,128)(2,1)S(1)} %collective-permute-done.11), channel_id=1, source_target_pairs={{0,14},{1,15},{2,0},{3,1},{4,2},{5,3},{6,4},{7,5},{8,6},{9,7},{10,... | collective-permute-start | bytes 786440 | tf_op jit(solution)/shard_map/ppermute | solution.py:68
  34.3 1.0 bitcast_dynamic-update-slice_fusion.3
  35.3 3.2 %collective-permute-done.12 = bf16[512,256]{1,0:T(8,128)(2,1)S(1)} collective-permute-done((bf16[512,256]{1,0:T(8,128)(2,1)S(1)}, bf16[512,256]{1,0:T(8,128)(2,1)S(1)}, u32[]{:S(2)}, u32[]{:S(2)}) %collective-permute-start.12) | collective-permute-done | bytes 262176 | tf_op jit(solution)/shard_map/ppermute | solution.py:64
  38.7 1.9 %collective-permute-done.6 = bf16[2,256,512]{2,1,0:T(8,128)(2,1)S(1)} collective-permute-done((bf16[2,256,512]{2,1,0:T(8,128)(2,1)S(1)}, bf16[2,256,512]{2,1,0:T(8,128)(2,1)S(1)}, u32[]{:S(2)}, u32[]{:S(2)}) %collective-permute-start.6) | collective-permute-done | bytes 524320 | tf_op jit(solution)/shard_map/ppermute | solution.py:154
  40.6 1.4 %collective-permute-done.7 = bf16[2,256,512]{2,1,0:T(8,128)(2,1)S(1)} collective-permute-done((bf16[2,256,512]{2,1,0:T(8,128)(2,1)S(1)}, bf16[2,256,512]{2,1,0:T(8,128)(2,1)S(1)}, u32[]{:S(2)}, u32[]{:S(2)}) %collective-permute-start.7) | collective-permute-done | bytes 524320 | tf_op jit(solution)/shard_map/ppermute | solution.py:154
  42.7 0.3 collective-permute-start.19
  44.8 1.6 %collective-permute-done.14 = bf16[512,256]{1,0:T(8,128)(2,1)S(1)} collective-permute-done((bf16[512,256]{1,0:T(8,128)(2,1)S(1)}, bf16[512,256]{1,0:T(8,128)(2,1)S(1)}, u32[]{:S(2)}, u32[]{:S(2)}) %collective-permute-start.14) | collective-permute-done | bytes 262176 | tf_op jit(solution)/shard_map/ppermute | solution.py:51
  47.7 1.2 %collective-permute-done.15 = f32[512,256]{1,0:T(8,128)S(1)} collective-permute-done((f32[512,256]{1,0:T(8,128)S(1)}, f32[512,256]{1,0:T(8,128)S(1)}, u32[]{:S(2)}, u32[]{:S(2)}) %collective-permute-start.15) | collective-permute-done | bytes 524320 | tf_op jit(solution)/shard_map/ppermute | solution.py:190
  49.1 6.5 %collective-permute-start.17 = (bf16[512,256]{1,0:T(8,128)(2,1)S(1)}, bf16[512,256]{1,0:T(8,128)(2,1)S(1)}, u32[]{:S(2)}, u32[]{:S(2)}) collective-permute-start(bf16[512,256]{1,0:T(8,128)(2,1)S(1)} %fusion.14), channel_id=1, source_target_pairs={{0,0},{1,1},{2,42},{3,43},{4,78},{5,79},{6,100},{7,101},{8,130},{9... | collective-permute-start | bytes 786440 | tf_op jit(solution)/shard_map/ppermute | solution.py:51
  55.7 3.1 %collective-permute-start.18 = (bf16[512,256]{1,0:T(8,128)(2,1)S(1)}, bf16[512,256]{1,0:T(8,128)(2,1)S(1)}, u32[]{:S(2)}, u32[]{:S(2)}) collective-permute-start(bf16[512,256]{1,0:T(8,128)(2,1)S(1)} %fusion.14), channel_id=1, source_target_pairs={{0,8},{1,9},{2,34},{3,35},{4,70},{5,71},{6,108},{7,109},{8,138},{9... | collective-permute-start | bytes 786440 | tf_op jit(solution)/shard_map/ppermute | solution.py:51
  59.6 0.7 collective-permute-done.16
  60.3 7.3 %collective-permute-done.17 = bf16[512,256]{1,0:T(8,128)(2,1)S(1)} collective-permute-done((bf16[512,256]{1,0:T(8,128)(2,1)S(1)}, bf16[512,256]{1,0:T(8,128)(2,1)S(1)}, u32[]{:S(2)}, u32[]{:S(2)}) %collective-permute-start.17) | collective-permute-done | bytes 262176 | tf_op jit(solution)/shard_map/ppermute | solution.py:51
  67.6 6.8 %collective-permute-done.18 = bf16[512,256]{1,0:T(8,128)(2,1)S(1)} collective-permute-done((bf16[512,256]{1,0:T(8,128)(2,1)S(1)}, bf16[512,256]{1,0:T(8,128)(2,1)S(1)}, u32[]{:S(2)}, u32[]{:S(2)}) %collective-permute-start.18) | collective-permute-done | bytes 262176 | tf_op jit(solution)/shard_map/ppermute | solution.py:51
  74.4 4.1 %collective-permute-start.20 = (bf16[512,256]{1,0:T(8,128)(2,1)S(1)}, bf16[512,256]{1,0:T(8,128)(2,1)S(1)}, u32[]{:S(2)}, u32[]{:S(2)}) collective-permute-start(bf16[512,256]{1,0:T(8,128)(2,1)S(1)} %collective-permute-done.17), channel_id=1, source_target_pairs={{0,2},{1,3},{2,4},{3,5},{4,6},{5,7},{6,8},{7,9},{8,10},{9,11},{10,... | collective-permute-start | bytes 786440 | tf_op jit(solution)/shard_map/ppermute | solution.py:64
  78.5 2.8 %collective-permute-start.21 = (bf16[512,256]{1,0:T(8,128)(2,1)S(1)}, bf16[512,256]{1,0:T(8,128)(2,1)S(1)}, u32[]{:S(2)}, u32[]{:S(2)}) collective-permute-start(bf16[512,256]{1,0:T(8,128)(2,1)S(1)} %collective-permute-done.17), channel_id=1, source_target_pairs={{0,14},{1,15},{2,0},{3,1},{4,2},{5,3},{6,4},{7,5},{8,6},{9,7},{10,... | collective-permute-start | bytes 786440 | tf_op jit(solution)/shard_map/ppermute | solution.py:68
  81.3 2.0 %collective-permute-start.24 = (bf16[512,256]{1,0:T(8,128)(2,1)S(1)}, bf16[512,256]{1,0:T(8,128)(2,1)S(1)}, u32[]{:S(2)}, u32[]{:S(2)}) collective-permute-start(bf16[512,256]{1,0:T(8,128)(2,1)S(1)} %collective-permute-done.18), channel_id=1, source_target_pairs={{0,14},{1,15},{2,0},{3,1},{4,2},{5,3},{6,4},{7,5},{8,6},{9,7},{10,... | collective-permute-start | bytes 786440 | tf_op jit(solution)/shard_map/ppermute | solution.py:68
  83.3 1.7 %broadcast_select_fusion = bf16[4,2,256,512]{3,2,1,0:T(8,128)(2,1)S(1)} fusion(bf16[4,2,256,512]{3,2,1,0:T(8,128)(2,1)} %collective-permute-done.19, pred[]{:T(512)S(6)} %ge.3), kind=kLoop, calls=%fused_computation | loop fusion | flops 1048576 | bytes 4194305 | tf_op jit(solution)/shard_map/jit(_where)/select_n | solution.py:198
  85.6 0.3 fusion.40
  86.2 2.0 %collective-permute-done.20 = bf16[512,256]{1,0:T(8,128)(2,1)S(1)} collective-permute-done((bf16[512,256]{1,0:T(8,128)(2,1)S(1)}, bf16[512,256]{1,0:T(8,128)(2,1)S(1)}, u32[]{:S(2)}, u32[]{:S(2)}) %collective-permute-start.20) | collective-permute-done | bytes 262176 | tf_op jit(solution)/shard_map/ppermute | solution.py:64
  88.4 0.3 fusion.25
  88.7 3.7 %collective-permute-start.26 = (bf16[512,256]{1,0:T(8,128)(2,1)S(1)}, bf16[512,256]{1,0:T(8,128)(2,1)S(1)}, u32[]{:S(2)}, u32[]{:S(2)}) collective-permute-start(bf16[512,256]{1,0:T(8,128)(2,1)S(1)} %collective-permute-done.21), channel_id=1, source_target_pairs={{0,14},{1,15},{2,0},{3,1},{4,2},{5,3},{6,4},{7,5},{8,6},{9,7},{10,... | collective-permute-start | bytes 786440 | tf_op jit(solution)/shard_map/ppermute | solution.py:68
  92.8 0.3 fusion.23
  93.1 0.6 collective-permute-done.24
  93.7 1.4 %collective-permute-start.22 = (bf16[256,256]{1,0:T(8,128)(2,1)S(1)}, bf16[256,256]{1,0:T(8,128)(2,1)S(1)}, u32[]{:S(2)}, u32[]{:S(2)}) collective-permute-start(bf16[256,256]{1,0:T(8,128)(2,1)S(1)} %broadcast_select_fusion.3), channel_id=1, source_target_pairs={{0,1},{1,0},{2,3},{3,2},{4,5},{5,4},{6,7},{7,6},{8,9},{9,8},{10,11... | collective-permute-start | bytes 393224 | tf_op jit(solution)/shard_map/ppermute | solution.py:107
  95.3 0.3 fusion.20
  95.6 2.4 %collective-permute-done.25 = bf16[512,256]{1,0:T(8,128)(2,1)S(1)} collective-permute-done((bf16[512,256]{1,0:T(8,128)(2,1)S(1)}, bf16[512,256]{1,0:T(8,128)(2,1)S(1)}, u32[]{:S(2)}, u32[]{:S(2)}) %collective-permute-start.25) | collective-permute-done | bytes 262176 | tf_op jit(solution)/shard_map/ppermute | solution.py:64
  98.8 0.3 fusion.16
  99.1 0.4 fusion.5
  99.5 0.4 fusion.2
  100.1 0.7 maximum_bitcast_fusion
  100.8 4.2 %collective-permute-done.28 = bf16[256,256]{1,0:T(8,128)(2,1)S(1)} collective-permute-done((bf16[256,256]{1,0:T(8,128)(2,1)S(1)}, bf16[256,256]{1,0:T(8,128)(2,1)S(1)}, u32[]{:S(2)}, u32[]{:S(2)}) %collective-permute-start.28) | collective-permute-done | bytes 131104 | tf_op jit(solution)/shard_map/ppermute | solution.py:131
  105.1 0.7 maximum_bitcast_fusion.1
  (76 shorter events, 8.0 us)
Async XLA Ops:
  0.6 15.9 %copy-start = (bf16[2,1,1,256,1,1,256]{6,3,5,4,2,1,0:T(8,128)(2,1)S(1)}, bf16[2,1,1,256,1,1,256]{6,3,5,4,2,1,0:T(8,128)(2,1)}, u32[]{:S(2)}) copy-start(bf16[2,1,1,256,1,1,256]{6,3,5,4,2,1,0:T(8,128)(2,1)} %param.5) | copy-start | bytes 786436
  1.7 6.4 %collective-permute-start = (bf16[256,256]{1,0:T(8,128)(2,1)S(1)}, bf16[256,256]{1,0:T(8,128)(2,1)S(1)}, u32[]{:S(2)}, u32[]{:S(2)}) collective-permute-start(bf16[256,256]{1,0:T(8,128)(2,1)S(1)} %get-tuple-element.46), channel_id=1, source_target_pairs={{0,0},{1,16},{2,2},{3,18},{4,4},{5,20},{6,6},{7,22},{8,8},{9,24},{... | collective-permute-start | bytes 393224 | tf_op jit(solution)/shard_map/ppermute | solution.py:51
  2.4 7.9 %collective-permute-start.1 = (bf16[256,256]{1,0:T(8,128)(2,1)S(1)}, bf16[256,256]{1,0:T(8,128)(2,1)S(1)}, u32[]{:S(2)}, u32[]{:S(2)}) collective-permute-start(bf16[256,256]{1,0:T(8,128)(2,1)S(1)} %get-tuple-element.47), channel_id=1, source_target_pairs={{0,1},{1,17},{2,3},{3,19},{4,5},{5,21},{6,7},{7,23},{8,9},{9,25},{... | collective-permute-start | bytes 393224 | tf_op jit(solution)/shard_map/ppermute | solution.py:51
  8.1 8.4 %collective-permute-start.2 = (bf16[256,256]{1,0:T(8,128)(2,1)S(1)}, bf16[256,256]{1,0:T(8,128)(2,1)S(1)}, u32[]{:S(2)}, u32[]{:S(2)}) collective-permute-start(bf16[256,256]{1,0:T(8,128)(2,1)S(1)} %select_bitcast_fusion.7), channel_id=1, source_target_pairs={{0,1},{1,0},{2,3},{3,2},{4,5},{5,4},{6,7},{7,6},{8,9},{9,8},{10,11... | collective-permute-start | bytes 393224 | tf_op jit(solution)/shard_map/ppermute | solution.py:131
  10.5 11.8 %collective-permute-start.8 = (bf16[512,256]{1,0:T(8,128)(2,1)S(1)}, bf16[512,256]{1,0:T(8,128)(2,1)S(1)}, u32[]{:S(2)}, u32[]{:S(2)}) collective-permute-start(bf16[512,256]{1,0:T(8,128)(2,1)S(1)} %bitcast_select_fusion), channel_id=1, source_target_pairs={{0,2},{1,3},{2,4},{3,5},{4,6},{5,7},{6,8},{7,9},{8,10},{9,11},{10,... | collective-permute-start | bytes 786440 | tf_op jit(solution)/shard_map/ppermute | solution.py:64
  12.5 9.8 %collective-permute-start.9 = (bf16[512,256]{1,0:T(8,128)(2,1)S(1)}, bf16[512,256]{1,0:T(8,128)(2,1)S(1)}, u32[]{:S(2)}, u32[]{:S(2)}) collective-permute-start(bf16[512,256]{1,0:T(8,128)(2,1)S(1)} %bitcast_select_fusion), channel_id=1, source_target_pairs={{0,14},{1,15},{2,0},{3,1},{4,2},{5,3},{6,4},{7,5},{8,6},{9,7},{10,... | collective-permute-start | bytes 786440 | tf_op jit(solution)/shard_map/ppermute | solution.py:68
  16.6 9.0 %collective-permute-start.4 = (bf16[256,512]{1,0:T(8,128)(2,1)S(1)}, bf16[256,512]{1,0:T(8,128)(2,1)}, u32[]{:S(2)}, u32[]{:S(2)}) collective-permute-start(bf16[256,512]{1,0:T(8,128)(2,1)S(1)} %get-tuple-element.45), channel_id=1, source_target_pairs={{0,64},{16,80},{32,96},{48,112},{64,0},{80,16},{96,32},{112,48},{1... | collective-permute-start | bytes 786440 | tf_op jit(solution)/shard_map/ppermute | solution.py:154
  18.1 10.4 %collective-permute-start.3 = (bf16[256,512]{1,0:T(8,128)(2,1)S(1)}, bf16[256,512]{1,0:T(8,128)(2,1)S(1)}, u32[]{:S(2)}, u32[]{:S(2)}) collective-permute-start(bf16[256,512]{1,0:T(8,128)(2,1)S(1)} %get-tuple-element.45), channel_id=1, source_target_pairs={{0,128},{16,144},{32,160},{48,176},{64,192},{80,208},{96,224},{112... | collective-permute-start | bytes 786440 | tf_op jit(solution)/shard_map/ppermute | solution.py:156
  22.3 8.6 %collective-permute-start.10 = (bf16[512,256]{1,0:T(8,128)(2,1)S(1)}, bf16[512,256]{1,0:T(8,128)(2,1)S(1)}, u32[]{:S(2)}, u32[]{:S(2)}) collective-permute-start(bf16[512,256]{1,0:T(8,128)(2,1)S(1)} %collective-permute-done.8), channel_id=1, source_target_pairs={{0,2},{1,3},{2,4},{3,5},{4,6},{5,7},{6,8},{7,9},{8,10},{9,11},{10,... | collective-permute-start | bytes 786440 | tf_op jit(solution)/shard_map/ppermute | solution.py:64
  22.3 8.7 %collective-permute-start.11 = (bf16[512,256]{1,0:T(8,128)(2,1)S(1)}, bf16[512,256]{1,0:T(8,128)(2,1)S(1)}, u32[]{:S(2)}, u32[]{:S(2)}) collective-permute-start(bf16[512,256]{1,0:T(8,128)(2,1)S(1)} %collective-permute-done.9), channel_id=1, source_target_pairs={{0,14},{1,15},{2,0},{3,1},{4,2},{5,3},{6,4},{7,5},{8,6},{9,7},{10,... | collective-permute-start | bytes 786440 | tf_op jit(solution)/shard_map/ppermute | solution.py:68
  25.6 9.7 %collective-permute-start.5 = (bf16[256,512]{1,0:T(8,128)(2,1)}, bf16[256,512]{1,0:T(8,128)(2,1)S(1)}, u32[]{:S(2)}, u32[]{:S(2)}) collective-permute-start(bf16[256,512]{1,0:T(8,128)(2,1)} %collective-permute-done.4), channel_id=1, source_target_pairs={{0,128},{16,144},{32,160},{48,176},{64,192},{80,208},{96,224},{112... | collective-permute-start | bytes 786440 | tf_op jit(solution)/shard_map/ppermute | solution.py:161
  28.6 12.0 %collective-permute-start.6 = (bf16[2,256,512]{2,1,0:T(8,128)(2,1)S(1)}, bf16[2,256,512]{2,1,0:T(8,128)(2,1)S(1)}, u32[]{:S(2)}, u32[]{:S(2)}) collective-permute-start(bf16[2,256,512]{2,1,0:T(8,128)(2,1)S(1)} %get-tuple-element.40), channel_id=1, source_target_pairs={{0,32},{16,48},{32,64},{48,80},{64,96},{80,112},{96,0},{112,16},{1... | collective-permute-start | bytes 1572872 | tf_op jit(solution)/shard_map/ppermute | solution.py:154
  29.1 12.9 %collective-permute-start.7 = (bf16[2,256,512]{2,1,0:T(8,128)(2,1)S(1)}, bf16[2,256,512]{2,1,0:T(8,128)(2,1)S(1)}, u32[]{:S(2)}, u32[]{:S(2)}) collective-permute-start(bf16[2,256,512]{2,1,0:T(8,128)(2,1)S(1)} %get-tuple-element.40), channel_id=1, source_target_pairs={{0,96},{16,112},{32,0},{48,16},{64,32},{80,48},{96,64},{112,80},{1... | collective-permute-start | bytes 1572872 | tf_op jit(solution)/shard_map/ppermute | solution.py:154
  30.9 7.7 %collective-permute-start.12 = (bf16[512,256]{1,0:T(8,128)(2,1)S(1)}, bf16[512,256]{1,0:T(8,128)(2,1)S(1)}, u32[]{:S(2)}, u32[]{:S(2)}) collective-permute-start(bf16[512,256]{1,0:T(8,128)(2,1)S(1)} %collective-permute-done.10), channel_id=1, source_target_pairs={{0,2},{1,3},{2,4},{3,5},{4,6},{5,7},{6,8},{7,9},{8,10},{9,11},{10,... | collective-permute-start | bytes 786440 | tf_op jit(solution)/shard_map/ppermute | solution.py:64
  31.0 7.6 %collective-permute-start.13 = (bf16[512,256]{1,0:T(8,128)(2,1)S(1)}, bf16[512,256]{1,0:T(8,128)(2,1)S(1)}, u32[]{:S(2)}, u32[]{:S(2)}) collective-permute-start(bf16[512,256]{1,0:T(8,128)(2,1)S(1)} %collective-permute-done.11), channel_id=1, source_target_pairs={{0,14},{1,15},{2,0},{3,1},{4,2},{5,3},{6,4},{7,5},{8,6},{9,7},{10,... | collective-permute-start | bytes 786440 | tf_op jit(solution)/shard_map/ppermute | solution.py:68
  38.6 7.8 %collective-permute-start.14 = (bf16[512,256]{1,0:T(8,128)(2,1)S(1)}, bf16[512,256]{1,0:T(8,128)(2,1)S(1)}, u32[]{:S(2)}, u32[]{:S(2)}) collective-permute-start(bf16[512,256]{1,0:T(8,128)(2,1)S(1)} %broadcast_select_fusion.1), channel_id=1, source_target_pairs={{0,2},{1,3},{2,4},{3,5},{4,6},{5,7},{6,8},{7,9},{8,10},{9,11},{10,... | collective-permute-start | bytes 786440 | tf_op jit(solution)/shard_map/ppermute | solution.py:51
  42.7 31.7 %collective-permute-start.19 = (bf16[4,2,256,512]{3,2,1,0:T(8,128)(2,1)S(1)}, bf16[4,2,256,512]{3,2,1,0:T(8,128)(2,1)}, u32[]{:S(2)}, u32[]{:S(2)}) collective-permute-start(bf16[4,2,256,512]{3,2,1,0:T(8,128)(2,1)S(1)} %bitcast_dynamic-update-slice_fusion), channel_id=1, source_target_pairs={{0,16},{16,0},{32,48},{48,32},{64,80},{80,64},{96,112},{112,96},{1... | collective-permute-start | bytes 6291464 | tf_op jit(solution)/shard_map/ppermute | solution.py:196
  46.8 2.0 %collective-permute-start.15 = (f32[512,256]{1,0:T(8,128)S(1)}, f32[512,256]{1,0:T(8,128)S(1)}, u32[]{:S(2)}, u32[]{:S(2)}) collective-permute-start(f32[512,256]{1,0:T(8,128)S(1)} %fusion.7), channel_id=1, source_target_pairs={{0,16},{16,0},{32,48},{48,32},{64,80},{80,64},{96,112},{112,96},{1... | collective-permute-start | bytes 1572872 | tf_op jit(solution)/shard_map/ppermute | solution.py:190
  47.6 11.3 %copy-start.1 = (bf16[2,1,1,256,1,1,256]{6,3,5,4,2,1,0:T(8,128)(2,1)S(1)}, bf16[2,1,1,256,1,1,256]{6,3,5,4,2,1,0:T(8,128)(2,1)}, u32[]{:S(2)}) copy-start(bf16[2,1,1,256,1,1,256]{6,3,5,4,2,1,0:T(8,128)(2,1)} %param.6) | copy-start | bytes 786436
  49.1 18.4 %collective-permute-start.17 = (bf16[512,256]{1,0:T(8,128)(2,1)S(1)}, bf16[512,256]{1,0:T(8,128)(2,1)S(1)}, u32[]{:S(2)}, u32[]{:S(2)}) collective-permute-start(bf16[512,256]{1,0:T(8,128)(2,1)S(1)} %fusion.14), channel_id=1, source_target_pairs={{0,0},{1,1},{2,42},{3,43},{4,78},{5,79},{6,100},{7,101},{8,130},{9... | collective-permute-start | bytes 786440 | tf_op jit(solution)/shard_map/ppermute | solution.py:51
  55.7 18.7 %collective-permute-start.18 = (bf16[512,256]{1,0:T(8,128)(2,1)S(1)}, bf16[512,256]{1,0:T(8,128)(2,1)S(1)}, u32[]{:S(2)}, u32[]{:S(2)}) collective-permute-start(bf16[512,256]{1,0:T(8,128)(2,1)S(1)} %fusion.14), channel_id=1, source_target_pairs={{0,8},{1,9},{2,34},{3,35},{4,70},{5,71},{6,108},{7,109},{8,138},{9... | collective-permute-start | bytes 786440 | tf_op jit(solution)/shard_map/ppermute | solution.py:51
  58.8 1.4 %collective-permute-start.16 = (bf16[256,256]{1,0:T(8,128)(2,1)S(1)}, bf16[256,256]{1,0:T(8,128)(2,1)S(1)}, u32[]{:S(2)}, u32[]{:S(2)}) collective-permute-start(bf16[256,256]{1,0:T(8,128)(2,1)S(1)} %slice.215), channel_id=1, source_target_pairs={{0,16},{16,0},{32,48},{48,32},{64,80},{80,64},{96,112},{112,96},{1... | collective-permute-start | bytes 393224 | tf_op jit(solution)/shard_map/ppermute | solution.py:199
  74.4 13.7 %collective-permute-start.20 = (bf16[512,256]{1,0:T(8,128)(2,1)S(1)}, bf16[512,256]{1,0:T(8,128)(2,1)S(1)}, u32[]{:S(2)}, u32[]{:S(2)}) collective-permute-start(bf16[512,256]{1,0:T(8,128)(2,1)S(1)} %collective-permute-done.17), channel_id=1, source_target_pairs={{0,2},{1,3},{2,4},{3,5},{4,6},{5,7},{6,8},{7,9},{8,10},{9,11},{10,... | collective-permute-start | bytes 786440 | tf_op jit(solution)/shard_map/ppermute | solution.py:64
  78.5 9.7 %collective-permute-start.21 = (bf16[512,256]{1,0:T(8,128)(2,1)S(1)}, bf16[512,256]{1,0:T(8,128)(2,1)S(1)}, u32[]{:S(2)}, u32[]{:S(2)}) collective-permute-start(bf16[512,256]{1,0:T(8,128)(2,1)S(1)} %collective-permute-done.17), channel_id=1, source_target_pairs={{0,14},{1,15},{2,0},{3,1},{4,2},{5,3},{6,4},{7,5},{8,6},{9,7},{10,... | collective-permute-start | bytes 786440 | tf_op jit(solution)/shard_map/ppermute | solution.py:68
  81.3 12.4 %collective-permute-start.24 = (bf16[512,256]{1,0:T(8,128)(2,1)S(1)}, bf16[512,256]{1,0:T(8,128)(2,1)S(1)}, u32[]{:S(2)}, u32[]{:S(2)}) collective-permute-start(bf16[512,256]{1,0:T(8,128)(2,1)S(1)} %collective-permute-done.18), channel_id=1, source_target_pairs={{0,14},{1,15},{2,0},{3,1},{4,2},{5,3},{6,4},{7,5},{8,6},{9,7},{10,... | collective-permute-start | bytes 786440 | tf_op jit(solution)/shard_map/ppermute | solution.py:68
  83.3 15.8 %collective-permute-start.23 = (bf16[512,256]{1,0:T(8,128)(2,1)S(1)}, bf16[512,256]{1,0:T(8,128)(2,1)S(1)}, u32[]{:S(2)}, u32[]{:S(2)}) collective-permute-start(bf16[512,256]{1,0:T(8,128)(2,1)S(1)} %collective-permute-done.18), channel_id=1, source_target_pairs={{0,2},{1,3},{2,4},{3,5},{4,6},{5,7},{6,8},{7,9},{8,10},{9,11},{10,... | collective-permute-start | bytes 786440 | tf_op jit(solution)/shard_map/ppermute | solution.py:64
  88.1 9.8 %collective-permute-start.25 = (bf16[512,256]{1,0:T(8,128)(2,1)S(1)}, bf16[512,256]{1,0:T(8,128)(2,1)S(1)}, u32[]{:S(2)}, u32[]{:S(2)}) collective-permute-start(bf16[512,256]{1,0:T(8,128)(2,1)S(1)} %collective-permute-done.20), channel_id=1, source_target_pairs={{0,2},{1,3},{2,4},{3,5},{4,6},{5,7},{6,8},{7,9},{8,10},{9,11},{10,... | collective-permute-start | bytes 786440 | tf_op jit(solution)/shard_map/ppermute | solution.py:64
  88.7 9.8 %collective-permute-start.26 = (bf16[512,256]{1,0:T(8,128)(2,1)S(1)}, bf16[512,256]{1,0:T(8,128)(2,1)S(1)}, u32[]{:S(2)}, u32[]{:S(2)}) collective-permute-start(bf16[512,256]{1,0:T(8,128)(2,1)S(1)} %collective-permute-done.21), channel_id=1, source_target_pairs={{0,14},{1,15},{2,0},{3,1},{4,2},{5,3},{6,4},{7,5},{8,6},{9,7},{10,... | collective-permute-start | bytes 786440 | tf_op jit(solution)/shard_map/ppermute | solution.py:68
  92.4 7.5 %collective-permute-start.27 = (bf16[256,256]{1,0:T(8,128)(2,1)S(1)}, bf16[256,256]{1,0:T(8,128)(2,1)S(1)}, u32[]{:S(2)}, u32[]{:S(2)}) collective-permute-start(bf16[256,256]{1,0:T(8,128)(2,1)S(1)} %select_bitcast_fusion.2), channel_id=1, source_target_pairs={{0,1},{1,0},{2,3},{3,2},{4,5},{5,4},{6,7},{7,6},{8,9},{9,8},{10,11... | collective-permute-start | bytes 393224 | tf_op jit(solution)/shard_map/ppermute | solution.py:107
  93.7 6.4 %collective-permute-start.22 = (bf16[256,256]{1,0:T(8,128)(2,1)S(1)}, bf16[256,256]{1,0:T(8,128)(2,1)S(1)}, u32[]{:S(2)}, u32[]{:S(2)}) collective-permute-start(bf16[256,256]{1,0:T(8,128)(2,1)S(1)} %broadcast_select_fusion.3), channel_id=1, source_target_pairs={{0,1},{1,0},{2,3},{3,2},{4,5},{5,4},{6,7},{7,6},{8,9},{9,8},{10,11... | collective-permute-start | bytes 393224 | tf_op jit(solution)/shard_map/ppermute | solution.py:107
  100.0 5.1 %collective-permute-start.28 = (bf16[256,256]{1,0:T(8,128)(2,1)S(1)}, bf16[256,256]{1,0:T(8,128)(2,1)S(1)}, u32[]{:S(2)}, u32[]{:S(2)}) collective-permute-start(bf16[256,256]{1,0:T(8,128)(2,1)S(1)} %subtract_convert_fusion), channel_id=1, source_target_pairs={{0,1},{1,0},{2,3},{3,2},{4,5},{5,4},{6,7},{7,6},{8,9},{9,8},{10,11... | collective-permute-start | bytes 393224 | tf_op jit(solution)/shard_map/ppermute | solution.py:131

commit v5 on v4

--- a/solution.py
+++ b/solution.py
@@ -33,14 +33,14 @@
 
 
 LAND = (
-    (0, 5, 7, 2, 1, 4, 6, 7),
-    (6, 3, 1, 0, 6, 7, 1, 0),
-    (7, 2, 0, 1, 3, 2, 0, 1),
-    (5, 4, 2, 7, 4, 5, 7, 2),
-    (2, 7, 4, 5, 7, 6, 5, 4),
-    (1, 0, 6, 3, 5, 0, 2, 3),
-    (4, 1, 3, 6, 0, 1, 3, 6),
-    (3, 6, 5, 4, 2, 3, 4, 5),
+    (1, 4, 7, 6, 1, 0, 3, 2),
+    (7, 6, 1, 4, 2, 3, 0, 1),
+    (6, 5, 0, 7, 3, 1, 2, 0),
+    (4, 3, 6, 1, 4, 6, 1, 7),
+    (3, 1, 2, 0, 7, 5, 6, 4),
+    (0, 2, 3, 5, 6, 7, 5, 3),
+    (5, 7, 4, 2, 5, 4, 7, 6),
+    (2, 0, 5, 3, 0, 2, 4, 5),
 )
 LANDED = [
     sum(p << (3 * LAND[p][col]) for p in range(NZ)) for col in range(NZ)

time: 106 us -> 102 us (0.962)
  starting transfers between devices: 52.2 us -> 47.7 us
    ppermute x5, starting transfers between devices: 13.3 us -> 9.55 us  [move(): return lax.ppermute(block, ('prow', 'pcol'), pairs)]
    ppermute x2, starting transfers between devices: 2.34 us -> 4.69 us  [swap(): return lax.ppermute(block, 'pcol', SWAP)]
    ppermute x5, waiting for transfers between devices: 15.7 us -> 17.9 us  [move(): return lax.ppermute(block, ('prow', 'pcol'), pairs)]
    ppermute x6, starting transfers between devices: 6.16 us -> 4.07 us  [up(): return lax.ppermute(block, 'pcol', UP)]
    ppermute x2, waiting for transfers between devices: 4.18 us -> 2.19 us  [swap(): return lax.ppermute(block, 'pcol', SWAP)]
    ppermute x6, starting transfers between devices: 19.2 us -> 17.2 us  [down(): return lax.ppermute(block, 'pcol', DOWN)]
  transfers between devices with their start and end apart: 29 -> 29, of which waited for: 14 -> 13; matrix products, arithmetic and copies ran while one was open for 14% -> 15% of each run, Pallas kernels for 0% -> 0%
where the time goes in v5:
time: 102 us; the launch traced here: 101 us
  starting transfers between devices  47.7 us (47%)
  waiting for transfers between devices  34.5 us (34%)
  matrix products  8.17 us (8%)
  other arithmetic  6.68 us (7%)
  local copies, waits for them, and re-layouts  2.34 us (2%)
  between operations  1.74 us (2%)
    ppermute x5, waiting for transfers between devices, move(): return lax.ppermute(block, ('prow', 'pcol'), pairs)  17.9 us
    ppermute x6, starting transfers between devices, down(): return lax.ppermute(block, 'pcol', DOWN)  17.2 us
    ppermute x5, starting transfers between devices, move(): return lax.ppermute(block, ('prow', 'pcol'), pairs)  9.55 us
    ppermute x6, waiting for transfers between devices, up(): return lax.ppermute(block, 'pcol', UP)  9.24 us
    ppermute x2, starting transfers between devices, swap(): return lax.ppermute(block, 'pcol', SWAP)  4.69 us
    dot_general x16, matrix products, add_inner(): lax.dot_general(u_rows(panel, owner), rows, (((0,), (0,)), ((), ())), pre...  4.52 us
    ppermute x6, starting transfers between devices, up(): return lax.ppermute(block, 'pcol', UP)  4.07 us
    dot_general x16, matrix products, add_product(): jnp.dot(block, cols, preferred_element_type=jnp.float32)  3.65 us
  transfers between devices with their start and end apart: 29, of which 13 were waited for; matrix products, arithmetic and copies ran while one was open for 15% of the time, Pallas kernels for 0%

profile of v5, /device:TPU:6, one launch (start us, length us, event | category | flops | bytes accessed | tf_op | source)
XLA Modules:
  0.0 101.2 jit_solution(1549292529916280085)
XLA Ops:
  0.7 1.0 %select_bitcast_fusion.6 = (bf16[256,256]{1,0:T(8,128)(2,1)S(1)}, bf16[256,256]{1,0:T(8,128)(2,1)S(1)}) fusion(pred[]{:T(512)S(6)} %eq.185, bf16[2,1,1,256,1,1,256]{6,3,5,4,2,1,0:T(8,128)(2,1)} %param.4), kind=kLoop, calls=%fused_computation.144 | loop fusion | flops 131072 | bytes 524289 | tf_op jit(solution)/shard_map/jit(_where)/select_n | solution.py:134
  1.7 0.7 collective-permute-start
  2.4 2.9 %collective-permute-start.1 = (bf16[256,256]{1,0:T(8,128)(2,1)S(1)}, bf16[256,256]{1,0:T(8,128)(2,1)S(1)}, u32[]{:S(2)}, u32[]{:S(2)}) collective-permute-start(bf16[256,256]{1,0:T(8,128)(2,1)S(1)} %get-tuple-element.47), channel_id=1, source_target_pairs={{0,1},{1,17},{2,3},{3,19},{4,5},{5,21},{6,7},{7,23},{8,9},{9,25},{... | collective-permute-start | bytes 393224 | tf_op jit(solution)/shard_map/ppermute | solution.py:51
  5.3 0.8 dynamic_slice.75
  6.1 0.9 compare_reduce_fusion
  7.1 1.0 select_bitcast_fusion.7
  8.1 2.2 %collective-permute-start.2 = (bf16[256,256]{1,0:T(8,128)(2,1)S(1)}, bf16[256,256]{1,0:T(8,128)(2,1)S(1)}, u32[]{:S(2)}, u32[]{:S(2)}) collective-permute-start(bf16[256,256]{1,0:T(8,128)(2,1)S(1)} %select_bitcast_fusion.7), channel_id=1, source_target_pairs={{0,1},{1,0},{2,3},{3,2},{4,5},{5,4},{6,7},{7,6},{8,9},{9,8},{10,11... | collective-permute-start | bytes 393224 | tf_op jit(solution)/shard_map/ppermute | solution.py:131
  10.5 2.0 %collective-permute-start.8 = (bf16[512,256]{1,0:T(8,128)(2,1)S(1)}, bf16[512,256]{1,0:T(8,128)(2,1)S(1)}, u32[]{:S(2)}, u32[]{:S(2)}) collective-permute-start(bf16[512,256]{1,0:T(8,128)(2,1)S(1)} %bitcast_select_fusion), channel_id=1, source_target_pairs={{0,2},{1,3},{2,4},{3,5},{4,6},{5,7},{6,8},{7,9},{8,10},{9,11},{10,... | collective-permute-start | bytes 786440 | tf_op jit(solution)/shard_map/ppermute | solution.py:64
  12.5 4.0 %collective-permute-start.9 = (bf16[512,256]{1,0:T(8,128)(2,1)S(1)}, bf16[512,256]{1,0:T(8,128)(2,1)S(1)}, u32[]{:S(2)}, u32[]{:S(2)}) collective-permute-start(bf16[512,256]{1,0:T(8,128)(2,1)S(1)} %bitcast_select_fusion), channel_id=1, source_target_pairs={{0,14},{1,15},{2,0},{3,1},{4,2},{5,3},{6,4},{7,5},{8,6},{9,7},{10,... | collective-permute-start | bytes 786440 | tf_op jit(solution)/shard_map/ppermute | solution.py:68
  16.6 1.5 %collective-permute-start.4 = (bf16[256,512]{1,0:T(8,128)(2,1)S(1)}, bf16[256,512]{1,0:T(8,128)(2,1)}, u32[]{:S(2)}, u32[]{:S(2)}) collective-permute-start(bf16[256,512]{1,0:T(8,128)(2,1)S(1)} %get-tuple-element.45), channel_id=1, source_target_pairs={{0,64},{16,80},{32,96},{48,112},{64,0},{80,16},{96,32},{112,48},{1... | collective-permute-start | bytes 786440 | tf_op jit(solution)/shard_map/ppermute | solution.py:154
  18.1 2.7 %collective-permute-start.3 = (bf16[256,512]{1,0:T(8,128)(2,1)S(1)}, bf16[256,512]{1,0:T(8,128)(2,1)S(1)}, u32[]{:S(2)}, u32[]{:S(2)}) collective-permute-start(bf16[256,512]{1,0:T(8,128)(2,1)S(1)} %get-tuple-element.45), channel_id=1, source_target_pairs={{0,128},{16,144},{32,160},{48,176},{64,192},{80,208},{96,224},{112... | collective-permute-start | bytes 786440 | tf_op jit(solution)/shard_map/ppermute | solution.py:156
  20.8 1.5 %collective-permute-done.8 = bf16[512,256]{1,0:T(8,128)(2,1)S(1)} collective-permute-done((bf16[512,256]{1,0:T(8,128)(2,1)S(1)}, bf16[512,256]{1,0:T(8,128)(2,1)S(1)}, u32[]{:S(2)}, u32[]{:S(2)}) %collective-permute-start.8) | collective-permute-done | bytes 262176 | tf_op jit(solution)/shard_map/ppermute | solution.py:64
  22.3 3.2 %collective-permute-start.11 = (bf16[512,256]{1,0:T(8,128)(2,1)S(1)}, bf16[512,256]{1,0:T(8,128)(2,1)S(1)}, u32[]{:S(2)}, u32[]{:S(2)}) collective-permute-start(bf16[512,256]{1,0:T(8,128)(2,1)S(1)} %collective-permute-done.9), channel_id=1, source_target_pairs={{0,14},{1,15},{2,0},{3,1},{4,2},{5,3},{6,4},{7,5},{8,6},{9,7},{10,... | collective-permute-start | bytes 786440 | tf_op jit(solution)/shard_map/ppermute | solution.py:68
  25.6 2.9 %collective-permute-start.5 = (bf16[256,512]{1,0:T(8,128)(2,1)}, bf16[256,512]{1,0:T(8,128)(2,1)S(1)}, u32[]{:S(2)}, u32[]{:S(2)}) collective-permute-start(bf16[256,512]{1,0:T(8,128)(2,1)} %collective-permute-done.4), channel_id=1, source_target_pairs={{0,128},{16,144},{32,160},{48,176},{64,192},{80,208},{96,224},{112... | collective-permute-start | bytes 786440 | tf_op jit(solution)/shard_map/ppermute | solution.py:161
  28.6 0.6 collective-permute-start.6
  29.1 1.5 %collective-permute-start.7 = (bf16[2,256,512]{2,1,0:T(8,128)(2,1)S(1)}, bf16[2,256,512]{2,1,0:T(8,128)(2,1)S(1)}, u32[]{:S(2)}, u32[]{:S(2)}) collective-permute-start(bf16[2,256,512]{2,1,0:T(8,128)(2,1)S(1)} %get-tuple-element.40), channel_id=1, source_target_pairs={{0,96},{16,112},{32,0},{48,16},{64,32},{80,48},{96,64},{112,80},{1... | collective-permute-start | bytes 1572872 | tf_op jit(solution)/shard_map/ppermute | solution.py:154
  31.0 3.4 %collective-permute-start.13 = (bf16[512,256]{1,0:T(8,128)(2,1)S(1)}, bf16[512,256]{1,0:T(8,128)(2,1)S(1)}, u32[]{:S(2)}, u32[]{:S(2)}) collective-permute-start(bf16[512,256]{1,0:T(8,128)(2,1)S(1)} %collective-permute-done.11), channel_id=1, source_target_pairs={{0,14},{1,15},{2,0},{3,1},{4,2},{5,3},{6,4},{7,5},{8,6},{9,7},{10,... | collective-permute-start | bytes 786440 | tf_op jit(solution)/shard_map/ppermute | solution.py:68
  34.3 1.0 bitcast_dynamic-update-slice_fusion.3
  35.3 3.2 %collective-permute-done.12 = bf16[512,256]{1,0:T(8,128)(2,1)S(1)} collective-permute-done((bf16[512,256]{1,0:T(8,128)(2,1)S(1)}, bf16[512,256]{1,0:T(8,128)(2,1)S(1)}, u32[]{:S(2)}, u32[]{:S(2)}) %collective-permute-start.12) | collective-permute-done | bytes 262176 | tf_op jit(solution)/shard_map/ppermute | solution.py:64
  38.7 1.9 %collective-permute-done.6 = bf16[2,256,512]{2,1,0:T(8,128)(2,1)S(1)} collective-permute-done((bf16[2,256,512]{2,1,0:T(8,128)(2,1)S(1)}, bf16[2,256,512]{2,1,0:T(8,128)(2,1)S(1)}, u32[]{:S(2)}, u32[]{:S(2)}) %collective-permute-start.6) | collective-permute-done | bytes 524320 | tf_op jit(solution)/shard_map/ppermute | solution.py:154
  40.6 1.4 %collective-permute-done.7 = bf16[2,256,512]{2,1,0:T(8,128)(2,1)S(1)} collective-permute-done((bf16[2,256,512]{2,1,0:T(8,128)(2,1)S(1)}, bf16[2,256,512]{2,1,0:T(8,128)(2,1)S(1)}, u32[]{:S(2)}, u32[]{:S(2)}) %collective-permute-start.7) | collective-permute-done | bytes 524320 | tf_op jit(solution)/shard_map/ppermute | solution.py:154
  42.7 0.3 collective-permute-start.19
  44.8 1.6 %collective-permute-done.14 = bf16[512,256]{1,0:T(8,128)(2,1)S(1)} collective-permute-done((bf16[512,256]{1,0:T(8,128)(2,1)S(1)}, bf16[512,256]{1,0:T(8,128)(2,1)S(1)}, u32[]{:S(2)}, u32[]{:S(2)}) %collective-permute-start.14) | collective-permute-done | bytes 262176 | tf_op jit(solution)/shard_map/ppermute | solution.py:51
  47.7 1.2 %collective-permute-done.15 = f32[512,256]{1,0:T(8,128)S(1)} collective-permute-done((f32[512,256]{1,0:T(8,128)S(1)}, f32[512,256]{1,0:T(8,128)S(1)}, u32[]{:S(2)}, u32[]{:S(2)}) %collective-permute-start.15) | collective-permute-done | bytes 524320 | tf_op jit(solution)/shard_map/ppermute | solution.py:190
  49.1 5.9 %collective-permute-start.17 = (bf16[512,256]{1,0:T(8,128)(2,1)S(1)}, bf16[512,256]{1,0:T(8,128)(2,1)S(1)}, u32[]{:S(2)}, u32[]{:S(2)}) collective-permute-start(bf16[512,256]{1,0:T(8,128)(2,1)S(1)} %fusion.14), channel_id=1, source_target_pairs={{0,2},{1,3},{2,40},{3,41},{4,78},{5,79},{6,108},{7,109},{8,130},{9... | collective-permute-start | bytes 786440 | tf_op jit(solution)/shard_map/ppermute | solution.py:51
  55.8 0.7 collective-permute-done.16
  56.5 10.7 %collective-permute-done.17 = bf16[512,256]{1,0:T(8,128)(2,1)S(1)} collective-permute-done((bf16[512,256]{1,0:T(8,128)(2,1)S(1)}, bf16[512,256]{1,0:T(8,128)(2,1)S(1)}, u32[]{:S(2)}, u32[]{:S(2)}) %collective-permute-start.17) | collective-permute-done | bytes 262176 | tf_op jit(solution)/shard_map/ppermute | solution.py:51
  67.2 5.6 %collective-permute-done.18 = bf16[512,256]{1,0:T(8,128)(2,1)S(1)} collective-permute-done((bf16[512,256]{1,0:T(8,128)(2,1)S(1)}, bf16[512,256]{1,0:T(8,128)(2,1)S(1)}, u32[]{:S(2)}, u32[]{:S(2)}) %collective-permute-start.18) | collective-permute-done | bytes 262176 | tf_op jit(solution)/shard_map/ppermute | solution.py:51
  72.8 3.2 %collective-permute-start.21 = (bf16[512,256]{1,0:T(8,128)(2,1)S(1)}, bf16[512,256]{1,0:T(8,128)(2,1)S(1)}, u32[]{:S(2)}, u32[]{:S(2)}) collective-permute-start(bf16[512,256]{1,0:T(8,128)(2,1)S(1)} %collective-permute-done.17), channel_id=1, source_target_pairs={{0,14},{1,15},{2,0},{3,1},{4,2},{5,3},{6,4},{7,5},{8,6},{9,7},{10,... | collective-permute-start | bytes 786440 | tf_op jit(solution)/shard_map/ppermute | solution.py:68
  76.1 2.0 %collective-permute-start.23 = (bf16[512,256]{1,0:T(8,128)(2,1)S(1)}, bf16[512,256]{1,0:T(8,128)(2,1)S(1)}, u32[]{:S(2)}, u32[]{:S(2)}) collective-permute-start(bf16[512,256]{1,0:T(8,128)(2,1)S(1)} %collective-permute-done.18), channel_id=1, source_target_pairs={{0,2},{1,3},{2,4},{3,5},{4,6},{5,7},{6,8},{7,9},{8,10},{9,11},{10,... | collective-permute-start | bytes 786440 | tf_op jit(solution)/shard_map/ppermute | solution.py:64
  78.1 1.7 %broadcast_select_fusion = bf16[4,2,256,512]{3,2,1,0:T(8,128)(2,1)S(1)} fusion(bf16[4,2,256,512]{3,2,1,0:T(8,128)(2,1)} %collective-permute-done.19, pred[]{:T(512)S(6)} %ge.3), kind=kLoop, calls=%fused_computation | loop fusion | flops 1048576 | bytes 4194305 | tf_op jit(solution)/shard_map/jit(_where)/select_n | solution.py:198
  79.8 0.3 fusion.44
  80.1 0.3 fusion.42
  80.4 0.3 fusion.40
  80.9 2.4 %collective-permute-done.20 = bf16[512,256]{1,0:T(8,128)(2,1)S(1)} collective-permute-done((bf16[512,256]{1,0:T(8,128)(2,1)S(1)}, bf16[512,256]{1,0:T(8,128)(2,1)S(1)}, u32[]{:S(2)}, u32[]{:S(2)}) %collective-permute-start.20) | collective-permute-done | bytes 262176 | tf_op jit(solution)/shard_map/ppermute | solution.py:64
  83.8 3.3 %collective-permute-start.26 = (bf16[512,256]{1,0:T(8,128)(2,1)S(1)}, bf16[512,256]{1,0:T(8,128)(2,1)S(1)}, u32[]{:S(2)}, u32[]{:S(2)}) collective-permute-start(bf16[512,256]{1,0:T(8,128)(2,1)S(1)} %collective-permute-done.21), channel_id=1, source_target_pairs={{0,14},{1,15},{2,0},{3,1},{4,2},{5,3},{6,4},{7,5},{8,6},{9,7},{10,... | collective-permute-start | bytes 786440 | tf_op jit(solution)/shard_map/ppermute | solution.py:68
  87.1 1.8 %collective-permute-start.27 = (bf16[256,256]{1,0:T(8,128)(2,1)S(1)}, bf16[256,256]{1,0:T(8,128)(2,1)S(1)}, u32[]{:S(2)}, u32[]{:S(2)}) collective-permute-start(bf16[256,256]{1,0:T(8,128)(2,1)S(1)} %select_bitcast_fusion.2), channel_id=1, source_target_pairs={{0,1},{1,0},{2,3},{3,2},{4,5},{5,4},{6,7},{7,6},{8,9},{9,8},{10,11... | collective-permute-start | bytes 393224 | tf_op jit(solution)/shard_map/ppermute | solution.py:107
  89.2 0.3 fusion.23
  89.5 0.7 collective-permute-start.22
  90.5 0.3 fusion.20
  90.8 2.1 %collective-permute-done.25 = bf16[512,256]{1,0:T(8,128)(2,1)S(1)} collective-permute-done((bf16[512,256]{1,0:T(8,128)(2,1)S(1)}, bf16[512,256]{1,0:T(8,128)(2,1)S(1)}, u32[]{:S(2)}, u32[]{:S(2)}) %collective-permute-start.25) | collective-permute-done | bytes 262176 | tf_op jit(solution)/shard_map/ppermute | solution.py:64
  93.8 0.3 fusion.16
  94.0 0.4 fusion.5
  94.4 0.4 fusion.2
  94.9 2.4 %collective-permute-start.28 = (bf16[256,256]{1,0:T(8,128)(2,1)S(1)}, bf16[256,256]{1,0:T(8,128)(2,1)S(1)}, u32[]{:S(2)}, u32[]{:S(2)}) collective-permute-start(bf16[256,256]{1,0:T(8,128)(2,1)S(1)} %subtract_convert_fusion), channel_id=1, source_target_pairs={{0,1},{1,0},{2,3},{3,2},{4,5},{5,4},{6,7},{7,6},{8,9},{9,8},{10,11... | collective-permute-start | bytes 393224 | tf_op jit(solution)/shard_map/ppermute | solution.py:131
  97.4 0.7 maximum_bitcast_fusion
  98.1 2.2 %collective-permute-done.28 = bf16[256,256]{1,0:T(8,128)(2,1)S(1)} collective-permute-done((bf16[256,256]{1,0:T(8,128)(2,1)S(1)}, bf16[256,256]{1,0:T(8,128)(2,1)S(1)}, u32[]{:S(2)}, u32[]{:S(2)}) %collective-permute-start.28) | collective-permute-done | bytes 131104 | tf_op jit(solution)/shard_map/ppermute | solution.py:131
  100.4 0.7 maximum_bitcast_fusion.1
  (76 shorter events, 7.5 us)
Async XLA Ops:
  0.6 15.9 %copy-start = (bf16[2,1,1,256,1,1,256]{6,3,5,4,2,1,0:T(8,128)(2,1)S(1)}, bf16[2,1,1,256,1,1,256]{6,3,5,4,2,1,0:T(8,128)(2,1)}, u32[]{:S(2)}) copy-start(bf16[2,1,1,256,1,1,256]{6,3,5,4,2,1,0:T(8,128)(2,1)} %param.5) | copy-start | bytes 786436
  1.7 6.4 %collective-permute-start = (bf16[256,256]{1,0:T(8,128)(2,1)S(1)}, bf16[256,256]{1,0:T(8,128)(2,1)S(1)}, u32[]{:S(2)}, u32[]{:S(2)}) collective-permute-start(bf16[256,256]{1,0:T(8,128)(2,1)S(1)} %get-tuple-element.46), channel_id=1, source_target_pairs={{0,0},{1,16},{2,2},{3,18},{4,4},{5,20},{6,6},{7,22},{8,8},{9,24},{... | collective-permute-start | bytes 393224 | tf_op jit(solution)/shard_map/ppermute | solution.py:51
  2.4 7.9 %collective-permute-start.1 = (bf16[256,256]{1,0:T(8,128)(2,1)S(1)}, bf16[256,256]{1,0:T(8,128)(2,1)S(1)}, u32[]{:S(2)}, u32[]{:S(2)}) collective-permute-start(bf16[256,256]{1,0:T(8,128)(2,1)S(1)} %get-tuple-element.47), channel_id=1, source_target_pairs={{0,1},{1,17},{2,3},{3,19},{4,5},{5,21},{6,7},{7,23},{8,9},{9,25},{... | collective-permute-start | bytes 393224 | tf_op jit(solution)/shard_map/ppermute | solution.py:51
  8.1 8.4 %collective-permute-start.2 = (bf16[256,256]{1,0:T(8,128)(2,1)S(1)}, bf16[256,256]{1,0:T(8,128)(2,1)S(1)}, u32[]{:S(2)}, u32[]{:S(2)}) collective-permute-start(bf16[256,256]{1,0:T(8,128)(2,1)S(1)} %select_bitcast_fusion.7), channel_id=1, source_target_pairs={{0,1},{1,0},{2,3},{3,2},{4,5},{5,4},{6,7},{7,6},{8,9},{9,8},{10,11... | collective-permute-start | bytes 393224 | tf_op jit(solution)/shard_map/ppermute | solution.py:131
  10.5 11.8 %collective-permute-start.8 = (bf16[512,256]{1,0:T(8,128)(2,1)S(1)}, bf16[512,256]{1,0:T(8,128)(2,1)S(1)}, u32[]{:S(2)}, u32[]{:S(2)}) collective-permute-start(bf16[512,256]{1,0:T(8,128)(2,1)S(1)} %bitcast_select_fusion), channel_id=1, source_target_pairs={{0,2},{1,3},{2,4},{3,5},{4,6},{5,7},{6,8},{7,9},{8,10},{9,11},{10,... | collective-permute-start | bytes 786440 | tf_op jit(solution)/shard_map/ppermute | solution.py:64
  12.5 9.8 %collective-permute-start.9 = (bf16[512,256]{1,0:T(8,128)(2,1)S(1)}, bf16[512,256]{1,0:T(8,128)(2,1)S(1)}, u32[]{:S(2)}, u32[]{:S(2)}) collective-permute-start(bf16[512,256]{1,0:T(8,128)(2,1)S(1)} %bitcast_select_fusion), channel_id=1, source_target_pairs={{0,14},{1,15},{2,0},{3,1},{4,2},{5,3},{6,4},{7,5},{8,6},{9,7},{10,... | collective-permute-start | bytes 786440 | tf_op jit(solution)/shard_map/ppermute | solution.py:68
  16.6 9.0 %collective-permute-start.4 = (bf16[256,512]{1,0:T(8,128)(2,1)S(1)}, bf16[256,512]{1,0:T(8,128)(2,1)}, u32[]{:S(2)}, u32[]{:S(2)}) collective-permute-start(bf16[256,512]{1,0:T(8,128)(2,1)S(1)} %get-tuple-element.45), channel_id=1, source_target_pairs={{0,64},{16,80},{32,96},{48,112},{64,0},{80,16},{96,32},{112,48},{1... | collective-permute-start | bytes 786440 | tf_op jit(solution)/shard_map/ppermute | solution.py:154
  18.1 10.4 %collective-permute-start.3 = (bf16[256,512]{1,0:T(8,128)(2,1)S(1)}, bf16[256,512]{1,0:T(8,128)(2,1)S(1)}, u32[]{:S(2)}, u32[]{:S(2)}) collective-permute-start(bf16[256,512]{1,0:T(8,128)(2,1)S(1)} %get-tuple-element.45), channel_id=1, source_target_pairs={{0,128},{16,144},{32,160},{48,176},{64,192},{80,208},{96,224},{112... | collective-permute-start | bytes 786440 | tf_op jit(solution)/shard_map/ppermute | solution.py:156
  22.3 8.6 %collective-permute-start.10 = (bf16[512,256]{1,0:T(8,128)(2,1)S(1)}, bf16[512,256]{1,0:T(8,128)(2,1)S(1)}, u32[]{:S(2)}, u32[]{:S(2)}) collective-permute-start(bf16[512,256]{1,0:T(8,128)(2,1)S(1)} %collective-permute-done.8), channel_id=1, source_target_pairs={{0,2},{1,3},{2,4},{3,5},{4,6},{5,7},{6,8},{7,9},{8,10},{9,11},{10,... | collective-permute-start | bytes 786440 | tf_op jit(solution)/shard_map/ppermute | solution.py:64
  22.3 8.7 %collective-permute-start.11 = (bf16[512,256]{1,0:T(8,128)(2,1)S(1)}, bf16[512,256]{1,0:T(8,128)(2,1)S(1)}, u32[]{:S(2)}, u32[]{:S(2)}) collective-permute-start(bf16[512,256]{1,0:T(8,128)(2,1)S(1)} %collective-permute-done.9), channel_id=1, source_target_pairs={{0,14},{1,15},{2,0},{3,1},{4,2},{5,3},{6,4},{7,5},{8,6},{9,7},{10,... | collective-permute-start | bytes 786440 | tf_op jit(solution)/shard_map/ppermute | solution.py:68
  25.6 9.7 %collective-permute-start.5 = (bf16[256,512]{1,0:T(8,128)(2,1)}, bf16[256,512]{1,0:T(8,128)(2,1)S(1)}, u32[]{:S(2)}, u32[]{:S(2)}) collective-permute-start(bf16[256,512]{1,0:T(8,128)(2,1)} %collective-permute-done.4), channel_id=1, source_target_pairs={{0,128},{16,144},{32,160},{48,176},{64,192},{80,208},{96,224},{112... | collective-permute-start | bytes 786440 | tf_op jit(solution)/shard_map/ppermute | solution.py:161
  28.6 12.0 %collective-permute-start.6 = (bf16[2,256,512]{2,1,0:T(8,128)(2,1)S(1)}, bf16[2,256,512]{2,1,0:T(8,128)(2,1)S(1)}, u32[]{:S(2)}, u32[]{:S(2)}) collective-permute-start(bf16[2,256,512]{2,1,0:T(8,128)(2,1)S(1)} %get-tuple-element.40), channel_id=1, source_target_pairs={{0,32},{16,48},{32,64},{48,80},{64,96},{80,112},{96,0},{112,16},{1... | collective-permute-start | bytes 1572872 | tf_op jit(solution)/shard_map/ppermute | solution.py:154
  29.1 12.9 %collective-permute-start.7 = (bf16[2,256,512]{2,1,0:T(8,128)(2,1)S(1)}, bf16[2,256,512]{2,1,0:T(8,128)(2,1)S(1)}, u32[]{:S(2)}, u32[]{:S(2)}) collective-permute-start(bf16[2,256,512]{2,1,0:T(8,128)(2,1)S(1)} %get-tuple-element.40), channel_id=1, source_target_pairs={{0,96},{16,112},{32,0},{48,16},{64,32},{80,48},{96,64},{112,80},{1... | collective-permute-start | bytes 1572872 | tf_op jit(solution)/shard_map/ppermute | solution.py:154
  30.9 7.7 %collective-permute-start.12 = (bf16[512,256]{1,0:T(8,128)(2,1)S(1)}, bf16[512,256]{1,0:T(8,128)(2,1)S(1)}, u32[]{:S(2)}, u32[]{:S(2)}) collective-permute-start(bf16[512,256]{1,0:T(8,128)(2,1)S(1)} %collective-permute-done.10), channel_id=1, source_target_pairs={{0,2},{1,3},{2,4},{3,5},{4,6},{5,7},{6,8},{7,9},{8,10},{9,11},{10,... | collective-permute-start | bytes 786440 | tf_op jit(solution)/shard_map/ppermute | solution.py:64
  31.0 7.6 %collective-permute-start.13 = (bf16[512,256]{1,0:T(8,128)(2,1)S(1)}, bf16[512,256]{1,0:T(8,128)(2,1)S(1)}, u32[]{:S(2)}, u32[]{:S(2)}) collective-permute-start(bf16[512,256]{1,0:T(8,128)(2,1)S(1)} %collective-permute-done.11), channel_id=1, source_target_pairs={{0,14},{1,15},{2,0},{3,1},{4,2},{5,3},{6,4},{7,5},{8,6},{9,7},{10,... | collective-permute-start | bytes 786440 | tf_op jit(solution)/shard_map/ppermute | solution.py:68
  38.6 7.8 %collective-permute-start.14 = (bf16[512,256]{1,0:T(8,128)(2,1)S(1)}, bf16[512,256]{1,0:T(8,128)(2,1)S(1)}, u32[]{:S(2)}, u32[]{:S(2)}) collective-permute-start(bf16[512,256]{1,0:T(8,128)(2,1)S(1)} %broadcast_select_fusion.1), channel_id=1, source_target_pairs={{0,2},{1,3},{2,4},{3,5},{4,6},{5,7},{6,8},{7,9},{8,10},{9,11},{10,... | collective-permute-start | bytes 786440 | tf_op jit(solution)/shard_map/ppermute | solution.py:51
  42.7 30.1 %collective-permute-start.19 = (bf16[4,2,256,512]{3,2,1,0:T(8,128)(2,1)S(1)}, bf16[4,2,256,512]{3,2,1,0:T(8,128)(2,1)}, u32[]{:S(2)}, u32[]{:S(2)}) collective-permute-start(bf16[4,2,256,512]{3,2,1,0:T(8,128)(2,1)S(1)} %bitcast_dynamic-update-slice_fusion), channel_id=1, source_target_pairs={{0,16},{16,0},{32,48},{48,32},{64,80},{80,64},{96,112},{112,96},{1... | collective-permute-start | bytes 6291464 | tf_op jit(solution)/shard_map/ppermute | solution.py:196
  46.8 2.0 %collective-permute-start.15 = (f32[512,256]{1,0:T(8,128)S(1)}, f32[512,256]{1,0:T(8,128)S(1)}, u32[]{:S(2)}, u32[]{:S(2)}) collective-permute-start(f32[512,256]{1,0:T(8,128)S(1)} %fusion.7), channel_id=1, source_target_pairs={{0,16},{16,0},{32,48},{48,32},{64,80},{80,64},{96,112},{112,96},{1... | collective-permute-start | bytes 1572872 | tf_op jit(solution)/shard_map/ppermute | solution.py:190
  47.6 7.5 %copy-start.1 = (bf16[2,1,1,256,1,1,256]{6,3,5,4,2,1,0:T(8,128)(2,1)S(1)}, bf16[2,1,1,256,1,1,256]{6,3,5,4,2,1,0:T(8,128)(2,1)}, u32[]{:S(2)}) copy-start(bf16[2,1,1,256,1,1,256]{6,3,5,4,2,1,0:T(8,128)(2,1)} %param.6) | copy-start | bytes 786436
  49.1 18.1 %collective-permute-start.17 = (bf16[512,256]{1,0:T(8,128)(2,1)S(1)}, bf16[512,256]{1,0:T(8,128)(2,1)S(1)}, u32[]{:S(2)}, u32[]{:S(2)}) collective-permute-start(bf16[512,256]{1,0:T(8,128)(2,1)S(1)} %fusion.14), channel_id=1, source_target_pairs={{0,2},{1,3},{2,40},{3,41},{4,78},{5,79},{6,108},{7,109},{8,130},{9... | collective-permute-start | bytes 786440 | tf_op jit(solution)/shard_map/ppermute | solution.py:51
  55.0 17.8 %collective-permute-start.18 = (bf16[512,256]{1,0:T(8,128)(2,1)S(1)}, bf16[512,256]{1,0:T(8,128)(2,1)S(1)}, u32[]{:S(2)}, u32[]{:S(2)}) collective-permute-start(bf16[512,256]{1,0:T(8,128)(2,1)S(1)} %fusion.14), channel_id=1, source_target_pairs={{0,10},{1,11},{2,32},{3,33},{4,70},{5,71},{6,100},{7,101},{8,138},... | collective-permute-start | bytes 786440 | tf_op jit(solution)/shard_map/ppermute | solution.py:51
  55.0 1.4 %collective-permute-start.16 = (bf16[256,256]{1,0:T(8,128)(2,1)S(1)}, bf16[256,256]{1,0:T(8,128)(2,1)S(1)}, u32[]{:S(2)}, u32[]{:S(2)}) collective-permute-start(bf16[256,256]{1,0:T(8,128)(2,1)S(1)} %slice.215), channel_id=1, source_target_pairs={{0,16},{16,0},{32,48},{48,32},{64,80},{80,64},{96,112},{112,96},{1... | collective-permute-start | bytes 393224 | tf_op jit(solution)/shard_map/ppermute | solution.py:199
  72.8 10.5 %collective-permute-start.20 = (bf16[512,256]{1,0:T(8,128)(2,1)S(1)}, bf16[512,256]{1,0:T(8,128)(2,1)S(1)}, u32[]{:S(2)}, u32[]{:S(2)}) collective-permute-start(bf16[512,256]{1,0:T(8,128)(2,1)S(1)} %collective-permute-done.17), channel_id=1, source_target_pairs={{0,2},{1,3},{2,4},{3,5},{4,6},{5,7},{6,8},{7,9},{8,10},{9,11},{10,... | collective-permute-start | bytes 786440 | tf_op jit(solution)/shard_map/ppermute | solution.py:64
  72.8 10.5 %collective-permute-start.21 = (bf16[512,256]{1,0:T(8,128)(2,1)S(1)}, bf16[512,256]{1,0:T(8,128)(2,1)S(1)}, u32[]{:S(2)}, u32[]{:S(2)}) collective-permute-start(bf16[512,256]{1,0:T(8,128)(2,1)S(1)} %collective-permute-done.17), channel_id=1, source_target_pairs={{0,14},{1,15},{2,0},{3,1},{4,2},{5,3},{6,4},{7,5},{8,6},{9,7},{10,... | collective-permute-start | bytes 786440 | tf_op jit(solution)/shard_map/ppermute | solution.py:68
  76.1 13.4 %collective-permute-start.24 = (bf16[512,256]{1,0:T(8,128)(2,1)S(1)}, bf16[512,256]{1,0:T(8,128)(2,1)S(1)}, u32[]{:S(2)}, u32[]{:S(2)}) collective-permute-start(bf16[512,256]{1,0:T(8,128)(2,1)S(1)} %collective-permute-done.18), channel_id=1, source_target_pairs={{0,14},{1,15},{2,0},{3,1},{4,2},{5,3},{6,4},{7,5},{8,6},{9,7},{10,... | collective-permute-start | bytes 786440 | tf_op jit(solution)/shard_map/ppermute | solution.py:68
  76.1 17.9 %collective-permute-start.23 = (bf16[512,256]{1,0:T(8,128)(2,1)S(1)}, bf16[512,256]{1,0:T(8,128)(2,1)S(1)}, u32[]{:S(2)}, u32[]{:S(2)}) collective-permute-start(bf16[512,256]{1,0:T(8,128)(2,1)S(1)} %collective-permute-done.18), channel_id=1, source_target_pairs={{0,2},{1,3},{2,4},{3,5},{4,6},{5,7},{6,8},{7,9},{8,10},{9,11},{10,... | collective-permute-start | bytes 786440 | tf_op jit(solution)/shard_map/ppermute | solution.py:64
  83.3 9.6 %collective-permute-start.25 = (bf16[512,256]{1,0:T(8,128)(2,1)S(1)}, bf16[512,256]{1,0:T(8,128)(2,1)S(1)}, u32[]{:S(2)}, u32[]{:S(2)}) collective-permute-start(bf16[512,256]{1,0:T(8,128)(2,1)S(1)} %collective-permute-done.20), channel_id=1, source_target_pairs={{0,2},{1,3},{2,4},{3,5},{4,6},{5,7},{6,8},{7,9},{8,10},{9,11},{10,... | collective-permute-start | bytes 786440 | tf_op jit(solution)/shard_map/ppermute | solution.py:64
  83.8 9.6 %collective-permute-start.26 = (bf16[512,256]{1,0:T(8,128)(2,1)S(1)}, bf16[512,256]{1,0:T(8,128)(2,1)S(1)}, u32[]{:S(2)}, u32[]{:S(2)}) collective-permute-start(bf16[512,256]{1,0:T(8,128)(2,1)S(1)} %collective-permute-done.21), channel_id=1, source_target_pairs={{0,14},{1,15},{2,0},{3,1},{4,2},{5,3},{6,4},{7,5},{8,6},{9,7},{10,... | collective-permute-start | bytes 786440 | tf_op jit(solution)/shard_map/ppermute | solution.py:68
  87.1 7.7 %collective-permute-start.27 = (bf16[256,256]{1,0:T(8,128)(2,1)S(1)}, bf16[256,256]{1,0:T(8,128)(2,1)S(1)}, u32[]{:S(2)}, u32[]{:S(2)}) collective-permute-start(bf16[256,256]{1,0:T(8,128)(2,1)S(1)} %select_bitcast_fusion.2), channel_id=1, source_target_pairs={{0,1},{1,0},{2,3},{3,2},{4,5},{5,4},{6,7},{7,6},{8,9},{9,8},{10,11... | collective-permute-start | bytes 393224 | tf_op jit(solution)/shard_map/ppermute | solution.py:107
  89.5 7.9 %collective-permute-start.22 = (bf16[256,256]{1,0:T(8,128)(2,1)S(1)}, bf16[256,256]{1,0:T(8,128)(2,1)S(1)}, u32[]{:S(2)}, u32[]{:S(2)}) collective-permute-start(bf16[256,256]{1,0:T(8,128)(2,1)S(1)} %broadcast_select_fusion.3), channel_id=1, source_target_pairs={{0,1},{1,0},{2,3},{3,2},{4,5},{5,4},{6,7},{7,6},{8,9},{9,8},{10,11... | collective-permute-start | bytes 393224 | tf_op jit(solution)/shard_map/ppermute | solution.py:107
  94.9 5.4 %collective-permute-start.28 = (bf16[256,256]{1,0:T(8,128)(2,1)S(1)}, bf16[256,256]{1,0:T(8,128)(2,1)S(1)}, u32[]{:S(2)}, u32[]{:S(2)}) collective-permute-start(bf16[256,256]{1,0:T(8,128)(2,1)S(1)} %subtract_convert_fusion), channel_id=1, source_target_pairs={{0,1},{1,0},{2,3},{3,2},{4,5},{5,4},{6,7},{7,6},{8,9},{9,8},{10,11... | collective-permute-start | bytes 393224 | tf_op jit(solution)/shard_map/ppermute | solution.py:131

commit v6 on v5

--- a/solution.py
+++ b/solution.py
@@ -218,9 +218,9 @@
             )
         )
 
-    total, (off_got, d_got) = z_two(
-        o_piece, o_other, add_inner, (zero, zero), (jnp.where(same, second, first), other(diag))
-    )
+    beside = jnp.stack([jnp.where(same, second, first), other(diag)])
+    total, (got,) = z_two(o_piece, o_other, add_inner, (zero, zero), (beside,))
+    off_got, d_got = got[0], got[1]
     first = total[0][:256] + total[1][256:]
     second = total[0][256:] + total[1][:256]
     d_mine = mine(diag)

time: 102 us -> 107 us (1.049)
  the two profiles are of different devices: /device:TPU:6 before, /device:TPU:24 now
where the time goes in v6:
time: 107 us
  waiting for transfers between devices  48.8 us (46%)
  starting transfers between devices  42.3 us (40%)
  matrix products  8.17 us (8%)
  other arithmetic  5.13 us (5%)
  local copies, waits for them, and re-layouts  1.44 us (1%)
  between operations  1.15 us (1%)
    ppermute x5, waiting for transfers between devices, move(): return lax.ppermute(block, ('prow', 'pcol'), pairs)  29.4 us
    ppermute x6, starting transfers between devices, down(): return lax.ppermute(block, 'pcol', DOWN)  18.2 us
    ppermute x6, waiting for transfers between devices, up(): return lax.ppermute(block, 'pcol', UP)  11.4 us
    ppermute x5, starting transfers between devices, move(): return lax.ppermute(block, ('prow', 'pcol'), pairs)  8.97 us
    ppermute x3, starting transfers between devices, along_x(): lax.ppermute(block, 'prow', row_perm(lambda h, x, c: (h, x + step, c)))  6.42 us
    dot_general x16, matrix products, add_inner(): lax.dot_general(u_rows(panel, owner), rows, (((0,), (0,)), ((), ())), pre...  4.54 us
    ppermute x6, starting transfers between devices, up(): return lax.ppermute(block, 'pcol', UP)  4.24 us
    ppermute x2, waiting for transfers between devices, swap(): return lax.ppermute(block, 'pcol', SWAP)  3.8 us
  transfers between devices with their start and end apart: 28, of which 13 were waited for; matrix products, arithmetic and copies ran while one was open for 12% of the time, Pallas kernels for 0%

profile of v6, /device:TPU:24, one launch (start us, length us, event | category | flops | bytes accessed | tf_op | source)
XLA Modules:
  0.0 107.0 jit_solution(10236911696274059037)
XLA Ops:
  0.7 1.0 select_bitcast_fusion.7
  1.7 2.1 %collective-permute-start = (bf16[256,256]{1,0:T(8,128)(2,1)S(1)}, bf16[256,256]{1,0:T(8,128)(2,1)S(1)}, u32[]{:S(2)}, u32[]{:S(2)}) collective-permute-start(bf16[256,256]{1,0:T(8,128)(2,1)S(1)} %get-tuple-element.44), channel_id=1, source_target_pairs={{0,0},{1,16},{2,2},{3,18},{4,4},{5,20},{6,6},{7,22},{8,8},{9,24},{... | collective-permute-start | bytes 393224 | tf_op jit(solution)/shard_map/ppermute | solution.py:51
  3.9 0.8 dynamic_slice.75
  4.7 0.9 compare_reduce_fusion
  5.7 1.0 select_bitcast_fusion.8
  6.7 1.8 %collective-permute-done = bf16[256,256]{1,0:T(8,128)(2,1)S(1)} collective-permute-done((bf16[256,256]{1,0:T(8,128)(2,1)S(1)}, bf16[256,256]{1,0:T(8,128)(2,1)S(1)}, u32[]{:S(2)}, u32[]{:S(2)}) %collective-permute-start) | collective-permute-done | bytes 131104 | tf_op jit(solution)/shard_map/ppermute | solution.py:51
  8.8 0.6 collective-permute-done.1
  9.6 2.0 %collective-permute-start.8 = (bf16[512,256]{1,0:T(8,128)(2,1)S(1)}, bf16[512,256]{1,0:T(8,128)(2,1)S(1)}, u32[]{:S(2)}, u32[]{:S(2)}) collective-permute-start(bf16[512,256]{1,0:T(8,128)(2,1)S(1)} %bitcast_select_fusion), channel_id=1, source_target_pairs={{0,2},{1,3},{2,4},{3,5},{4,6},{5,7},{6,8},{7,9},{8,10},{9,11},{10,... | collective-permute-start | bytes 786440 | tf_op jit(solution)/shard_map/ppermute | solution.py:64
  11.5 4.0 %collective-permute-start.9 = (bf16[512,256]{1,0:T(8,128)(2,1)S(1)}, bf16[512,256]{1,0:T(8,128)(2,1)S(1)}, u32[]{:S(2)}, u32[]{:S(2)}) collective-permute-start(bf16[512,256]{1,0:T(8,128)(2,1)S(1)} %bitcast_select_fusion), channel_id=1, source_target_pairs={{0,14},{1,15},{2,0},{3,1},{4,2},{5,3},{6,4},{7,5},{8,6},{9,7},{10,... | collective-permute-start | bytes 786440 | tf_op jit(solution)/shard_map/ppermute | solution.py:68
  15.7 3.1 %collective-permute-start.4 = (bf16[256,512]{1,0:T(8,128)(2,1)S(1)}, bf16[256,512]{1,0:T(8,128)(2,1)S(1)}, u32[]{:S(2)}, u32[]{:S(2)}) collective-permute-start(bf16[256,512]{1,0:T(8,128)(2,1)S(1)} %get-tuple-element.43), channel_id=1, source_target_pairs={{0,64},{16,80},{32,96},{48,112},{64,0},{80,16},{96,32},{112,48},{1... | collective-permute-start | bytes 786440 | tf_op jit(solution)/shard_map/ppermute | solution.py:154
  18.8 1.2 %collective-permute-start.3 = (bf16[256,512]{1,0:T(8,128)(2,1)S(1)}, bf16[256,512]{1,0:T(8,128)(2,1)S(1)}, u32[]{:S(2)}, u32[]{:S(2)}) collective-permute-start(bf16[256,512]{1,0:T(8,128)(2,1)S(1)} %get-tuple-element.43), channel_id=1, source_target_pairs={{0,128},{16,144},{32,160},{48,176},{64,192},{80,208},{96,224},{112... | collective-permute-start | bytes 786440 | tf_op jit(solution)/shard_map/ppermute | solution.py:156
  20.0 1.1 %collective-permute-done.8 = bf16[512,256]{1,0:T(8,128)(2,1)S(1)} collective-permute-done((bf16[512,256]{1,0:T(8,128)(2,1)S(1)}, bf16[512,256]{1,0:T(8,128)(2,1)S(1)}, u32[]{:S(2)}, u32[]{:S(2)}) %collective-permute-start.8) | collective-permute-done | bytes 262176 | tf_op jit(solution)/shard_map/ppermute | solution.py:64
  21.2 3.2 %collective-permute-start.11 = (bf16[512,256]{1,0:T(8,128)(2,1)S(1)}, bf16[512,256]{1,0:T(8,128)(2,1)S(1)}, u32[]{:S(2)}, u32[]{:S(2)}) collective-permute-start(bf16[512,256]{1,0:T(8,128)(2,1)S(1)} %collective-permute-done.9), channel_id=1, source_target_pairs={{0,14},{1,15},{2,0},{3,1},{4,2},{5,3},{6,4},{7,5},{8,6},{9,7},{10,... | collective-permute-start | bytes 786440 | tf_op jit(solution)/shard_map/ppermute | solution.py:68
  24.4 2.1 %collective-permute-start.5 = (bf16[256,512]{1,0:T(8,128)(2,1)S(1)}, bf16[256,512]{1,0:T(8,128)(2,1)S(1)}, u32[]{:S(2)}, u32[]{:S(2)}) collective-permute-start(bf16[256,512]{1,0:T(8,128)(2,1)S(1)} %collective-permute-done.4), channel_id=1, source_target_pairs={{0,128},{16,144},{32,160},{48,176},{64,192},{80,208},{96,224},{112... | collective-permute-start | bytes 786440 | tf_op jit(solution)/shard_map/ppermute | solution.py:161
  26.5 1.2 %collective-permute-done.3 = bf16[256,512]{1,0:T(8,128)(2,1)S(1)} collective-permute-done((bf16[256,512]{1,0:T(8,128)(2,1)S(1)}, bf16[256,512]{1,0:T(8,128)(2,1)S(1)}, u32[]{:S(2)}, u32[]{:S(2)}) %collective-permute-start.3) | collective-permute-done | bytes 262176 | tf_op jit(solution)/shard_map/ppermute | solution.py:156
  27.9 3.2 %collective-permute-start.7 = (bf16[2,256,512]{2,1,0:T(8,128)(2,1)S(1)}, bf16[2,256,512]{2,1,0:T(8,128)(2,1)S(1)}, u32[]{:S(2)}, u32[]{:S(2)}) collective-permute-start(bf16[2,256,512]{2,1,0:T(8,128)(2,1)S(1)} %get-tuple-element.38), channel_id=1, source_target_pairs={{0,96},{16,112},{32,0},{48,16},{64,32},{80,48},{96,64},{112,80},{1... | collective-permute-start | bytes 1572872 | tf_op jit(solution)/shard_map/ppermute | solution.py:154
  31.5 4.0 %collective-permute-start.13 = (bf16[512,256]{1,0:T(8,128)(2,1)S(1)}, bf16[512,256]{1,0:T(8,128)(2,1)S(1)}, u32[]{:S(2)}, u32[]{:S(2)}) collective-permute-start(bf16[512,256]{1,0:T(8,128)(2,1)S(1)} %collective-permute-done.11), channel_id=1, source_target_pairs={{0,14},{1,15},{2,0},{3,1},{4,2},{5,3},{6,4},{7,5},{8,6},{9,7},{10,... | collective-permute-start | bytes 786440 | tf_op jit(solution)/shard_map/ppermute | solution.py:68
  35.6 4.2 %collective-permute-done.12 = bf16[512,256]{1,0:T(8,128)(2,1)S(1)} collective-permute-done((bf16[512,256]{1,0:T(8,128)(2,1)S(1)}, bf16[512,256]{1,0:T(8,128)(2,1)S(1)}, u32[]{:S(2)}, u32[]{:S(2)}) %collective-permute-start.12) | collective-permute-done | bytes 262176 | tf_op jit(solution)/shard_map/ppermute | solution.py:64
  42.8 4.9 %collective-permute-done.14 = bf16[512,256]{1,0:T(8,128)(2,1)S(1)} collective-permute-done((bf16[512,256]{1,0:T(8,128)(2,1)S(1)}, bf16[512,256]{1,0:T(8,128)(2,1)S(1)}, u32[]{:S(2)}, u32[]{:S(2)}) %collective-permute-start.14) | collective-permute-done | bytes 262176 | tf_op jit(solution)/shard_map/ppermute | solution.py:51
  49.0 1.2 %collective-permute-done.15 = f32[512,256]{1,0:T(8,128)S(1)} collective-permute-done((f32[512,256]{1,0:T(8,128)S(1)}, f32[512,256]{1,0:T(8,128)S(1)}, u32[]{:S(2)}, u32[]{:S(2)}) %collective-permute-start.15) | collective-permute-done | bytes 524320 | tf_op jit(solution)/shard_map/ppermute | solution.py:190
  50.3 0.3 fusion.14
  50.8 5.2 %collective-permute-start.17 = (bf16[512,256]{1,0:T(8,128)(2,1)S(1)}, bf16[512,256]{1,0:T(8,128)(2,1)S(1)}, u32[]{:S(2)}, u32[]{:S(2)}) collective-permute-start(bf16[512,256]{1,0:T(8,128)(2,1)S(1)} %fusion.14), channel_id=1, source_target_pairs={{0,2},{1,3},{2,40},{3,41},{4,78},{5,79},{6,108},{7,109},{8,130},{9... | collective-permute-start | bytes 786440 | tf_op jit(solution)/shard_map/ppermute | solution.py:51
  56.0 1.3 %collective-permute-start.18 = (bf16[512,256]{1,0:T(8,128)(2,1)S(1)}, bf16[512,256]{1,0:T(8,128)(2,1)S(1)}, u32[]{:S(2)}, u32[]{:S(2)}) collective-permute-start(bf16[512,256]{1,0:T(8,128)(2,1)S(1)} %fusion.14), channel_id=1, source_target_pairs={{0,10},{1,11},{2,32},{3,33},{4,70},{5,71},{6,100},{7,101},{8,138},... | collective-permute-start | bytes 786440 | tf_op jit(solution)/shard_map/ppermute | solution.py:51
  57.4 13.9 %collective-permute-done.17 = bf16[512,256]{1,0:T(8,128)(2,1)S(1)} collective-permute-done((bf16[512,256]{1,0:T(8,128)(2,1)S(1)}, bf16[512,256]{1,0:T(8,128)(2,1)S(1)}, u32[]{:S(2)}, u32[]{:S(2)}) %collective-permute-start.17) | collective-permute-done | bytes 262176 | tf_op jit(solution)/shard_map/ppermute | solution.py:51
  71.3 8.1 %collective-permute-done.18 = bf16[512,256]{1,0:T(8,128)(2,1)S(1)} collective-permute-done((bf16[512,256]{1,0:T(8,128)(2,1)S(1)}, bf16[512,256]{1,0:T(8,128)(2,1)S(1)}, u32[]{:S(2)}, u32[]{:S(2)}) %collective-permute-start.18) | collective-permute-done | bytes 262176 | tf_op jit(solution)/shard_map/ppermute | solution.py:51
  79.4 3.2 %collective-permute-start.21 = (bf16[512,256]{1,0:T(8,128)(2,1)S(1)}, bf16[512,256]{1,0:T(8,128)(2,1)S(1)}, u32[]{:S(2)}, u32[]{:S(2)}) collective-permute-start(bf16[512,256]{1,0:T(8,128)(2,1)S(1)} %collective-permute-done.17), channel_id=1, source_target_pairs={{0,14},{1,15},{2,0},{3,1},{4,2},{5,3},{6,4},{7,5},{8,6},{9,7},{10,... | collective-permute-start | bytes 786440 | tf_op jit(solution)/shard_map/ppermute | solution.py:68
  82.7 2.0 %collective-permute-start.23 = (bf16[512,256]{1,0:T(8,128)(2,1)S(1)}, bf16[512,256]{1,0:T(8,128)(2,1)S(1)}, u32[]{:S(2)}, u32[]{:S(2)}) collective-permute-start(bf16[512,256]{1,0:T(8,128)(2,1)S(1)} %collective-permute-done.18), channel_id=1, source_target_pairs={{0,2},{1,3},{2,4},{3,5},{4,6},{5,7},{6,8},{7,9},{8,10},{9,11},{10,... | collective-permute-start | bytes 786440 | tf_op jit(solution)/shard_map/ppermute | solution.py:64
  84.8 0.3 fusion.45
  85.1 0.3 fusion.43
  85.3 0.3 fusion.41
  85.6 0.3 fusion.28
  85.9 3.4 %collective-permute-done.20 = bf16[512,256]{1,0:T(8,128)(2,1)S(1)} collective-permute-done((bf16[512,256]{1,0:T(8,128)(2,1)S(1)}, bf16[512,256]{1,0:T(8,128)(2,1)S(1)}, u32[]{:S(2)}, u32[]{:S(2)}) %collective-permute-start.20) | collective-permute-done | bytes 262176 | tf_op jit(solution)/shard_map/ppermute | solution.py:64
  89.6 0.3 fusion.26
  89.9 3.6 %collective-permute-start.26 = (bf16[512,256]{1,0:T(8,128)(2,1)S(1)}, bf16[512,256]{1,0:T(8,128)(2,1)S(1)}, u32[]{:S(2)}, u32[]{:S(2)}) collective-permute-start(bf16[512,256]{1,0:T(8,128)(2,1)S(1)} %collective-permute-done.21), channel_id=1, source_target_pairs={{0,14},{1,15},{2,0},{3,1},{4,2},{5,3},{6,4},{7,5},{8,6},{9,7},{10,... | collective-permute-start | bytes 786440 | tf_op jit(solution)/shard_map/ppermute | solution.py:68
  93.8 0.3 fusion.24
  94.1 0.3 fusion.34
  94.4 0.3 fusion.21
  94.7 2.6 %collective-permute-done.25 = bf16[512,256]{1,0:T(8,128)(2,1)S(1)} collective-permute-done((bf16[512,256]{1,0:T(8,128)(2,1)S(1)}, bf16[512,256]{1,0:T(8,128)(2,1)S(1)}, u32[]{:S(2)}, u32[]{:S(2)}) %collective-permute-start.25) | collective-permute-done | bytes 262176 | tf_op jit(solution)/shard_map/ppermute | solution.py:64
  97.5 0.3 fusion.19
  97.8 0.3 fusion.30
  98.1 0.3 fusion.17
  98.4 0.4 fusion.5
  98.8 0.4 fusion.2
  99.2 1.8 %collective-permute-done.22 = bf16[2,256,256]{2,1,0:T(8,128)(2,1)S(1)} collective-permute-done((bf16[2,256,256]{2,1,0:T(8,128)(2,1)S(1)}, bf16[2,256,256]{2,1,0:T(8,128)(2,1)S(1)}, u32[]{:S(2)}, u32[]{:S(2)}) %collective-permute-start.22) | collective-permute-done | bytes 262176 | tf_op jit(solution)/shard_map/ppermute | solution.py:107
  101.0 0.5 collective-permute-start.27
  101.5 0.7 maximum_bitcast_fusion
  102.3 3.8 %collective-permute-done.27 = bf16[256,256]{1,0:T(8,128)(2,1)S(1)} collective-permute-done((bf16[256,256]{1,0:T(8,128)(2,1)S(1)}, bf16[256,256]{1,0:T(8,128)(2,1)S(1)}, u32[]{:S(2)}, u32[]{:S(2)}) %collective-permute-start.27) | collective-permute-done | bytes 131104 | tf_op jit(solution)/shard_map/ppermute | solution.py:131
  106.2 0.7 maximum_bitcast_fusion.1
  (75 shorter events, 7.0 us)
Async XLA Ops:
  0.6 15.0 %copy-start = (bf16[2,1,1,256,1,1,256]{6,3,5,4,2,1,0:T(8,128)(2,1)S(1)}, bf16[2,1,1,256,1,1,256]{6,3,5,4,2,1,0:T(8,128)(2,1)}, u32[]{:S(2)}) copy-start(bf16[2,1,1,256,1,1,256]{6,3,5,4,2,1,0:T(8,128)(2,1)} %param.5) | copy-start | bytes 786436
  1.7 6.8 %collective-permute-start = (bf16[256,256]{1,0:T(8,128)(2,1)S(1)}, bf16[256,256]{1,0:T(8,128)(2,1)S(1)}, u32[]{:S(2)}, u32[]{:S(2)}) collective-permute-start(bf16[256,256]{1,0:T(8,128)(2,1)S(1)} %get-tuple-element.44), channel_id=1, source_target_pairs={{0,0},{1,16},{2,2},{3,18},{4,4},{5,20},{6,6},{7,22},{8,8},{9,24},{... | collective-permute-start | bytes 393224 | tf_op jit(solution)/shard_map/ppermute | solution.py:51
  3.8 5.6 %collective-permute-start.1 = (bf16[256,256]{1,0:T(8,128)(2,1)S(1)}, bf16[256,256]{1,0:T(8,128)(2,1)S(1)}, u32[]{:S(2)}, u32[]{:S(2)}) collective-permute-start(bf16[256,256]{1,0:T(8,128)(2,1)S(1)} %get-tuple-element.45), channel_id=1, source_target_pairs={{0,1},{1,17},{2,3},{3,19},{4,5},{5,21},{6,7},{7,23},{8,9},{9,25},{... | collective-permute-start | bytes 393224 | tf_op jit(solution)/shard_map/ppermute | solution.py:51
  8.5 7.0 %collective-permute-start.2 = (bf16[256,256]{1,0:T(8,128)(2,1)S(1)}, bf16[256,256]{1,0:T(8,128)(2,1)S(1)}, u32[]{:S(2)}, u32[]{:S(2)}) collective-permute-start(bf16[256,256]{1,0:T(8,128)(2,1)S(1)} %select_bitcast_fusion.8), channel_id=1, source_target_pairs={{0,1},{1,0},{2,3},{3,2},{4,5},{5,4},{6,7},{7,6},{8,9},{9,8},{10,11... | collective-permute-start | bytes 393224 | tf_op jit(solution)/shard_map/ppermute | solution.py:131
  9.6 11.6 %collective-permute-start.8 = (bf16[512,256]{1,0:T(8,128)(2,1)S(1)}, bf16[512,256]{1,0:T(8,128)(2,1)S(1)}, u32[]{:S(2)}, u32[]{:S(2)}) collective-permute-start(bf16[512,256]{1,0:T(8,128)(2,1)S(1)} %bitcast_select_fusion), channel_id=1, source_target_pairs={{0,2},{1,3},{2,4},{3,5},{4,6},{5,7},{6,8},{7,9},{8,10},{9,11},{10,... | collective-permute-start | bytes 786440 | tf_op jit(solution)/shard_map/ppermute | solution.py:64
  11.5 9.6 %collective-permute-start.9 = (bf16[512,256]{1,0:T(8,128)(2,1)S(1)}, bf16[512,256]{1,0:T(8,128)(2,1)S(1)}, u32[]{:S(2)}, u32[]{:S(2)}) collective-permute-start(bf16[512,256]{1,0:T(8,128)(2,1)S(1)} %bitcast_select_fusion), channel_id=1, source_target_pairs={{0,14},{1,15},{2,0},{3,1},{4,2},{5,3},{6,4},{7,5},{8,6},{9,7},{10,... | collective-permute-start | bytes 786440 | tf_op jit(solution)/shard_map/ppermute | solution.py:68
  15.7 8.7 %collective-permute-start.4 = (bf16[256,512]{1,0:T(8,128)(2,1)S(1)}, bf16[256,512]{1,0:T(8,128)(2,1)S(1)}, u32[]{:S(2)}, u32[]{:S(2)}) collective-permute-start(bf16[256,512]{1,0:T(8,128)(2,1)S(1)} %get-tuple-element.43), channel_id=1, source_target_pairs={{0,64},{16,80},{32,96},{48,112},{64,0},{80,16},{96,32},{112,48},{1... | collective-permute-start | bytes 786440 | tf_op jit(solution)/shard_map/ppermute | solution.py:154
  18.8 8.9 %collective-permute-start.3 = (bf16[256,512]{1,0:T(8,128)(2,1)S(1)}, bf16[256,512]{1,0:T(8,128)(2,1)S(1)}, u32[]{:S(2)}, u32[]{:S(2)}) collective-permute-start(bf16[256,512]{1,0:T(8,128)(2,1)S(1)} %get-tuple-element.43), channel_id=1, source_target_pairs={{0,128},{16,144},{32,160},{48,176},{64,192},{80,208},{96,224},{112... | collective-permute-start | bytes 786440 | tf_op jit(solution)/shard_map/ppermute | solution.py:156
  21.1 10.1 %collective-permute-start.10 = (bf16[512,256]{1,0:T(8,128)(2,1)S(1)}, bf16[512,256]{1,0:T(8,128)(2,1)S(1)}, u32[]{:S(2)}, u32[]{:S(2)}) collective-permute-start(bf16[512,256]{1,0:T(8,128)(2,1)S(1)} %collective-permute-done.8), channel_id=1, source_target_pairs={{0,2},{1,3},{2,4},{3,5},{4,6},{5,7},{6,8},{7,9},{8,10},{9,11},{10,... | collective-permute-start | bytes 786440 | tf_op jit(solution)/shard_map/ppermute | solution.py:64
  21.2 10.3 %collective-permute-start.11 = (bf16[512,256]{1,0:T(8,128)(2,1)S(1)}, bf16[512,256]{1,0:T(8,128)(2,1)S(1)}, u32[]{:S(2)}, u32[]{:S(2)}) collective-permute-start(bf16[512,256]{1,0:T(8,128)(2,1)S(1)} %collective-permute-done.9), channel_id=1, source_target_pairs={{0,14},{1,15},{2,0},{3,1},{4,2},{5,3},{6,4},{7,5},{8,6},{9,7},{10,... | collective-permute-start | bytes 786440 | tf_op jit(solution)/shard_map/ppermute | solution.py:68
  24.4 11.2 %collective-permute-start.5 = (bf16[256,512]{1,0:T(8,128)(2,1)S(1)}, bf16[256,512]{1,0:T(8,128)(2,1)S(1)}, u32[]{:S(2)}, u32[]{:S(2)}) collective-permute-start(bf16[256,512]{1,0:T(8,128)(2,1)S(1)} %collective-permute-done.4), channel_id=1, source_target_pairs={{0,128},{16,144},{32,160},{48,176},{64,192},{80,208},{96,224},{112... | collective-permute-start | bytes 786440 | tf_op jit(solution)/shard_map/ppermute | solution.py:161
  27.7 12.3 %collective-permute-start.6 = (bf16[2,256,512]{2,1,0:T(8,128)(2,1)S(1)}, bf16[2,256,512]{2,1,0:T(8,128)(2,1)S(1)}, u32[]{:S(2)}, u32[]{:S(2)}) collective-permute-start(bf16[2,256,512]{2,1,0:T(8,128)(2,1)S(1)} %get-tuple-element.38), channel_id=1, source_target_pairs={{0,32},{16,48},{32,64},{48,80},{64,96},{80,112},{96,0},{112,16},{1... | collective-permute-start | bytes 1572872 | tf_op jit(solution)/shard_map/ppermute | solution.py:154
  27.9 12.3 %collective-permute-start.7 = (bf16[2,256,512]{2,1,0:T(8,128)(2,1)S(1)}, bf16[2,256,512]{2,1,0:T(8,128)(2,1)S(1)}, u32[]{:S(2)}, u32[]{:S(2)}) collective-permute-start(bf16[2,256,512]{2,1,0:T(8,128)(2,1)S(1)} %get-tuple-element.38), channel_id=1, source_target_pairs={{0,96},{16,112},{32,0},{48,16},{64,32},{80,48},{96,64},{112,80},{1... | collective-permute-start | bytes 1572872 | tf_op jit(solution)/shard_map/ppermute | solution.py:154
  31.2 8.5 %collective-permute-start.12 = (bf16[512,256]{1,0:T(8,128)(2,1)S(1)}, bf16[512,256]{1,0:T(8,128)(2,1)S(1)}, u32[]{:S(2)}, u32[]{:S(2)}) collective-permute-start(bf16[512,256]{1,0:T(8,128)(2,1)S(1)} %collective-permute-done.10), channel_id=1, source_target_pairs={{0,2},{1,3},{2,4},{3,5},{4,6},{5,7},{6,8},{7,9},{8,10},{9,11},{10,... | collective-permute-start | bytes 786440 | tf_op jit(solution)/shard_map/ppermute | solution.py:64
  31.5 8.3 %collective-permute-start.13 = (bf16[512,256]{1,0:T(8,128)(2,1)S(1)}, bf16[512,256]{1,0:T(8,128)(2,1)S(1)}, u32[]{:S(2)}, u32[]{:S(2)}) collective-permute-start(bf16[512,256]{1,0:T(8,128)(2,1)S(1)} %collective-permute-done.11), channel_id=1, source_target_pairs={{0,14},{1,15},{2,0},{3,1},{4,2},{5,3},{6,4},{7,5},{8,6},{9,7},{10,... | collective-permute-start | bytes 786440 | tf_op jit(solution)/shard_map/ppermute | solution.py:68
  39.8 7.9 %collective-permute-start.14 = (bf16[512,256]{1,0:T(8,128)(2,1)S(1)}, bf16[512,256]{1,0:T(8,128)(2,1)S(1)}, u32[]{:S(2)}, u32[]{:S(2)}) collective-permute-start(bf16[512,256]{1,0:T(8,128)(2,1)S(1)} %broadcast_select_fusion.1), channel_id=1, source_target_pairs={{0,2},{1,3},{2,4},{3,5},{4,6},{5,7},{6,8},{7,9},{8,10},{9,11},{10,... | collective-permute-start | bytes 786440 | tf_op jit(solution)/shard_map/ppermute | solution.py:51
  40.9 38.5 %collective-permute-start.19 = (bf16[4,2,256,512]{3,2,1,0:T(8,128)(2,1)S(1)}, bf16[4,2,256,512]{3,2,1,0:T(8,128)(2,1)S(1)}, u32[]{:S(2)}, u32[]{:S(2)}) collective-permute-start(bf16[4,2,256,512]{3,2,1,0:T(8,128)(2,1)S(1)} %bitcast_dynamic-update-slice_fusion), channel_id=1, source_target_pairs={{0,16},{16,0},{32,48},{48,32},{64,80},{80,64},{96,112},{112,96},{1... | collective-permute-start | bytes 6291464 | tf_op jit(solution)/shard_map/ppermute | solution.py:196
  48.2 2.0 %collective-permute-start.15 = (f32[512,256]{1,0:T(8,128)S(1)}, f32[512,256]{1,0:T(8,128)S(1)}, u32[]{:S(2)}, u32[]{:S(2)}) collective-permute-start(f32[512,256]{1,0:T(8,128)S(1)} %fusion.7), channel_id=1, source_target_pairs={{0,16},{16,0},{32,48},{48,32},{64,80},{80,64},{96,112},{112,96},{1... | collective-permute-start | bytes 1572872 | tf_op jit(solution)/shard_map/ppermute | solution.py:190
  49.0 1.8 %copy-start.1 = (bf16[2,1,1,256,1,1,256]{6,3,5,4,2,1,0:T(8,128)(2,1)S(1)}, bf16[2,1,1,256,1,1,256]{6,3,5,4,2,1,0:T(8,128)(2,1)}, u32[]{:S(2)}) copy-start(bf16[2,1,1,256,1,1,256]{6,3,5,4,2,1,0:T(8,128)(2,1)} %param.6) | copy-start | bytes 786436
  50.6 6.8 %collective-permute-start.16 = (bf16[256,256]{1,0:T(8,128)(2,1)S(1)}, bf16[256,256]{1,0:T(8,128)(2,1)S(1)}, u32[]{:S(2)}, u32[]{:S(2)}) collective-permute-start(bf16[256,256]{1,0:T(8,128)(2,1)S(1)} %slice.223), channel_id=1, source_target_pairs={{0,16},{16,0},{32,48},{48,32},{64,80},{80,64},{96,112},{112,96},{1... | collective-permute-start | bytes 393224 | tf_op jit(solution)/shard_map/ppermute | solution.py:199
  50.8 20.5 %collective-permute-start.17 = (bf16[512,256]{1,0:T(8,128)(2,1)S(1)}, bf16[512,256]{1,0:T(8,128)(2,1)S(1)}, u32[]{:S(2)}, u32[]{:S(2)}) collective-permute-start(bf16[512,256]{1,0:T(8,128)(2,1)S(1)} %fusion.14), channel_id=1, source_target_pairs={{0,2},{1,3},{2,40},{3,41},{4,78},{5,79},{6,108},{7,109},{8,130},{9... | collective-permute-start | bytes 786440 | tf_op jit(solution)/shard_map/ppermute | solution.py:51
  56.0 23.4 %collective-permute-start.18 = (bf16[512,256]{1,0:T(8,128)(2,1)S(1)}, bf16[512,256]{1,0:T(8,128)(2,1)S(1)}, u32[]{:S(2)}, u32[]{:S(2)}) collective-permute-start(bf16[512,256]{1,0:T(8,128)(2,1)S(1)} %fusion.14), channel_id=1, source_target_pairs={{0,10},{1,11},{2,32},{3,33},{4,70},{5,71},{6,100},{7,101},{8,138},... | collective-permute-start | bytes 786440 | tf_op jit(solution)/shard_map/ppermute | solution.py:51
  79.4 9.9 %collective-permute-start.20 = (bf16[512,256]{1,0:T(8,128)(2,1)S(1)}, bf16[512,256]{1,0:T(8,128)(2,1)S(1)}, u32[]{:S(2)}, u32[]{:S(2)}) collective-permute-start(bf16[512,256]{1,0:T(8,128)(2,1)S(1)} %collective-permute-done.17), channel_id=1, source_target_pairs={{0,2},{1,3},{2,4},{3,5},{4,6},{5,7},{6,8},{7,9},{8,10},{9,11},{10,... | collective-permute-start | bytes 786440 | tf_op jit(solution)/shard_map/ppermute | solution.py:64
  79.4 9.9 %collective-permute-start.21 = (bf16[512,256]{1,0:T(8,128)(2,1)S(1)}, bf16[512,256]{1,0:T(8,128)(2,1)S(1)}, u32[]{:S(2)}, u32[]{:S(2)}) collective-permute-start(bf16[512,256]{1,0:T(8,128)(2,1)S(1)} %collective-permute-done.17), channel_id=1, source_target_pairs={{0,14},{1,15},{2,0},{3,1},{4,2},{5,3},{6,4},{7,5},{8,6},{9,7},{10,... | collective-permute-start | bytes 786440 | tf_op jit(solution)/shard_map/ppermute | solution.py:68
  82.6 11.5 %collective-permute-start.24 = (bf16[512,256]{1,0:T(8,128)(2,1)S(1)}, bf16[512,256]{1,0:T(8,128)(2,1)S(1)}, u32[]{:S(2)}, u32[]{:S(2)}) collective-permute-start(bf16[512,256]{1,0:T(8,128)(2,1)S(1)} %collective-permute-done.18), channel_id=1, source_target_pairs={{0,14},{1,15},{2,0},{3,1},{4,2},{5,3},{6,4},{7,5},{8,6},{9,7},{10,... | collective-permute-start | bytes 786440 | tf_op jit(solution)/shard_map/ppermute | solution.py:68
  82.7 15.7 %collective-permute-start.23 = (bf16[512,256]{1,0:T(8,128)(2,1)S(1)}, bf16[512,256]{1,0:T(8,128)(2,1)S(1)}, u32[]{:S(2)}, u32[]{:S(2)}) collective-permute-start(bf16[512,256]{1,0:T(8,128)(2,1)S(1)} %collective-permute-done.18), channel_id=1, source_target_pairs={{0,2},{1,3},{2,4},{3,5},{4,6},{5,7},{6,8},{7,9},{8,10},{9,11},{10,... | collective-permute-start | bytes 786440 | tf_op jit(solution)/shard_map/ppermute | solution.py:64
  89.3 7.9 %collective-permute-start.25 = (bf16[512,256]{1,0:T(8,128)(2,1)S(1)}, bf16[512,256]{1,0:T(8,128)(2,1)S(1)}, u32[]{:S(2)}, u32[]{:S(2)}) collective-permute-start(bf16[512,256]{1,0:T(8,128)(2,1)S(1)} %collective-permute-done.20), channel_id=1, source_target_pairs={{0,2},{1,3},{2,4},{3,5},{4,6},{5,7},{6,8},{7,9},{8,10},{9,11},{10,... | collective-permute-start | bytes 786440 | tf_op jit(solution)/shard_map/ppermute | solution.py:64
  89.9 7.9 %collective-permute-start.26 = (bf16[512,256]{1,0:T(8,128)(2,1)S(1)}, bf16[512,256]{1,0:T(8,128)(2,1)S(1)}, u32[]{:S(2)}, u32[]{:S(2)}) collective-permute-start(bf16[512,256]{1,0:T(8,128)(2,1)S(1)} %collective-permute-done.21), channel_id=1, source_target_pairs={{0,14},{1,15},{2,0},{3,1},{4,2},{5,3},{6,4},{7,5},{8,6},{9,7},{10,... | collective-permute-start | bytes 786440 | tf_op jit(solution)/shard_map/ppermute | solution.py:68
  93.5 7.4 %collective-permute-start.22 = (bf16[2,256,256]{2,1,0:T(8,128)(2,1)S(1)}, bf16[2,256,256]{2,1,0:T(8,128)(2,1)S(1)}, u32[]{:S(2)}, u32[]{:S(2)}) collective-permute-start(bf16[2,256,256]{2,1,0:T(8,128)(2,1)S(1)} %pad_maximum_fusion.2), channel_id=1, source_target_pairs={{0,1},{1,0},{2,3},{3,2},{4,5},{5,4},{6,7},{7,6},{8,9},{9,8},{10,11... | collective-permute-start | bytes 786440 | tf_op jit(solution)/shard_map/ppermute | solution.py:107
  101.0 5.1 %collective-permute-start.27 = (bf16[256,256]{1,0:T(8,128)(2,1)S(1)}, bf16[256,256]{1,0:T(8,128)(2,1)S(1)}, u32[]{:S(2)}, u32[]{:S(2)}) collective-permute-start(bf16[256,256]{1,0:T(8,128)(2,1)S(1)} %fusion.15), channel_id=1, source_target_pairs={{0,1},{1,0},{2,3},{3,2},{4,5},{5,4},{6,7},{7,6},{8,9},{9,8},{10,11... | collective-permute-start | bytes 393224 | tf_op jit(solution)/shard_map/ppermute | solution.py:131

commit v7 on v5

--- a/solution.py
+++ b/solution.py
@@ -102,7 +102,7 @@
     *one, total = tie(*one, total)
     two = up(one[0]), down(one[1])
     swapped = []
-    for block, after in zip(beside, one):
+    for block, after in zip(beside, (one[0], three[0])):
         block, _ = tie(block, after)
         swapped.append(lax.ppermute(block, "pcol", SWAP))
     total = add(total, NZ // 2, opposite)

time: 102 us -> 102 us (level)
  transfers between devices with their start and end apart: 29 -> 29, of which waited for: 13 -> 14; matrix products, arithmetic and copies ran while one was open for 15% -> 15% of each run, Pallas kernels for 0% -> 0%
where the time goes in v7:
time: 102 us; the launch traced here: 101 us
  starting transfers between devices  47.1 us (46%)
  waiting for transfers between devices  35.1 us (34%)
  matrix products  8.17 us (8%)
  other arithmetic  6.68 us (7%)
  local copies, waits for them, and re-layouts  2.34 us (2%)
  between operations  1.74 us (2%)
    ppermute x5, waiting for transfers between devices, move(): return lax.ppermute(block, ('prow', 'pcol'), pairs)  17.9 us
    ppermute x6, starting transfers between devices, down(): return lax.ppermute(block, 'pcol', DOWN)  17.1 us
    ppermute x6, waiting for transfers between devices, up(): return lax.ppermute(block, 'pcol', UP)  9.83 us
    ppermute x5, starting transfers between devices, move(): return lax.ppermute(block, ('prow', 'pcol'), pairs)  9.55 us
    ppermute x2, starting transfers between devices, swap(): return lax.ppermute(block, 'pcol', SWAP)  4.69 us
    dot_general x16, matrix products, add_inner(): lax.dot_general(u_rows(panel, owner), rows, (((0,), (0,)), ((), ())), pre...  4.52 us
    ppermute x6, starting transfers between devices, up(): return lax.ppermute(block, 'pcol', UP)  4.07 us
    dot_general x16, matrix products, add_product(): jnp.dot(block, cols, preferred_element_type=jnp.float32)  3.65 us
  transfers between devices with their start and end apart: 29, of which 14 were waited for; matrix products, arithmetic and copies ran while one was open for 15% of the time, Pallas kernels for 0%

profile of v7, /device:TPU:6, one launch (start us, length us, event | category | flops | bytes accessed | tf_op | source)
XLA Modules:
  0.0 101.2 jit_solution(16727117961490896749)
XLA Ops:
  0.7 1.0 %select_bitcast_fusion.6 = (bf16[256,256]{1,0:T(8,128)(2,1)S(1)}, bf16[256,256]{1,0:T(8,128)(2,1)S(1)}) fusion(pred[]{:T(512)S(6)} %eq.185, bf16[2,1,1,256,1,1,256]{6,3,5,4,2,1,0:T(8,128)(2,1)} %param.4), kind=kLoop, calls=%fused_computation.144 | loop fusion | flops 131072 | bytes 524289 | tf_op jit(solution)/shard_map/jit(_where)/select_n | solution.py:134
  1.7 0.7 collective-permute-start
  2.4 2.9 %collective-permute-start.1 = (bf16[256,256]{1,0:T(8,128)(2,1)S(1)}, bf16[256,256]{1,0:T(8,128)(2,1)S(1)}, u32[]{:S(2)}, u32[]{:S(2)}) collective-permute-start(bf16[256,256]{1,0:T(8,128)(2,1)S(1)} %get-tuple-element.47), channel_id=1, source_target_pairs={{0,1},{1,17},{2,3},{3,19},{4,5},{5,21},{6,7},{7,23},{8,9},{9,25},{... | collective-permute-start | bytes 393224 | tf_op jit(solution)/shard_map/ppermute | solution.py:51
  5.3 0.8 dynamic_slice.75
  6.1 0.9 compare_reduce_fusion
  7.1 1.0 select_bitcast_fusion.7
  8.1 2.2 %collective-permute-start.2 = (bf16[256,256]{1,0:T(8,128)(2,1)S(1)}, bf16[256,256]{1,0:T(8,128)(2,1)S(1)}, u32[]{:S(2)}, u32[]{:S(2)}) collective-permute-start(bf16[256,256]{1,0:T(8,128)(2,1)S(1)} %select_bitcast_fusion.7), channel_id=1, source_target_pairs={{0,1},{1,0},{2,3},{3,2},{4,5},{5,4},{6,7},{7,6},{8,9},{9,8},{10,11... | collective-permute-start | bytes 393224 | tf_op jit(solution)/shard_map/ppermute | solution.py:131
  10.5 2.0 %collective-permute-start.8 = (bf16[512,256]{1,0:T(8,128)(2,1)S(1)}, bf16[512,256]{1,0:T(8,128)(2,1)S(1)}, u32[]{:S(2)}, u32[]{:S(2)}) collective-permute-start(bf16[512,256]{1,0:T(8,128)(2,1)S(1)} %bitcast_select_fusion), channel_id=1, source_target_pairs={{0,2},{1,3},{2,4},{3,5},{4,6},{5,7},{6,8},{7,9},{8,10},{9,11},{10,... | collective-permute-start | bytes 786440 | tf_op jit(solution)/shard_map/ppermute | solution.py:64
  12.5 4.0 %collective-permute-start.9 = (bf16[512,256]{1,0:T(8,128)(2,1)S(1)}, bf16[512,256]{1,0:T(8,128)(2,1)S(1)}, u32[]{:S(2)}, u32[]{:S(2)}) collective-permute-start(bf16[512,256]{1,0:T(8,128)(2,1)S(1)} %bitcast_select_fusion), channel_id=1, source_target_pairs={{0,14},{1,15},{2,0},{3,1},{4,2},{5,3},{6,4},{7,5},{8,6},{9,7},{10,... | collective-permute-start | bytes 786440 | tf_op jit(solution)/shard_map/ppermute | solution.py:68
  16.6 1.5 %collective-permute-start.4 = (bf16[256,512]{1,0:T(8,128)(2,1)S(1)}, bf16[256,512]{1,0:T(8,128)(2,1)}, u32[]{:S(2)}, u32[]{:S(2)}) collective-permute-start(bf16[256,512]{1,0:T(8,128)(2,1)S(1)} %get-tuple-element.45), channel_id=1, source_target_pairs={{0,64},{16,80},{32,96},{48,112},{64,0},{80,16},{96,32},{112,48},{1... | collective-permute-start | bytes 786440 | tf_op jit(solution)/shard_map/ppermute | solution.py:154
  18.1 2.7 %collective-permute-start.3 = (bf16[256,512]{1,0:T(8,128)(2,1)S(1)}, bf16[256,512]{1,0:T(8,128)(2,1)S(1)}, u32[]{:S(2)}, u32[]{:S(2)}) collective-permute-start(bf16[256,512]{1,0:T(8,128)(2,1)S(1)} %get-tuple-element.45), channel_id=1, source_target_pairs={{0,128},{16,144},{32,160},{48,176},{64,192},{80,208},{96,224},{112... | collective-permute-start | bytes 786440 | tf_op jit(solution)/shard_map/ppermute | solution.py:156
  20.8 1.5 %collective-permute-done.8 = bf16[512,256]{1,0:T(8,128)(2,1)S(1)} collective-permute-done((bf16[512,256]{1,0:T(8,128)(2,1)S(1)}, bf16[512,256]{1,0:T(8,128)(2,1)S(1)}, u32[]{:S(2)}, u32[]{:S(2)}) %collective-permute-start.8) | collective-permute-done | bytes 262176 | tf_op jit(solution)/shard_map/ppermute | solution.py:64
  22.3 3.2 %collective-permute-start.11 = (bf16[512,256]{1,0:T(8,128)(2,1)S(1)}, bf16[512,256]{1,0:T(8,128)(2,1)S(1)}, u32[]{:S(2)}, u32[]{:S(2)}) collective-permute-start(bf16[512,256]{1,0:T(8,128)(2,1)S(1)} %collective-permute-done.9), channel_id=1, source_target_pairs={{0,14},{1,15},{2,0},{3,1},{4,2},{5,3},{6,4},{7,5},{8,6},{9,7},{10,... | collective-permute-start | bytes 786440 | tf_op jit(solution)/shard_map/ppermute | solution.py:68
  25.6 2.9 %collective-permute-start.5 = (bf16[256,512]{1,0:T(8,128)(2,1)}, bf16[256,512]{1,0:T(8,128)(2,1)S(1)}, u32[]{:S(2)}, u32[]{:S(2)}) collective-permute-start(bf16[256,512]{1,0:T(8,128)(2,1)} %collective-permute-done.4), channel_id=1, source_target_pairs={{0,128},{16,144},{32,160},{48,176},{64,192},{80,208},{96,224},{112... | collective-permute-start | bytes 786440 | tf_op jit(solution)/shard_map/ppermute | solution.py:161
  28.6 0.6 collective-permute-start.6
  29.1 1.5 %collective-permute-start.7 = (bf16[2,256,512]{2,1,0:T(8,128)(2,1)S(1)}, bf16[2,256,512]{2,1,0:T(8,128)(2,1)S(1)}, u32[]{:S(2)}, u32[]{:S(2)}) collective-permute-start(bf16[2,256,512]{2,1,0:T(8,128)(2,1)S(1)} %get-tuple-element.40), channel_id=1, source_target_pairs={{0,96},{16,112},{32,0},{48,16},{64,32},{80,48},{96,64},{112,80},{1... | collective-permute-start | bytes 1572872 | tf_op jit(solution)/shard_map/ppermute | solution.py:154
  31.0 3.4 %collective-permute-start.13 = (bf16[512,256]{1,0:T(8,128)(2,1)S(1)}, bf16[512,256]{1,0:T(8,128)(2,1)S(1)}, u32[]{:S(2)}, u32[]{:S(2)}) collective-permute-start(bf16[512,256]{1,0:T(8,128)(2,1)S(1)} %collective-permute-done.11), channel_id=1, source_target_pairs={{0,14},{1,15},{2,0},{3,1},{4,2},{5,3},{6,4},{7,5},{8,6},{9,7},{10,... | collective-permute-start | bytes 786440 | tf_op jit(solution)/shard_map/ppermute | solution.py:68
  34.3 1.0 bitcast_dynamic-update-slice_fusion.3
  35.3 3.2 %collective-permute-done.12 = bf16[512,256]{1,0:T(8,128)(2,1)S(1)} collective-permute-done((bf16[512,256]{1,0:T(8,128)(2,1)S(1)}, bf16[512,256]{1,0:T(8,128)(2,1)S(1)}, u32[]{:S(2)}, u32[]{:S(2)}) %collective-permute-start.12) | collective-permute-done | bytes 262176 | tf_op jit(solution)/shard_map/ppermute | solution.py:64
  38.7 1.9 %collective-permute-done.6 = bf16[2,256,512]{2,1,0:T(8,128)(2,1)S(1)} collective-permute-done((bf16[2,256,512]{2,1,0:T(8,128)(2,1)S(1)}, bf16[2,256,512]{2,1,0:T(8,128)(2,1)S(1)}, u32[]{:S(2)}, u32[]{:S(2)}) %collective-permute-start.6) | collective-permute-done | bytes 524320 | tf_op jit(solution)/shard_map/ppermute | solution.py:154
  40.6 1.4 %collective-permute-done.7 = bf16[2,256,512]{2,1,0:T(8,128)(2,1)S(1)} collective-permute-done((bf16[2,256,512]{2,1,0:T(8,128)(2,1)S(1)}, bf16[2,256,512]{2,1,0:T(8,128)(2,1)S(1)}, u32[]{:S(2)}, u32[]{:S(2)}) %collective-permute-start.7) | collective-permute-done | bytes 524320 | tf_op jit(solution)/shard_map/ppermute | solution.py:154
  42.7 0.3 collective-permute-start.19
  44.8 1.6 %collective-permute-done.14 = bf16[512,256]{1,0:T(8,128)(2,1)S(1)} collective-permute-done((bf16[512,256]{1,0:T(8,128)(2,1)S(1)}, bf16[512,256]{1,0:T(8,128)(2,1)S(1)}, u32[]{:S(2)}, u32[]{:S(2)}) %collective-permute-start.14) | collective-permute-done | bytes 262176 | tf_op jit(solution)/shard_map/ppermute | solution.py:51
  47.7 1.2 %collective-permute-done.15 = f32[512,256]{1,0:T(8,128)S(1)} collective-permute-done((f32[512,256]{1,0:T(8,128)S(1)}, f32[512,256]{1,0:T(8,128)S(1)}, u32[]{:S(2)}, u32[]{:S(2)}) %collective-permute-start.15) | collective-permute-done | bytes 524320 | tf_op jit(solution)/shard_map/ppermute | solution.py:190
  49.1 5.9 %collective-permute-start.17 = (bf16[512,256]{1,0:T(8,128)(2,1)S(1)}, bf16[512,256]{1,0:T(8,128)(2,1)S(1)}, u32[]{:S(2)}, u32[]{:S(2)}) collective-permute-start(bf16[512,256]{1,0:T(8,128)(2,1)S(1)} %fusion.14), channel_id=1, source_target_pairs={{0,2},{1,3},{2,40},{3,41},{4,78},{5,79},{6,108},{7,109},{8,130},{9... | collective-permute-start | bytes 786440 | tf_op jit(solution)/shard_map/ppermute | solution.py:51
  55.8 0.7 collective-permute-done.16
  56.5 10.7 %collective-permute-done.17 = bf16[512,256]{1,0:T(8,128)(2,1)S(1)} collective-permute-done((bf16[512,256]{1,0:T(8,128)(2,1)S(1)}, bf16[512,256]{1,0:T(8,128)(2,1)S(1)}, u32[]{:S(2)}, u32[]{:S(2)}) %collective-permute-start.17) | collective-permute-done | bytes 262176 | tf_op jit(solution)/shard_map/ppermute | solution.py:51
  67.2 5.6 %collective-permute-done.18 = bf16[512,256]{1,0:T(8,128)(2,1)S(1)} collective-permute-done((bf16[512,256]{1,0:T(8,128)(2,1)S(1)}, bf16[512,256]{1,0:T(8,128)(2,1)S(1)}, u32[]{:S(2)}, u32[]{:S(2)}) %collective-permute-start.18) | collective-permute-done | bytes 262176 | tf_op jit(solution)/shard_map/ppermute | solution.py:51
  72.8 3.2 %collective-permute-start.21 = (bf16[512,256]{1,0:T(8,128)(2,1)S(1)}, bf16[512,256]{1,0:T(8,128)(2,1)S(1)}, u32[]{:S(2)}, u32[]{:S(2)}) collective-permute-start(bf16[512,256]{1,0:T(8,128)(2,1)S(1)} %collective-permute-done.17), channel_id=1, source_target_pairs={{0,14},{1,15},{2,0},{3,1},{4,2},{5,3},{6,4},{7,5},{8,6},{9,7},{10,... | collective-permute-start | bytes 786440 | tf_op jit(solution)/shard_map/ppermute | solution.py:68
  76.1 2.0 %collective-permute-start.23 = (bf16[512,256]{1,0:T(8,128)(2,1)S(1)}, bf16[512,256]{1,0:T(8,128)(2,1)S(1)}, u32[]{:S(2)}, u32[]{:S(2)}) collective-permute-start(bf16[512,256]{1,0:T(8,128)(2,1)S(1)} %collective-permute-done.18), channel_id=1, source_target_pairs={{0,2},{1,3},{2,4},{3,5},{4,6},{5,7},{6,8},{7,9},{8,10},{9,11},{10,... | collective-permute-start | bytes 786440 | tf_op jit(solution)/shard_map/ppermute | solution.py:64
  78.1 1.7 %broadcast_select_fusion = bf16[4,2,256,512]{3,2,1,0:T(8,128)(2,1)S(1)} fusion(bf16[4,2,256,512]{3,2,1,0:T(8,128)(2,1)} %collective-permute-done.19, pred[]{:T(512)S(6)} %ge.3), kind=kLoop, calls=%fused_computation | loop fusion | flops 1048576 | bytes 4194305 | tf_op jit(solution)/shard_map/jit(_where)/select_n | solution.py:198
  79.8 0.3 fusion.44
  80.1 0.3 fusion.42
  80.4 0.3 fusion.40
  80.9 2.4 %collective-permute-done.20 = bf16[512,256]{1,0:T(8,128)(2,1)S(1)} collective-permute-done((bf16[512,256]{1,0:T(8,128)(2,1)S(1)}, bf16[512,256]{1,0:T(8,128)(2,1)S(1)}, u32[]{:S(2)}, u32[]{:S(2)}) %collective-permute-start.20) | collective-permute-done | bytes 262176 | tf_op jit(solution)/shard_map/ppermute | solution.py:64
  83.3 3.2 %collective-permute-start.26 = (bf16[512,256]{1,0:T(8,128)(2,1)S(1)}, bf16[512,256]{1,0:T(8,128)(2,1)S(1)}, u32[]{:S(2)}, u32[]{:S(2)}) collective-permute-start(bf16[512,256]{1,0:T(8,128)(2,1)S(1)} %collective-permute-done.21), channel_id=1, source_target_pairs={{0,14},{1,15},{2,0},{3,1},{4,2},{5,3},{6,4},{7,5},{8,6},{9,7},{10,... | collective-permute-start | bytes 786440 | tf_op jit(solution)/shard_map/ppermute | solution.py:68
  86.8 0.3 fusion.25
  87.1 1.8 %collective-permute-done.23 = bf16[512,256]{1,0:T(8,128)(2,1)S(1)} collective-permute-done((bf16[512,256]{1,0:T(8,128)(2,1)S(1)}, bf16[512,256]{1,0:T(8,128)(2,1)S(1)}, u32[]{:S(2)}, u32[]{:S(2)}) %collective-permute-start.23) | collective-permute-done | bytes 262176 | tf_op jit(solution)/shard_map/ppermute | solution.py:64
  88.9 1.8 %collective-permute-start.27 = (bf16[256,256]{1,0:T(8,128)(2,1)S(1)}, bf16[256,256]{1,0:T(8,128)(2,1)S(1)}, u32[]{:S(2)}, u32[]{:S(2)}) collective-permute-start(bf16[256,256]{1,0:T(8,128)(2,1)S(1)} %select_bitcast_fusion.2), channel_id=1, source_target_pairs={{0,1},{1,0},{2,3},{3,2},{4,5},{5,4},{6,7},{7,6},{8,9},{9,8},{10,11... | collective-permute-start | bytes 393224 | tf_op jit(solution)/shard_map/ppermute | solution.py:107
  91.7 0.3 fusion.20
  92.0 0.9 collective-permute-done.25
  93.8 0.3 fusion.16
  94.0 0.4 fusion.5
  94.4 0.4 fusion.2
  94.9 2.4 %collective-permute-start.28 = (bf16[256,256]{1,0:T(8,128)(2,1)S(1)}, bf16[256,256]{1,0:T(8,128)(2,1)S(1)}, u32[]{:S(2)}, u32[]{:S(2)}) collective-permute-start(bf16[256,256]{1,0:T(8,128)(2,1)S(1)} %subtract_convert_fusion), channel_id=1, source_target_pairs={{0,1},{1,0},{2,3},{3,2},{4,5},{5,4},{6,7},{7,6},{8,9},{9,8},{10,11... | collective-permute-start | bytes 393224 | tf_op jit(solution)/shard_map/ppermute | solution.py:131
  97.4 0.7 maximum_bitcast_fusion
  98.1 2.2 %collective-permute-done.28 = bf16[256,256]{1,0:T(8,128)(2,1)S(1)} collective-permute-done((bf16[256,256]{1,0:T(8,128)(2,1)S(1)}, bf16[256,256]{1,0:T(8,128)(2,1)S(1)}, u32[]{:S(2)}, u32[]{:S(2)}) %collective-permute-start.28) | collective-permute-done | bytes 131104 | tf_op jit(solution)/shard_map/ppermute | solution.py:131
  100.4 0.7 maximum_bitcast_fusion.1
  (76 shorter events, 7.8 us)
Async XLA Ops:
  0.6 15.9 %copy-start = (bf16[2,1,1,256,1,1,256]{6,3,5,4,2,1,0:T(8,128)(2,1)S(1)}, bf16[2,1,1,256,1,1,256]{6,3,5,4,2,1,0:T(8,128)(2,1)}, u32[]{:S(2)}) copy-start(bf16[2,1,1,256,1,1,256]{6,3,5,4,2,1,0:T(8,128)(2,1)} %param.5) | copy-start | bytes 786436
  1.7 6.4 %collective-permute-start = (bf16[256,256]{1,0:T(8,128)(2,1)S(1)}, bf16[256,256]{1,0:T(8,128)(2,1)S(1)}, u32[]{:S(2)}, u32[]{:S(2)}) collective-permute-start(bf16[256,256]{1,0:T(8,128)(2,1)S(1)} %get-tuple-element.46), channel_id=1, source_target_pairs={{0,0},{1,16},{2,2},{3,18},{4,4},{5,20},{6,6},{7,22},{8,8},{9,24},{... | collective-permute-start | bytes 393224 | tf_op jit(solution)/shard_map/ppermute | solution.py:51
  2.4 7.9 %collective-permute-start.1 = (bf16[256,256]{1,0:T(8,128)(2,1)S(1)}, bf16[256,256]{1,0:T(8,128)(2,1)S(1)}, u32[]{:S(2)}, u32[]{:S(2)}) collective-permute-start(bf16[256,256]{1,0:T(8,128)(2,1)S(1)} %get-tuple-element.47), channel_id=1, source_target_pairs={{0,1},{1,17},{2,3},{3,19},{4,5},{5,21},{6,7},{7,23},{8,9},{9,25},{... | collective-permute-start | bytes 393224 | tf_op jit(solution)/shard_map/ppermute | solution.py:51
  8.1 8.4 %collective-permute-start.2 = (bf16[256,256]{1,0:T(8,128)(2,1)S(1)}, bf16[256,256]{1,0:T(8,128)(2,1)S(1)}, u32[]{:S(2)}, u32[]{:S(2)}) collective-permute-start(bf16[256,256]{1,0:T(8,128)(2,1)S(1)} %select_bitcast_fusion.7), channel_id=1, source_target_pairs={{0,1},{1,0},{2,3},{3,2},{4,5},{5,4},{6,7},{7,6},{8,9},{9,8},{10,11... | collective-permute-start | bytes 393224 | tf_op jit(solution)/shard_map/ppermute | solution.py:131
  10.5 11.8 %collective-permute-start.8 = (bf16[512,256]{1,0:T(8,128)(2,1)S(1)}, bf16[512,256]{1,0:T(8,128)(2,1)S(1)}, u32[]{:S(2)}, u32[]{:S(2)}) collective-permute-start(bf16[512,256]{1,0:T(8,128)(2,1)S(1)} %bitcast_select_fusion), channel_id=1, source_target_pairs={{0,2},{1,3},{2,4},{3,5},{4,6},{5,7},{6,8},{7,9},{8,10},{9,11},{10,... | collective-permute-start | bytes 786440 | tf_op jit(solution)/shard_map/ppermute | solution.py:64
  12.5 9.8 %collective-permute-start.9 = (bf16[512,256]{1,0:T(8,128)(2,1)S(1)}, bf16[512,256]{1,0:T(8,128)(2,1)S(1)}, u32[]{:S(2)}, u32[]{:S(2)}) collective-permute-start(bf16[512,256]{1,0:T(8,128)(2,1)S(1)} %bitcast_select_fusion), channel_id=1, source_target_pairs={{0,14},{1,15},{2,0},{3,1},{4,2},{5,3},{6,4},{7,5},{8,6},{9,7},{10,... | collective-permute-start | bytes 786440 | tf_op jit(solution)/shard_map/ppermute | solution.py:68
  16.6 9.0 %collective-permute-start.4 = (bf16[256,512]{1,0:T(8,128)(2,1)S(1)}, bf16[256,512]{1,0:T(8,128)(2,1)}, u32[]{:S(2)}, u32[]{:S(2)}) collective-permute-start(bf16[256,512]{1,0:T(8,128)(2,1)S(1)} %get-tuple-element.45), channel_id=1, source_target_pairs={{0,64},{16,80},{32,96},{48,112},{64,0},{80,16},{96,32},{112,48},{1... | collective-permute-start | bytes 786440 | tf_op jit(solution)/shard_map/ppermute | solution.py:154
  18.1 10.4 %collective-permute-start.3 = (bf16[256,512]{1,0:T(8,128)(2,1)S(1)}, bf16[256,512]{1,0:T(8,128)(2,1)S(1)}, u32[]{:S(2)}, u32[]{:S(2)}) collective-permute-start(bf16[256,512]{1,0:T(8,128)(2,1)S(1)} %get-tuple-element.45), channel_id=1, source_target_pairs={{0,128},{16,144},{32,160},{48,176},{64,192},{80,208},{96,224},{112... | collective-permute-start | bytes 786440 | tf_op jit(solution)/shard_map/ppermute | solution.py:156
  22.3 8.6 %collective-permute-start.10 = (bf16[512,256]{1,0:T(8,128)(2,1)S(1)}, bf16[512,256]{1,0:T(8,128)(2,1)S(1)}, u32[]{:S(2)}, u32[]{:S(2)}) collective-permute-start(bf16[512,256]{1,0:T(8,128)(2,1)S(1)} %collective-permute-done.8), channel_id=1, source_target_pairs={{0,2},{1,3},{2,4},{3,5},{4,6},{5,7},{6,8},{7,9},{8,10},{9,11},{10,... | collective-permute-start | bytes 786440 | tf_op jit(solution)/shard_map/ppermute | solution.py:64
  22.3 8.7 %collective-permute-start.11 = (bf16[512,256]{1,0:T(8,128)(2,1)S(1)}, bf16[512,256]{1,0:T(8,128)(2,1)S(1)}, u32[]{:S(2)}, u32[]{:S(2)}) collective-permute-start(bf16[512,256]{1,0:T(8,128)(2,1)S(1)} %collective-permute-done.9), channel_id=1, source_target_pairs={{0,14},{1,15},{2,0},{3,1},{4,2},{5,3},{6,4},{7,5},{8,6},{9,7},{10,... | collective-permute-start | bytes 786440 | tf_op jit(solution)/shard_map/ppermute | solution.py:68
  25.6 9.7 %collective-permute-start.5 = (bf16[256,512]{1,0:T(8,128)(2,1)}, bf16[256,512]{1,0:T(8,128)(2,1)S(1)}, u32[]{:S(2)}, u32[]{:S(2)}) collective-permute-start(bf16[256,512]{1,0:T(8,128)(2,1)} %collective-permute-done.4), channel_id=1, source_target_pairs={{0,128},{16,144},{32,160},{48,176},{64,192},{80,208},{96,224},{112... | collective-permute-start | bytes 786440 | tf_op jit(solution)/shard_map/ppermute | solution.py:161
  28.6 12.0 %collective-permute-start.6 = (bf16[2,256,512]{2,1,0:T(8,128)(2,1)S(1)}, bf16[2,256,512]{2,1,0:T(8,128)(2,1)S(1)}, u32[]{:S(2)}, u32[]{:S(2)}) collective-permute-start(bf16[2,256,512]{2,1,0:T(8,128)(2,1)S(1)} %get-tuple-element.40), channel_id=1, source_target_pairs={{0,32},{16,48},{32,64},{48,80},{64,96},{80,112},{96,0},{112,16},{1... | collective-permute-start | bytes 1572872 | tf_op jit(solution)/shard_map/ppermute | solution.py:154
  29.1 12.9 %collective-permute-start.7 = (bf16[2,256,512]{2,1,0:T(8,128)(2,1)S(1)}, bf16[2,256,512]{2,1,0:T(8,128)(2,1)S(1)}, u32[]{:S(2)}, u32[]{:S(2)}) collective-permute-start(bf16[2,256,512]{2,1,0:T(8,128)(2,1)S(1)} %get-tuple-element.40), channel_id=1, source_target_pairs={{0,96},{16,112},{32,0},{48,16},{64,32},{80,48},{96,64},{112,80},{1... | collective-permute-start | bytes 1572872 | tf_op jit(solution)/shard_map/ppermute | solution.py:154
  30.9 7.7 %collective-permute-start.12 = (bf16[512,256]{1,0:T(8,128)(2,1)S(1)}, bf16[512,256]{1,0:T(8,128)(2,1)S(1)}, u32[]{:S(2)}, u32[]{:S(2)}) collective-permute-start(bf16[512,256]{1,0:T(8,128)(2,1)S(1)} %collective-permute-done.10), channel_id=1, source_target_pairs={{0,2},{1,3},{2,4},{3,5},{4,6},{5,7},{6,8},{7,9},{8,10},{9,11},{10,... | collective-permute-start | bytes 786440 | tf_op jit(solution)/shard_map/ppermute | solution.py:64
  31.0 7.6 %collective-permute-start.13 = (bf16[512,256]{1,0:T(8,128)(2,1)S(1)}, bf16[512,256]{1,0:T(8,128)(2,1)S(1)}, u32[]{:S(2)}, u32[]{:S(2)}) collective-permute-start(bf16[512,256]{1,0:T(8,128)(2,1)S(1)} %collective-permute-done.11), channel_id=1, source_target_pairs={{0,14},{1,15},{2,0},{3,1},{4,2},{5,3},{6,4},{7,5},{8,6},{9,7},{10,... | collective-permute-start | bytes 786440 | tf_op jit(solution)/shard_map/ppermute | solution.py:68
  38.6 7.8 %collective-permute-start.14 = (bf16[512,256]{1,0:T(8,128)(2,1)S(1)}, bf16[512,256]{1,0:T(8,128)(2,1)S(1)}, u32[]{:S(2)}, u32[]{:S(2)}) collective-permute-start(bf16[512,256]{1,0:T(8,128)(2,1)S(1)} %broadcast_select_fusion.1), channel_id=1, source_target_pairs={{0,2},{1,3},{2,4},{3,5},{4,6},{5,7},{6,8},{7,9},{8,10},{9,11},{10,... | collective-permute-start | bytes 786440 | tf_op jit(solution)/shard_map/ppermute | solution.py:51
  42.7 30.1 %collective-permute-start.19 = (bf16[4,2,256,512]{3,2,1,0:T(8,128)(2,1)S(1)}, bf16[4,2,256,512]{3,2,1,0:T(8,128)(2,1)}, u32[]{:S(2)}, u32[]{:S(2)}) collective-permute-start(bf16[4,2,256,512]{3,2,1,0:T(8,128)(2,1)S(1)} %bitcast_dynamic-update-slice_fusion), channel_id=1, source_target_pairs={{0,16},{16,0},{32,48},{48,32},{64,80},{80,64},{96,112},{112,96},{1... | collective-permute-start | bytes 6291464 | tf_op jit(solution)/shard_map/ppermute | solution.py:196
  46.8 2.0 %collective-permute-start.15 = (f32[512,256]{1,0:T(8,128)S(1)}, f32[512,256]{1,0:T(8,128)S(1)}, u32[]{:S(2)}, u32[]{:S(2)}) collective-permute-start(f32[512,256]{1,0:T(8,128)S(1)} %fusion.7), channel_id=1, source_target_pairs={{0,16},{16,0},{32,48},{48,32},{64,80},{80,64},{96,112},{112,96},{1... | collective-permute-start | bytes 1572872 | tf_op jit(solution)/shard_map/ppermute | solution.py:190
  47.6 7.5 %copy-start.1 = (bf16[2,1,1,256,1,1,256]{6,3,5,4,2,1,0:T(8,128)(2,1)S(1)}, bf16[2,1,1,256,1,1,256]{6,3,5,4,2,1,0:T(8,128)(2,1)}, u32[]{:S(2)}) copy-start(bf16[2,1,1,256,1,1,256]{6,3,5,4,2,1,0:T(8,128)(2,1)} %param.6) | copy-start | bytes 786436
  49.1 18.1 %collective-permute-start.17 = (bf16[512,256]{1,0:T(8,128)(2,1)S(1)}, bf16[512,256]{1,0:T(8,128)(2,1)S(1)}, u32[]{:S(2)}, u32[]{:S(2)}) collective-permute-start(bf16[512,256]{1,0:T(8,128)(2,1)S(1)} %fusion.14), channel_id=1, source_target_pairs={{0,2},{1,3},{2,40},{3,41},{4,78},{5,79},{6,108},{7,109},{8,130},{9... | collective-permute-start | bytes 786440 | tf_op jit(solution)/shard_map/ppermute | solution.py:51
  55.0 17.8 %collective-permute-start.18 = (bf16[512,256]{1,0:T(8,128)(2,1)S(1)}, bf16[512,256]{1,0:T(8,128)(2,1)S(1)}, u32[]{:S(2)}, u32[]{:S(2)}) collective-permute-start(bf16[512,256]{1,0:T(8,128)(2,1)S(1)} %fusion.14), channel_id=1, source_target_pairs={{0,10},{1,11},{2,32},{3,33},{4,70},{5,71},{6,100},{7,101},{8,138},... | collective-permute-start | bytes 786440 | tf_op jit(solution)/shard_map/ppermute | solution.py:51
  55.0 1.4 %collective-permute-start.16 = (bf16[256,256]{1,0:T(8,128)(2,1)S(1)}, bf16[256,256]{1,0:T(8,128)(2,1)S(1)}, u32[]{:S(2)}, u32[]{:S(2)}) collective-permute-start(bf16[256,256]{1,0:T(8,128)(2,1)S(1)} %slice.215), channel_id=1, source_target_pairs={{0,16},{16,0},{32,48},{48,32},{64,80},{80,64},{96,112},{112,96},{1... | collective-permute-start | bytes 393224 | tf_op jit(solution)/shard_map/ppermute | solution.py:199
  72.8 10.5 %collective-permute-start.20 = (bf16[512,256]{1,0:T(8,128)(2,1)S(1)}, bf16[512,256]{1,0:T(8,128)(2,1)S(1)}, u32[]{:S(2)}, u32[]{:S(2)}) collective-permute-start(bf16[512,256]{1,0:T(8,128)(2,1)S(1)} %collective-permute-done.17), channel_id=1, source_target_pairs={{0,2},{1,3},{2,4},{3,5},{4,6},{5,7},{6,8},{7,9},{8,10},{9,11},{10,... | collective-permute-start | bytes 786440 | tf_op jit(solution)/shard_map/ppermute | solution.py:64
  72.8 10.5 %collective-permute-start.21 = (bf16[512,256]{1,0:T(8,128)(2,1)S(1)}, bf16[512,256]{1,0:T(8,128)(2,1)S(1)}, u32[]{:S(2)}, u32[]{:S(2)}) collective-permute-start(bf16[512,256]{1,0:T(8,128)(2,1)S(1)} %collective-permute-done.17), channel_id=1, source_target_pairs={{0,14},{1,15},{2,0},{3,1},{4,2},{5,3},{6,4},{7,5},{8,6},{9,7},{10,... | collective-permute-start | bytes 786440 | tf_op jit(solution)/shard_map/ppermute | solution.py:68
  76.1 15.4 %collective-permute-start.24 = (bf16[512,256]{1,0:T(8,128)(2,1)S(1)}, bf16[512,256]{1,0:T(8,128)(2,1)S(1)}, u32[]{:S(2)}, u32[]{:S(2)}) collective-permute-start(bf16[512,256]{1,0:T(8,128)(2,1)S(1)} %collective-permute-done.18), channel_id=1, source_target_pairs={{0,14},{1,15},{2,0},{3,1},{4,2},{5,3},{6,4},{7,5},{8,6},{9,7},{10,... | collective-permute-start | bytes 786440 | tf_op jit(solution)/shard_map/ppermute | solution.py:68
  76.1 12.8 %collective-permute-start.23 = (bf16[512,256]{1,0:T(8,128)(2,1)S(1)}, bf16[512,256]{1,0:T(8,128)(2,1)S(1)}, u32[]{:S(2)}, u32[]{:S(2)}) collective-permute-start(bf16[512,256]{1,0:T(8,128)(2,1)S(1)} %collective-permute-done.18), channel_id=1, source_target_pairs={{0,2},{1,3},{2,4},{3,5},{4,6},{5,7},{6,8},{7,9},{8,10},{9,11},{10,... | collective-permute-start | bytes 786440 | tf_op jit(solution)/shard_map/ppermute | solution.py:64
  83.3 9.6 %collective-permute-start.25 = (bf16[512,256]{1,0:T(8,128)(2,1)S(1)}, bf16[512,256]{1,0:T(8,128)(2,1)S(1)}, u32[]{:S(2)}, u32[]{:S(2)}) collective-permute-start(bf16[512,256]{1,0:T(8,128)(2,1)S(1)} %collective-permute-done.20), channel_id=1, source_target_pairs={{0,2},{1,3},{2,4},{3,5},{4,6},{5,7},{6,8},{7,9},{8,10},{9,11},{10,... | collective-permute-start | bytes 786440 | tf_op jit(solution)/shard_map/ppermute | solution.py:64
  83.3 10.2 %collective-permute-start.26 = (bf16[512,256]{1,0:T(8,128)(2,1)S(1)}, bf16[512,256]{1,0:T(8,128)(2,1)S(1)}, u32[]{:S(2)}, u32[]{:S(2)}) collective-permute-start(bf16[512,256]{1,0:T(8,128)(2,1)S(1)} %collective-permute-done.21), channel_id=1, source_target_pairs={{0,14},{1,15},{2,0},{3,1},{4,2},{5,3},{6,4},{7,5},{8,6},{9,7},{10,... | collective-permute-start | bytes 786440 | tf_op jit(solution)/shard_map/ppermute | solution.py:68
  88.9 5.9 %collective-permute-start.27 = (bf16[256,256]{1,0:T(8,128)(2,1)S(1)}, bf16[256,256]{1,0:T(8,128)(2,1)S(1)}, u32[]{:S(2)}, u32[]{:S(2)}) collective-permute-start(bf16[256,256]{1,0:T(8,128)(2,1)S(1)} %select_bitcast_fusion.2), channel_id=1, source_target_pairs={{0,1},{1,0},{2,3},{3,2},{4,5},{5,4},{6,7},{7,6},{8,9},{9,8},{10,11... | collective-permute-start | bytes 393224 | tf_op jit(solution)/shard_map/ppermute | solution.py:107
  90.7 6.7 %collective-permute-start.22 = (bf16[256,256]{1,0:T(8,128)(2,1)S(1)}, bf16[256,256]{1,0:T(8,128)(2,1)S(1)}, u32[]{:S(2)}, u32[]{:S(2)}) collective-permute-start(bf16[256,256]{1,0:T(8,128)(2,1)S(1)} %broadcast_select_fusion.3), channel_id=1, source_target_pairs={{0,1},{1,0},{2,3},{3,2},{4,5},{5,4},{6,7},{7,6},{8,9},{9,8},{10,11... | collective-permute-start | bytes 393224 | tf_op jit(solution)/shard_map/ppermute | solution.py:107
  94.9 5.4 %collective-permute-start.28 = (bf16[256,256]{1,0:T(8,128)(2,1)S(1)}, bf16[256,256]{1,0:T(8,128)(2,1)S(1)}, u32[]{:S(2)}, u32[]{:S(2)}) collective-permute-start(bf16[256,256]{1,0:T(8,128)(2,1)S(1)} %subtract_convert_fusion), channel_id=1, source_target_pairs={{0,1},{1,0},{2,3},{3,2},{4,5},{5,4},{6,7},{7,6},{8,9},{9,8},{10,11... | collective-permute-start | bytes 393224 | tf_op jit(solution)/shard_map/ppermute | solution.py:131
